TPU v7x, 32 devices: a whole 2x2x4 slice. The times are simulated.
32 devices in a mesh: region: 4 (over x, core), sub: 8 (over z, y).
Axes of the slice: x: 2, y: 2, z: 4, core: 2. Of those that a mesh axis runs over, the one named last changes fastest.
Arguments:
- multipliers: float32 [32, 3, 3, 256], P(('region', 'sub')), may hold values from -6 to 6
- direction: float32 [32, 3, 3, 256], P(('region', 'sub')), may hold values from -12 to 12
- residual: float32 [32, 3, 3, 256], P(('region', 'sub')), may hold values from -12 to 12
- reaction: float32 [32, 16, 256], P(('region', 'sub')), may hold values from 0.1 to 2
- viscosity: float32 [32, 16, 256], P(('region', 'sub')), may hold values from 0.5 to 5
- primal_index: int32 [32, 96], P(('region', 'sub')), may hold values from 17 to 2286, as said below
- region_inverse: float32 [4, 768, 768], P('region', 'sub'), as said below
- coarse_map: float32 [32, 96, 384], P(('region', 'sub')), may hold values from -0.4375 to 0.4375
- global_inverse: float32 [384, 384], replicated, as said below
Outputs:
- new_multipliers: float32 [32, 3, 3, 256], P(('region', 'sub'))
- new_residual: float32 [32, 3, 3, 256], P(('region', 'sub'))
- velocity: float32 [32, 3, 16, 256], P(('region', 'sub'))
- pressure: float32 [32, 16, 256], P(('region', 'sub'))
Inputs may be any that keep to these rules, and one draw needn't show every extreme that they name: `primal_index`: each row holds 96 different positions, each in the interior of a face (neither face index 0 nor 16 - 1); every row contains the first such position and the last one. `region_inverse`: each region's matrix is symmetric positive definite. `global_inverse`: symmetric positive definite.
All inputs are finite; a program needn't handle non-finite values.
Results may differ from a plain program's by a relative error of at most 0.0001.
Values sent between devices are 32-bit elements; how exact they have to be, the bound alone decides.
No kernel may reach another device: no remote copies, remote signals or barrier semaphores. Data moves between devices by JAX's collectives and lax.ppermute only.
A program may use at most 64 MiB of HBM per device.

v0:
```python
import jax
import jax.numpy as jnp
from jax import lax
from jax.sharding import PartitionSpec as P

DOM_Z = 4
LEVELS = 3
SWEEPS = 1
COARSE_SWEEPS = 8
VCYCLES = 2


damping = 0.8


def shifted_2(x, axis, by):
    count = lax.axis_size(axis)
    return lax.ppermute(x, axis, [(i, (i + by) % count) for i in range(count)])


def operate(field, react, weight, cells):
    width = field.shape[-1]
    padded = jnp.pad(field, ((0, 0), (1, 1), (cells, cells)))
    middle = padded[:, 1:-1]
    position = lax.broadcasted_iota(jnp.int32, (1, 1, width), 2) % cells
    above = jnp.where(position < cells - 1, middle[:, :, cells + 1 : cells + 1 + width], 0.0)
    beneath = jnp.where(position > 0, middle[:, :, cells - 1 : cells - 1 + width], 0.0)
    beside = padded[:, 2:, cells : cells + width] + padded[:, :-2, cells : cells + width]
    beside = beside + middle[:, :, 2 * cells :] + middle[:, :, :width]
    beside = beside + above + beneath
    return react * field + weight * (6.0 * field - beside)


def restrict(array, cells):
    lead = array.shape[:-2]
    depth = array.shape[-2]
    half = cells // 2
    blocks = array.reshape(lead + (depth // 2, 2, half, 2, half, 2)).mean(axis=(-5, -3, -1))
    return blocks.reshape(lead + (depth // 2, half * half))


def prolong(array, cells):
    lead = array.shape[:-2]
    depth = array.shape[-2]
    cubic = array.reshape(lead + (depth, cells, cells))
    grown = jnp.repeat(jnp.repeat(jnp.repeat(cubic, 2, axis=-3), 2, axis=-2), 2, axis=-1)
    return grown.reshape(lead + (2 * depth, 4 * cells * cells))


def relax(field, source, react, weight, cells, count):
    diagonal = react + 6.0 * weight
    for _ in range(count):
        field = field + damping * (source - operate(field, react, weight, cells)) / diagonal
    return field


def vcycle(field, source, reacts, cells, level):
    weight = 0.25**level
    if level == LEVELS - 1:
        return relax(field, source, reacts[level], weight, cells, COARSE_SWEEPS)
    field = relax(field, source, reacts[level], weight, cells, SWEEPS)
    remain = restrict(source - operate(field, reacts[level], weight, cells), cells)
    coarse = vcycle(jnp.zeros_like(remain), remain, reacts, cells // 2, level + 1)
    field = field + prolong(coarse, cells // 2)
    return relax(field, source, reacts[level], weight, cells, SWEEPS)


def local_solve(source, react, cells):
    reacts = [react]
    size_now = cells
    for _ in range(LEVELS - 1):
        reacts.append(restrict(reacts[-1], size_now))
        size_now = size_now // 2
    field = jnp.zeros_like(source)
    for _ in range(VCYCLES):
        field = vcycle(field, source, reacts, cells, 0)
    return field


def face_cells(picked, cells):
    face = cells * cells
    block = picked // (3 * face)
    component = picked // face % 3
    spot = picked % face
    first = spot // cells
    second = spot % cells
    upper = cells - 1
    place = jnp.where(
        block == 0,
        upper * face + spot,
        jnp.where(
            block == 1, first * face + upper * cells + second, first * face + second * cells + upper
        ),
    )
    return component * (cells * face) + place


def body(
    multipliers,
    direction,
    residual,
    reaction,
    viscosity,
    primal_index,
    region_inverse,
    coarse_map,
    global_inverse,
):
    highest = lax.Precision.HIGHEST
    react = reaction[0]
    cells = react.shape[0]
    face = react.shape[1]
    upper_end = cells - 1
    active = direction[0]
    below_x = shifted_2(active[0], "region", 1)
    below_y = shifted_2(active[1], "sub", DOM_Z)
    below_z = shifted_2(active[2], "sub", 1)
    source = jnp.zeros((3, cells, face), jnp.float32)
    source = source.at[:, upper_end, :].add(active[0])
    source = source.at[:, :, face - cells :].add(active[1].reshape(3, cells, cells))
    source = source.at[:, :, upper_end::cells].add(active[2].reshape(3, cells, cells))
    source = source.at[:, 0, :].add(-below_x)
    source = source.at[:, :, :cells].add(-below_y.reshape(3, cells, cells))
    source = source.at[:, :, 0::cells].add(-below_z.reshape(3, cells, cells))
    picked = primal_index[0]
    primal = jnp.take(active.reshape(-1), picked)
    rows = region_inverse[0]
    mapping = coarse_map[0]
    share = jnp.dot(primal, mapping, precision=highest)
    piece_primal = lax.all_gather(primal[None, :], "sub", axis=0, tiled=True)
    piece_share = lax.all_gather(share[None, :], "sub", axis=0, tiled=True)
    region_part = jnp.dot(rows, piece_primal.reshape(-1), precision=highest)
    region_total = jnp.sum(piece_share, axis=0)
    total = lax.psum(region_total, "region")
    top = jnp.dot(global_inverse, total, precision=highest)
    lifted = region_part + jnp.dot(mapping, top, precision=highest)
    base = local_solve(source, react, cells)
    spots = face_cells(picked, cells)
    velocity = base.reshape(-1).at[spots].add(lifted).reshape(3, cells, face)
    upper_x = velocity[:, upper_end, :]
    upper_y = velocity[:, :, face - cells :].reshape(3, face)
    upper_z = velocity[:, :, upper_end::cells].reshape(3, face)
    lower_x = velocity[:, 0, :]
    lower_y = velocity[:, :, :cells].reshape(3, face)
    lower_z = velocity[:, :, 0::cells].reshape(3, face)
    squares = jnp.sum(residual[0] * residual[0])
    after_x = shifted_2(lower_x, "region", -1)
    after_y = shifted_2(lower_y, "sub", -DOM_Z)
    after_z = shifted_2(lower_z, "sub", -1)
    jump = jnp.stack([upper_x - after_x, upper_y - after_y, upper_z - after_z])
    curvature, squares_all = lax.psum((jnp.sum(active * jump), squares), ("region", "sub"))
    step_x = jnp.concatenate([velocity[0, 1:], after_x[0][None]], axis=0) - velocity[0]
    step_y = (
        jnp.concatenate([velocity[1][:, cells:], after_y[1].reshape(cells, cells)], axis=1)
        - velocity[1]
    )
    position = lax.broadcasted_iota(jnp.int32, (1, face), 1) % cells
    edge_values = jnp.repeat(after_z[2].reshape(cells, cells), cells, axis=1)
    shifted = jnp.pad(velocity[2][:, 1:], ((0, 0), (0, 1)))
    step_z = jnp.where(position == cells - 1, edge_values, shifted) - velocity[2]
    pressure = -viscosity[0] * (step_x + step_y + step_z)
    alpha = squares_all / curvature
    new_multipliers = (multipliers[0] + alpha * active)[None]
    new_residual = (residual[0] - alpha * jump)[None]
    return (new_multipliers, new_residual, velocity[None], pressure[None])


def solution(mesh):
    in_specs = (
        P(("region", "sub"), None, None, None),
        P(("region", "sub"), None, None, None),
        P(("region", "sub"), None, None, None),
        P(("region", "sub"), None, None),
        P(("region", "sub"), None, None),
        P(("region", "sub"), None),
        P("region", "sub", None),
        P(("region", "sub"), None, None),
        P(),
    )
    out_specs = (
        P(("region", "sub"), None, None, None),
        P(("region", "sub"), None, None, None),
        P(("region", "sub"), None, None, None),
        P(("region", "sub"), None, None),
    )
    return jax.shard_map(body, mesh=mesh, in_specs=in_specs, out_specs=out_specs, check_vma=False)
```

profile of v0, /device:TPU:0, one launch (start us, length us, event | category | flops | bytes accessed | tf_op | source)
XLA Modules:
  0.0 160.4 jit_solution(2502869876383405660)
XLA Ops:
  0.7 0.8 fusion.275
  2.0 3.7 %collective-permute-start.1 = (f32[3,256]{1,0:T(4,128)S(1)}, f32[3,256]{1,0:T(4,128)S(1)}, u32[]{:S(2)}, u32[]{:S(2)}) collective-permute-start(f32[3,256]{1,0:T(4,128)S(1)} %bitcast.180), channel_id=1, source_target_pairs={{0,4},{1,5},{2,6},{3,7},{4,0},{5,1},{6,2},{7,3},{8,12},{9,13},{10,... | collective-permute-start | bytes 9224 | tf_op jit(solution)/shard_map/ppermute | solution.py:18
  5.7 1.5 collective-permute-start.2
  7.3 0.7 add_bitcast_fusion
  8.0 0.7 broadcast_multiply_fusion.6
  8.7 1.8 %reshape_squeeze.17 = f32[8,2,8,2,8,2]{5,4,3,2,1,0:T(8,128)S(1)} reshape(f32[1,16,256]{2,1,0:T(8,128)} %param.20) | data formatting | bytes 32768 | tf_op jit(solution)/shard_map/reshape;squeeze | solution.py:38
  12.0 1.1 gather_fusion
  13.4 25.9 %all-gather.2 = f32[8,1,384]{2,1,0:T(1,128)S(1)} all-gather(f32[1,1,384]{2,1,0:T(1,128)S(1)} %convolution_bitcast_fusion.1), channel_id=2, replica_groups=mesh['region'=4,'sub'=8] {'sub'}, dimensions={0}, use_global_device_ids=true | all-gather | bytes 13824 | tf_op jit(solution)/shard_map/all_gather | solution.py:131
  39.3 5.7 %psum.22 = f32[384]{0:T(512)S(1)} all-reduce(f32[384]{0:T(512)S(1)} %reduce_sum.88), channel_id=1, replica_groups=mesh['region'=4,'sub'=8] {'region'}, use_global_device_ids=true, to_apply=%region_11.12 | all-reduce | flops 384 | bytes 3072 | tf_op jit(solution)/shard_map/psum | solution.py:134
  45.8 18.1 %all-gather.1 = f32[8,1,96]{2,1,0:T(1,128)S(1)} all-gather(f32[1,1,96]{2,1,0:T(1,128)S(1)} %fusion.271), channel_id=1, replica_groups=mesh['region'=4,'sub'=8] {'sub'}, dimensions={0}, use_global_device_ids=true | all-gather | bytes 3456 | tf_op jit(solution)/shard_map/all_gather | solution.py:130
  64.4 0.7 reduce.26
  65.2 0.6 multiply_reduce_fusion
  67.0 1.1 scatter_fusion
  68.9 4.3 %scatter-add.44 = f32[3,16,256]{1,0,2:T(4,128)S(1)} dynamic-update-slice(f32[3,16,256]{1,0,2:T(4,128)S(1)} %scatter_fusion, f32[3,1,256]{1,0,2:T(4,128)S(1)} %slice_add_fusion, s32[]{:T(128)} %constant.334.clone.1, s32[]{:T(128)} %constant.334.clone.1, s32[]{:T(128)} %constant.334.clone.1) | dynamic-update-slice | bytes 6148 | tf_op jit(solution)/shard_map/scatter-add | solution.py:122
  73.2 1.1 scatter_fusion.1
  74.4 2.0 %fusion.12 = f32[3,16,256]{1,0,2:T(4,128)S(1)} fusion(f32[3,16,256]{1,0,2:T(4,128)S(1)} %scatter_fusion.1, f32[3,16,256]{1,0,2:T(4,128)S(1)} %broadcast.795, f32[16,256]{0,1:T(8,128)S(1)} %copy.133, f32[16,256]{0,1:T(8,128)S(1)} %copy.132, pred[256]{0:T(512)(128)(4,1)S(1)} %get-tuple-element.105, pred[256]{0:T(512)(128)(4,1)S(1)} %get-tuple-element.106), kind=kLoop, calls=%fused_computation.29 | loop fusion | flops 147456 | bytes 180736 | tf_op jit(solution)/shard_map/div | solution.py:53
  76.4 2.0 %add_subtract_fusion.1 = f32[3,16,256]{1,0,2:T(4,128)S(1)} fusion(f32[3,16,256]{1,0,2:T(4,128)S(1)} %scatter_fusion.1, f32[3,16,256]{1,0,2:T(4,128)S(1)} %fusion.12, f32[16,256]{0,1:T(8,128)S(1)} %copy.134, pred[256]{0:T(512)(128)(4,1)S(1)} %get-tuple-element.105, pred[256]{0:T(512)(128)(4,1)S(1)} %get-tuple-element.106), kind=kLoop, calls=%fused_computation.56 | loop fusion | flops 147456 | bytes 164352 | tf_op jit(solution)/shard_map/sub | solution.py:62
  78.5 4.8 %reshape.717 = f32[3,8,2,8,2,8,2]{6,5,4,3,2,1,0:T(8,128)} reshape(f32[3,16,256]{2,1,0:T(8,128)S(1)} %copy.135) | data formatting | bytes 98304 | tf_op jit(solution)/shard_map/reshape | solution.py:38
  83.4 2.2 %reduce_sum.82 = f32[3,8,8,8]{3,2,1,0:T(8,128)S(1)} reduce(f32[3,8,2,8,2,8,2]{6,5,4,3,2,1,0:T(8,128)} %reshape.717, f32[]{:T(128)} %constant.333.clone.1), dimensions={2,4,6}, to_apply=%region_4.0 | reduce | flops 10752 | bytes 55300 | tf_op jit(solution)/shard_map/reduce_sum | solution.py:38
  88.7 2.1 %bitcast_add_fusion.1 = f32[3,16,256]{1,0,2:T(4,128)S(1)} fusion(f32[3,16,16,8]{1,0,3,2:T(4,128)S(1)} %bitcast.162, f32[16,256]{0,1:T(8,128)S(1)} %copy.133, f32[3,16,256]{1,0,2:T(4,128)S(1)} %scatter_fusion.1, f32[3,16,256]{1,0,2:T(4,128)S(1)} %broadcast.795, pred[256]{0:T(512)(128)(4,1)S(1)} %get-tuple-element.105, ...), kind=kLoop, calls=%fused_computation.32 | loop fusion | flops 159744 | bytes 205312 | tf_op jit(solution)/shard_map/add | solution.py:64
  90.7 2.1 %divide_add_fusion.2 = f32[3,16,256]{1,0,2:T(4,128)S(1)} fusion(f32[3,16,256]{1,0,2:T(4,128)S(1)} %bitcast_add_fusion.1, f32[3,16,256]{1,0,2:T(4,128)S(1)} %scatter_fusion.1, f32[16,256]{0,1:T(8,128)S(1)} %copy.134, f32[16,256]{0,1:T(8,128)S(1)} %copy.133, pred[256]{0:T(512)(128)(4,1)S(1)} %get-tuple-element.105, pred[256]{0:T(512)(128)(4,1)S(1)} %get-tuple-element.106), kind=kLoop, calls=%fused_computation.17 | loop fusion | flops 184320 | bytes 180736 | tf_op jit(solution)/shard_map/add | solution.py:53
  92.8 2.1 %divide_add_fusion.1 = f32[3,16,256]{1,0,2:T(4,128)S(1)} fusion(f32[3,16,256]{1,0,2:T(4,128)S(1)} %divide_add_fusion.2, f32[3,16,256]{1,0,2:T(4,128)S(1)} %scatter_fusion.1, f32[16,256]{0,1:T(8,128)S(1)} %copy.134, f32[16,256]{0,1:T(8,128)S(1)} %copy.133, pred[256]{0:T(512)(128)(4,1)S(1)} %get-tuple-element.105, pred[256]{0:T(512)(128)(4,1)S(1)} %get-tuple-element.106), kind=kLoop, calls=%fused_computation.16 | loop fusion | flops 184320 | bytes 180736 | tf_op jit(solution)/shard_map/add | solution.py:53
  94.9 2.2 %add_subtract_fusion = f32[3,16,256]{1,0,2:T(4,128)S(1)} fusion(f32[3,16,256]{1,0,2:T(4,128)S(1)} %scatter_fusion.1, f32[3,16,256]{1,0,2:T(4,128)S(1)} %divide_add_fusion.1, f32[16,256]{0,1:T(8,128)S(1)} %copy.134, pred[256]{0:T(512)(128)(4,1)S(1)} %get-tuple-element.105, pred[256]{0:T(512)(128)(4,1)S(1)} %get-tuple-element.106), kind=kLoop, calls=%fused_computation.40 | loop fusion | flops 147456 | bytes 164352 | tf_op jit(solution)/shard_map/sub | solution.py:62
  97.2 4.8 %reshape.725 = f32[3,8,2,8,2,8,2]{6,5,4,3,2,1,0:T(8,128)} reshape(f32[3,16,256]{2,1,0:T(8,128)S(1)} %copy.147) | data formatting | bytes 98304 | tf_op jit(solution)/shard_map/reshape | solution.py:38
  102.1 2.2 %reduce_sum.86 = f32[3,8,8,8]{3,2,1,0:T(8,128)S(1)} reduce(f32[3,8,2,8,2,8,2]{6,5,4,3,2,1,0:T(8,128)} %reshape.725, f32[]{:T(128)} %constant.333.clone.1), dimensions={2,4,6}, to_apply=%region_8.9 | reduce | flops 10752 | bytes 55300 | tf_op jit(solution)/shard_map/reduce_sum | solution.py:38
  107.5 2.1 %divide_add_fusion = f32[3,16,256]{1,0,2:T(4,128)S(1)} fusion(f32[3,16,256]{1,0,2:T(4,128)S(1)} %bitcast_add_fusion, f32[3,16,256]{1,0,2:T(4,128)S(1)} %scatter_fusion.1, f32[16,256]{0,1:T(8,128)S(1)} %copy.134, f32[16,256]{0,1:T(8,128)S(1)} %copy.133, pred[256]{0:T(512)(128)(4,1)S(1)} %get-tuple-element.105, pred[256]{0:T(512)(128)(4,1)S(1)} %get-tuple-element.106), kind=kLoop, calls=%fused_computation.15 | loop fusion | flops 184320 | bytes 180736 | tf_op jit(solution)/shard_map/add | solution.py:53
  109.7 1.1 scatter_fusion.2
  111.4 0.6 broadcast_in_dim_reshape.2
  112.9 2.8 %collective-permute-done.5 = f32[3,256]{1,0:T(4,128)S(1)} collective-permute-done((f32[3,256]{1,0:T(4,128)S(1)}, f32[3,256]{1,0:T(4,128)S(1)}, u32[]{:S(2)}, u32[]{:S(2)}) %collective-permute-start.5) | collective-permute-done | bytes 3104 | tf_op jit(solution)/shard_map/ppermute | solution.py:18
  116.0 1.0 collective-permute-done.4
  117.7 39.4 %all-reduce.28 = (f32[]{:T(128)}, f32[]{:T(128)}) all-reduce(f32[]{:T(128)} %multiply_reduce_fusion, f32[]{:T(128)} %fusion.96), channel_id=1, replica_groups=mesh['region'=4,'sub'=8] {'region','sub'}, use_global_device_ids=true, to_apply=%region_1.0 | all-reduce | flops 2 | bytes 16 | tf_op jit(solution)/shard_map/psum | solution.py:151
  159.7 0.7 fusion.95
  (179 shorter events, 15.6 us)
Async XLA Ops:
  0.6 44.3 %copy-start = (f32[384,384]{1,0:T(8,128)S(1)}, f32[384,384]{1,0:T(8,128)}, u32[]{:S(2)}) copy-start(f32[384,384]{1,0:T(8,128)} %param.25) | copy-start | bytes 1769476
  0.6 11.3 %copy-start.4 = (f32[1,3,3,256]{3,0,2,1:T(1,128)S(1)}, f32[1,3,3,256]{3,0,2,1:T(1,128)}, u32[]{:S(2)}) copy-start(f32[1,3,3,256]{3,0,2,1:T(1,128)} %param.18) | copy-start | bytes 27652
  0.7 11.2 %copy-start.8 = (s32[1,96]{1,0:T(1,128)S(1)}, s32[1,96]{1,0:T(1,128)}, u32[]{:S(2)}) copy-start(s32[1,96]{1,0:T(1,128)} %param.22) | copy-start | bytes 1156
  0.7 12.5 %copy-start.1 = (f32[1,96,384]{2,1,0:T(8,128)S(1)}, f32[1,96,384]{2,1,0:T(8,128)}, u32[]{:S(2)}) copy-start(f32[1,96,384]{2,1,0:T(8,128)} %param.24) | copy-start | bytes 442372
  0.7 64.5 %copy-start.5 = (f32[1,3,3,256]{3,0,2,1:T(1,128)S(1)}, f32[1,3,3,256]{3,0,2,1:T(1,128)}, u32[]{:S(2)}) copy-start(f32[1,3,3,256]{3,0,2,1:T(1,128)} %param.19) | copy-start | bytes 27652
  0.7 65.1 %copy-start.2 = (f32[1,96,768]{2,1,0:T(8,128)S(1)}, f32[1,96,768]{2,1,0:T(8,128)}, u32[]{:S(2)}) copy-start(f32[1,96,768]{2,1,0:T(8,128)} %param.23) | copy-start | bytes 884740
  1.5 66.6 %collective-permute-start = (f32[3,256]{1,0:T(4,128)S(1)}, f32[3,256]{1,0:T(4,128)S(1)}, u32[]{:S(2)}, u32[]{:S(2)}) collective-permute-start(f32[3,256]{1,0:T(4,128)S(1)} %bitcast.181), channel_id=1, source_target_pairs={{0,8},{8,16},{16,24},{24,0},{1,9},{9,17},{17,25},{25,1},{2,10},{10... | collective-permute-start | bytes 9224 | tf_op jit(solution)/shard_map/ppermute | solution.py:18
  2.0 66.4 %collective-permute-start.1 = (f32[3,256]{1,0:T(4,128)S(1)}, f32[3,256]{1,0:T(4,128)S(1)}, u32[]{:S(2)}, u32[]{:S(2)}) collective-permute-start(f32[3,256]{1,0:T(4,128)S(1)} %bitcast.180), channel_id=1, source_target_pairs={{0,4},{1,5},{2,6},{3,7},{4,0},{5,1},{6,2},{7,3},{8,12},{9,13},{10,... | collective-permute-start | bytes 9224 | tf_op jit(solution)/shard_map/ppermute | solution.py:18
  5.7 62.9 %collective-permute-start.2 = (f32[3,256]{1,0:T(4,128)S(1)}, f32[3,256]{1,0:T(4,128)S(1)}, u32[]{:S(2)}, u32[]{:S(2)}) collective-permute-start(f32[3,256]{1,0:T(4,128)S(1)} %bitcast.179), channel_id=1, source_target_pairs={{0,1},{1,2},{2,3},{3,4},{4,5},{5,6},{6,7},{7,0},{8,9},{9,10},{10,1... | collective-permute-start | bytes 9224 | tf_op jit(solution)/shard_map/ppermute | solution.py:18
  8.7 58.0 %copy-start.3 = (f32[1,16,256]{2,1,0:T(8,128)S(1)}, f32[1,16,256]{2,1,0:T(8,128)}, u32[]{:S(2)}) copy-start(f32[1,16,256]{2,1,0:T(8,128)} %param.20) | copy-start | bytes 49156
  107.3 51.8 %copy-start.7 = (f32[1,3,3,256]{3,0,2,1:T(1,128)S(1)}, f32[1,3,3,256]{3,0,2,1:T(1,128)}, u32[]{:S(2)}) copy-start(f32[1,3,3,256]{3,0,2,1:T(1,128)} %param.17) | copy-start | bytes 27652
  107.3 52.4 %copy-start.6 = (f32[1,16,256]{2,1,0:T(8,128)S(1)}, f32[1,16,256]{2,1,0:T(8,128)}, u32[]{:S(2)}) copy-start(f32[1,16,256]{2,1,0:T(8,128)} %param.21) | copy-start | bytes 49156
  111.0 1.9 %collective-permute-start.3 = (f32[3,256]{1,0:T(4,128)S(1)}, f32[3,256]{1,0:T(4,128)S(1)}, u32[]{:S(2)}, u32[]{:S(2)}) collective-permute-start(f32[3,256]{1,0:T(4,128)S(1)} %bitcast.182), channel_id=1, source_target_pairs={{0,24},{8,0},{16,8},{24,16},{1,25},{9,1},{17,9},{25,17},{2,26},{10... | collective-permute-start | bytes 9224 | tf_op jit(solution)/shard_map/ppermute | solution.py:18
  112.1 3.6 %collective-permute-start.5 = (f32[3,256]{1,0:T(4,128)S(1)}, f32[3,256]{1,0:T(4,128)S(1)}, u32[]{:S(2)}, u32[]{:S(2)}) collective-permute-start(f32[3,256]{1,0:T(4,128)S(1)} %reshape.739), channel_id=1, source_target_pairs={{0,7},{1,0},{2,1},{3,2},{4,3},{5,4},{6,5},{7,6},{8,15},{9,8},{10,9... | collective-permute-start | bytes 9224 | tf_op jit(solution)/shard_map/ppermute | solution.py:18
  112.5 4.5 %collective-permute-start.4 = (f32[3,256]{1,0:T(4,128)S(1)}, f32[3,256]{1,0:T(4,128)S(1)}, u32[]{:S(2)}, u32[]{:S(2)}) collective-permute-start(f32[3,256]{1,0:T(4,128)S(1)} %reshape.737), channel_id=1, source_target_pairs={{0,4},{1,5},{2,6},{3,7},{4,0},{5,1},{6,2},{7,3},{8,12},{9,13},{10,... | collective-permute-start | bytes 9224 | tf_op jit(solution)/shard_map/ppermute | solution.py:18
where the time goes:
time: 161 us; the launch traced here: 160 us
  blocking collectives  89.1 us (55%)
  other arithmetic  30 us (19%)
  local copies, waits for them, and re-layouts  27.3 us (17%)
  starting transfers between devices  6.06 us (4%)
  waiting for transfers between devices  3.82 us (2%)
  between operations  2.82 us (2%)
    psum x1, blocking collectives, body(): lax.psum((jnp.sum(active * jump), squares), ('region', 'sub'))  39.4 us
    all_gather x1, blocking collectives, body(): piece_share = lax.all_gather(share[None, :], 'sub', axis=0, tiled=True)  25.9 us
    all_gather x1, blocking collectives, body(): piece_primal = lax.all_gather(primal[None, :], 'sub', axis=0, tiled=True)  18.1 us
    reshape x4, local copies, waits for them, and re-layouts, restrict(): array.reshape(lead + (depth // 2, 2, half, 2, half, 2))  10.7 us
    add x17, other arithmetic, relax(): field + damping * (source - operate(field, react, weight, cells)) / diagonal  7.44 us
    ppermute x6, starting transfers between devices, shifted_2(): return lax.ppermute(x, axis, [(i, (i + by) % count) for i in range(count)])  6.06 us
    psum x1, blocking collectives, body(): total = lax.psum(region_total, 'region')  5.67 us
    reduce_sum x6, other arithmetic, restrict(): array.reshape(lead + (depth // 2, 2, half, 2, half, 2))  5 us
  transfers between devices with their start and end apart: 6, of which 2 were waited for; matrix products, arithmetic and copies ran while one was open for 8% of the time, Pallas kernels for 0%

commit v1 on v0

v1 whole, which is shorter than its diff:
```python
import functools

import jax
import jax.numpy as jnp
from jax import lax
from jax.experimental import pallas as pl
from jax.experimental.pallas import tpu as pltpu
from jax.sharding import PartitionSpec as P

DOM_Z = 4
LEVELS = 3
SWEEPS = 1
COARSE_SWEEPS = 8
VCYCLES = 2
LANES = 128

damping = 0.8


def shifted_2(x, axis, by):
    count = lax.axis_size(axis)
    return lax.ppermute(x, axis, [(i, (i + by) % count) for i in range(count)])


def iota(shape, dim):
    return lax.broadcasted_iota(jnp.int32, shape, dim)


def parts_of(x, count=3):
    result = []
    for step in range(count):
        piece = x.astype(jnp.bfloat16)
        result.append(piece)
        if step < count - 1:
            x = x - piece.astype(jnp.float32)
    return result


def times_choice(x, choice):
    rows = x.shape[0]
    stacked = jnp.concatenate(parts_of(x), axis=0)
    y = jnp.dot(stacked, choice, preferred_element_type=jnp.float32)
    return y[:rows] + y[rows : 2 * rows] + y[2 * rows :]


def choice_times(choice, x):
    width = x.shape[1]
    stacked = jnp.concatenate(parts_of(x), axis=1)
    y = jnp.dot(choice, stacked, preferred_element_type=jnp.float32)
    return y[:, :width] + y[:, width : 2 * width] + y[:, 2 * width :]


def one_hot(condition):
    return jnp.where(condition, 1.0, 0.0).astype(jnp.bfloat16)


def decode(picked, cells):
    face = cells * cells
    zero = jnp.zeros_like(picked)
    one = zero + 1
    block = jnp.where(picked >= 3 * face, one, zero) + jnp.where(picked >= 6 * face, one, zero)
    rest = picked - 3 * face * block
    component = jnp.where(rest >= face, one, zero) + jnp.where(rest >= 2 * face, one, zero)
    spot = rest - face * component
    first = lax.div(spot, zero + cells)
    second = spot - first * cells
    end = cells - 1
    x = jnp.where(block == 0, end, first)
    y = jnp.where(block == 0, first, jnp.where(block == 1, end, second))
    z = jnp.where(block == 2, end, second)
    return 3 * block + component, spot, component * cells + x, y * cells + z


def spread(faces, cells):
    face = cells * cells
    here = lax.div(iota((cells, face), 1), jnp.full((cells, face), cells, jnp.int32)) == iota((cells, face), 0)
    rows = [jnp.where(here, jnp.broadcast_to(faces[c : c + 1], (cells, face)), 0.0) for c in range(faces.shape[0])]
    return jnp.concatenate(rows, axis=0)


def mask_sum(x, cells):
    face = cells * cells
    here = lax.div(iota((cells, face), 1), jnp.full((cells, face), cells, jnp.int32)) == iota((cells, face), 0)
    rows = [
        jnp.sum(jnp.where(here, x[c * cells : (c + 1) * cells], 0.0), axis=0, keepdims=True)
        for c in range(x.shape[0] // cells)
    ]
    return jnp.concatenate(rows, axis=0)


def place_matrices(cells):
    face = cells * cells
    row = iota((face, face), 0)
    column = iota((face, face), 1)
    second = row - lax.div(row, jnp.full((face, face), cells, jnp.int32)) * cells
    end = cells - 1
    lower = jnp.concatenate([one_hot(column == second), one_hot(column == second * cells)], axis=0)
    upper = jnp.concatenate(
        [one_hot(column == second + end * cells), one_hot(column == second * cells + end)], axis=0
    )
    return lower, upper


def pick_matrices(cells):
    face = cells * cells
    row = iota((face, face), 0)
    column = iota((face, face), 1)
    second = column - lax.div(column, jnp.full((face, face), cells, jnp.int32)) * cells
    end = cells - 1
    return jnp.concatenate(
        [
            one_hot(row == second),
            one_hot(row == second * cells),
            one_hot(row == second + end * cells),
            one_hot(row == second * cells + end),
        ],
        axis=1,
    )


def shift(field, by, dim):
    size = field.shape[dim]
    return pltpu.roll(field, by % size, dim)


def pair_mean(field, cells, step, where_x, where_y, where_z):
    for position, dim, reach in ((where_z, 1, step), (where_y, 1, step * cells), (where_x, 0, step)):
        even = (position & step) == 0
        field = 0.5 * (field + jnp.where(even, shift(field, -reach, dim), shift(field, reach, dim)))
    return field


def positions(rows, cells):
    face = cells * cells
    shape = (rows, face)
    lane = iota(shape, 1)
    row = iota(shape, 0)
    where_x = row & (cells - 1)
    where_z = lane & (cells - 1)
    where_y = lax.shift_right_logical(lane, jnp.full(shape, cells.bit_length() - 1, jnp.int32))
    return where_x, where_y, where_z


def before_kernel(
    cells,
    columns,
    direction,
    residual,
    reaction,
    primal_index,
    region_inverse,
    coarse_map,
    source_out,
    front_out,
    inverse_out,
    lower_out,
    upper_out,
    pick_out,
    spots_out,
    choose_out,
):
    face = cells * cells
    lower, upper = place_matrices(cells)
    lower_out[...] = lower
    upper_out[...] = upper
    pick_out[...] = pick_matrices(cells)
    where_x, where_y, where_z = positions(cells, cells)
    react = reaction[0]
    for level in range(LEVELS):
        weight = 0.25**level
        diagonal = react + 6.0 * weight
        inverse_out[level] = damping / diagonal
        inverse_out[LEVELS + level] = diagonal
        if level < LEVELS - 1:
            react = pair_mean(react, cells, 2**level, where_x, where_y, where_z)
    faces = [direction[0, d] for d in range(3)]
    row_x = iota((cells, face), 0)
    source = times_choice(jnp.concatenate([spread(faces[1], cells), spread(faces[2], cells)], axis=1), upper)
    own_x = jnp.concatenate(
        [jnp.where(row_x == cells - 1, jnp.broadcast_to(faces[0][c : c + 1], (cells, face)), 0.0) for c in range(3)],
        axis=0,
    )
    source_out[...] = source + own_x
    picked = primal_index[...]
    count = picked.shape[1]
    group_row, _, place_row, _ = decode(picked, cells)
    choose_out[...] = jnp.concatenate(
        [
            one_hot(iota((3 * cells, count), 0) == place_row),
            one_hot(iota((16, count), 0) == group_row),
        ],
        axis=0,
    )
    wide = jnp.broadcast_to(picked.astype(jnp.float32), (count, count))
    diagonal = iota((count, count), 0) == iota((count, count), 1)
    picked_column = jnp.sum(jnp.where(diagonal, wide, 0.0), axis=1, keepdims=True).astype(jnp.int32)
    group, spot, _, lane = decode(picked_column, cells)
    on_spot = iota((count, face), 1) == spot
    on_lane = iota((count, face), 1) == lane
    spots_out[...] = jnp.concatenate([jnp.where(on_lane, 1.0, 0.0), jnp.where(on_spot, 1.0, 0.0)], axis=1)
    nine = jnp.concatenate(faces + [jnp.zeros((7, face), jnp.float32)], axis=0)
    gathered = choice_times(one_hot(iota((count, 16), 1) == group), nine)
    primal = jnp.sum(jnp.where(on_spot, gathered, 0.0), axis=1, keepdims=True)
    share = jnp.sum(primal * coarse_map[0], axis=0, keepdims=True)
    product = jnp.sum(primal * region_inverse[0], axis=0, keepdims=True)
    line = jnp.sum(
        jnp.where(iota((count, LANES), 0) == iota((count, LANES), 1), primal, 0.0), axis=0, keepdims=True
    )
    squares = jnp.sum(residual[0] * residual[0])
    line = jnp.where(iota((1, LANES), 1) == count + 1, squares, line)
    front_out[...] = jnp.zeros_like(front_out)
    width = product.shape[1]
    used = width // LANES
    for i in range(used):
        front_out[i : i + 1, :] = product[:, i * LANES : (i + 1) * LANES]
    front_out[used : used + 1, :] = line
    for i in range(columns // LANES):
        front_out[used + 1 + i : used + 2 + i, :] = share[:, i * LANES : (i + 1) * LANES]


def solve_kernel(
    cells,
    head,
    sizes,
    source_own,
    below_x,
    below_y,
    below_z,
    inverses,
    front,
    lower,
    pick,
    base_out,
    ends_out,
    send_out,
):
    face = cells * cells
    rows = 3 * cells
    n_region, n_sub = sizes
    row_x = iota((cells, face), 0)
    source = source_own[...] - times_choice(
        jnp.concatenate([spread(below_y[...], cells), spread(below_z[...], cells)], axis=1), lower[...]
    )
    source = source - jnp.concatenate(
        [jnp.where(row_x == 0, jnp.broadcast_to(below_x[c : c + 1, :], (cells, face)), 0.0) for c in range(3)],
        axis=0,
    )
    where_x, where_y, where_z = positions(rows, cells)

    def tall(x):
        return jnp.concatenate([x] * 3, axis=0)

    inverse = [tall(inverses[level]) for level in range(LEVELS)]
    diagonal = [tall(inverses[LEVELS + level]) for level in range(LEVELS)]

    def beside(field, level):
        step = 2**level
        last = cells - step
        total = jnp.where(where_x < last, shift(field, -step, 0), 0.0)
        total = total + jnp.where(where_x >= step, shift(field, step, 0), 0.0)
        total = total + jnp.where(where_y < last, shift(field, -step * cells, 1), 0.0)
        total = total + jnp.where(where_y >= step, shift(field, step * cells, 1), 0.0)
        total = total + jnp.where(where_z < last, shift(field, -step, 1), 0.0)
        return total + jnp.where(where_z >= step, shift(field, step, 1), 0.0)

    def relax(field, right, level, sweeps):
        weight = 0.25**level
        for _ in range(sweeps):
            if field is None:
                field = inverse[level] * right
            else:
                field = (1.0 - damping) * field + inverse[level] * (right + weight * beside(field, level))
        return field

    def vcycle(field, right, level):
        if level == LEVELS - 1:
            return relax(field, right, level, COARSE_SWEEPS)
        field = relax(field, right, level, SWEEPS)
        remain = right - diagonal[level] * field + 0.25**level * beside(field, level)
        remain = pair_mean(remain, cells, 2**level, where_x, where_y, where_z)
        field = field + vcycle(None, remain, level + 1)
        return relax(field, right, level, SWEEPS)

    field = None
    for _ in range(VCYCLES):
        field = vcycle(field, source, 0)
    base_out[...] = field
    energy = jnp.sum(source * field)
    ends = times_choice(field, pick[...])
    lower_y, lower_z, upper_y, upper_z = [
        mask_sum(ends[:, i * face : (i + 1) * face], cells) for i in range(4)
    ]
    lower_x = jnp.concatenate([field[c * cells : c * cells + 1] for c in range(3)], axis=0)
    upper_x = jnp.concatenate([field[(c + 1) * cells - 1 : (c + 1) * cells] for c in range(3)], axis=0)
    ends_out[...] = jnp.concatenate([upper_x, upper_y, upper_z, jnp.zeros((7, face), jnp.float32)], axis=0)
    scalar_row, scalar_lane, halo_row = head
    message = front[...]
    at_scalar = (iota(message.shape, 0) == scalar_row) & (iota(message.shape, 1) == scalar_lane)
    message = jnp.where(at_scalar, energy, message)
    for device in range(n_region * n_sub):
        send_out[device] = message
    me_region = lax.axis_index("region")
    me_sub = lax.axis_index("sub")
    to_x = lax.rem(me_region + n_region - 1, n_region) * n_sub + me_sub
    to_y = me_region * n_sub + lax.rem(me_sub + n_sub - DOM_Z, n_sub)
    to_z = me_region * n_sub + lax.rem(me_sub + n_sub - 1, n_sub)
    for target, values in ((to_x, lower_x), (to_y, lower_y), (to_z, lower_z)):
        for i in range(face // LANES):
            send_out[target, halo_row + 3 * i : halo_row + 3 * i + 3, :] = values[:, i * LANES : (i + 1) * LANES]


def after_kernel(
    cells,
    head,
    sizes,
    received,
    base,
    ends,
    upper,
    spots,
    choose,
    direction,
    multipliers,
    residual,
    viscosity,
    region_inverse,
    coarse_map,
    global_inverse,
    multipliers_out,
    residual_out,
    velocity_out,
    pressure_out,
):
    face = cells * cells
    n_region, n_sub = sizes
    scalar_row, count, halo_row = head
    used = scalar_row
    columns = global_inverse.shape[0]
    me_region = lax.axis_index("region")
    me_sub = lax.axis_index("sub")
    region_sums = [jnp.sum(received[r * n_sub : (r + 1) * n_sub], axis=0) for r in range(n_region)]
    everything = functools.reduce(lambda a, b: a + b, region_sums)
    total = jnp.concatenate(
        [everything[used + 1 + i : used + 2 + i] for i in range(columns // LANES)], axis=1
    )
    products = jnp.concatenate(
        [jnp.concatenate([region_sums[r][i : i + 1] for i in range(used)], axis=1) for r in range(n_region)], axis=0
    )
    lines = received[:, scalar_row, :]
    primal = jnp.concatenate(
        [
            jnp.concatenate([lines[r * n_sub + q : r * n_sub + q + 1, :count] for q in range(n_sub)], axis=1)
            for r in range(n_region)
        ],
        axis=0,
    )
    top = jnp.dot(
        jnp.broadcast_to(total, (8, columns)), global_inverse[...], precision=lax.Precision.HIGHEST,
        preferred_element_type=jnp.float32,
    )[:1]
    own_line = everything[scalar_row : scalar_row + 1]
    lane = iota((1, LANES), 1)
    energy = jnp.sum(jnp.where(lane == count, own_line, 0.0), axis=1, keepdims=True)
    squares = jnp.sum(jnp.where(lane == count + 1, own_line, 0.0), axis=1, keepdims=True)
    quadratic = jnp.sum(jnp.sum(products * primal, axis=0, keepdims=True), axis=1, keepdims=True)
    curvature = energy + quadratic + jnp.sum(total * top, axis=1, keepdims=True)
    alpha = squares / curvature
    mine = jnp.sum(
        jnp.where(iota(primal.shape, 0) == me_region, primal, 0.0), axis=0, keepdims=True
    )
    weighed = jnp.sum(region_inverse[0] * mine, axis=1, keepdims=True)
    lifted = weighed + jnp.sum(coarse_map[0] * top, axis=1, keepdims=True)
    added = choice_times(choose[...], lifted * spots[...])
    velocity = base[...] + added[: 3 * cells, :face]
    upper_faces = ends[:9] + added[3 * cells : 3 * cells + 9, face:]
    for c in range(3):
        velocity_out[0, c] = velocity[c * cells : (c + 1) * cells]
    from_x = lax.rem(me_region + 1, n_region) * n_sub + me_sub
    from_y = me_region * n_sub + lax.rem(me_sub + DOM_Z, n_sub)
    from_z = me_region * n_sub + lax.rem(me_sub + 1, n_sub)
    after = [
        jnp.concatenate(
            [received[place, halo_row + 3 * i : halo_row + 3 * i + 3, :] for i in range(face // LANES)], axis=1
        )
        for place in (from_x, from_y, from_z)
    ]
    for d in range(3):
        jump = upper_faces[3 * d : 3 * d + 3] - after[d]
        residual_out[0, d] = residual[0, d] - alpha * jump
        multipliers_out[0, d] = multipliers[0, d] + alpha * direction[0, d]
    ahead = jnp.concatenate(
        [spread(after[1][1:2], cells), spread(after[2][2:3], cells)], axis=1
    )
    ahead = times_choice(ahead, upper[...])
    where_x, where_y, where_z = positions(cells, cells)
    end = cells - 1
    field_x, field_y, field_z = [velocity[c * cells : (c + 1) * cells] for c in range(3)]
    step_x = jnp.where(where_x == end, jnp.broadcast_to(after[0][0:1], (cells, face)), shift(field_x, -1, 0))
    step_y = jnp.where(where_y == end, 0.0, shift(field_y, -cells, 1))
    step_z = jnp.where(where_z == end, 0.0, shift(field_z, -1, 1))
    step = (step_x - field_x) + (step_y - field_y) + (step_z - field_z) + ahead
    pressure_out[0] = -viscosity[0] * step


def body(
    sizes,
    multipliers,
    direction,
    residual,
    reaction,
    viscosity,
    primal_index,
    region_inverse,
    coarse_map,
    global_inverse,
):
    n_region, n_sub = sizes
    devices = n_region * n_sub
    cells = reaction.shape[1]
    face = reaction.shape[2]
    count = primal_index.shape[1]
    columns = coarse_map.shape[2]
    used = region_inverse.shape[2] // LANES
    halo_row = used + 1 + columns // LANES
    height = -(-(halo_row + 3 * face // LANES) // 8) * 8
    head = (used, count, halo_row)
    rows = 3 * cells
    f32 = jnp.float32
    vmem = pl.BlockSpec(memory_space=pltpu.VMEM)

    def call(kernel, out_shape, *operands):
        return pl.pallas_call(
            kernel,
            out_shape=out_shape,
            in_specs=[vmem] * len(operands),
            out_specs=[vmem] * len(out_shape),
            compiler_params=pltpu.CompilerParams(vmem_limit_bytes=32 * 1024 * 1024),
        )(*operands)

    active = direction[0]
    below_x = shifted_2(active[0], "region", 1)
    below_y = shifted_2(active[1], "sub", DOM_Z)
    below_z = shifted_2(active[2], "sub", 1)
    source, front, inverses, lower, upper, pick, spots, choose = call(
        functools.partial(before_kernel, cells, columns),
        [
            jax.ShapeDtypeStruct((rows, face), f32),
            jax.ShapeDtypeStruct((height, LANES), f32),
            jax.ShapeDtypeStruct((2 * LEVELS, cells, face), f32),
            jax.ShapeDtypeStruct((2 * face, face), jnp.bfloat16),
            jax.ShapeDtypeStruct((2 * face, face), jnp.bfloat16),
            jax.ShapeDtypeStruct((face, 4 * face), jnp.bfloat16),
            jax.ShapeDtypeStruct((count, 2 * face), f32),
            jax.ShapeDtypeStruct((rows + 16, count), jnp.bfloat16),
        ],
        direction,
        residual,
        reaction,
        primal_index,
        region_inverse,
        coarse_map,
    )
    base, ends, sent = call(
        functools.partial(solve_kernel, cells, head, sizes),
        [
            jax.ShapeDtypeStruct((rows, face), f32),
            jax.ShapeDtypeStruct((16, face), f32),
            jax.ShapeDtypeStruct((devices, height, LANES), f32),
        ],
        source,
        below_x,
        below_y,
        below_z,
        inverses,
        front,
        lower,
        pick,
    )
    received = lax.all_to_all(sent, ("region", "sub"), 0, 0, tiled=True)
    return tuple(
        call(
            functools.partial(after_kernel, cells, head, sizes),
            [
                jax.ShapeDtypeStruct(multipliers.shape, f32),
                jax.ShapeDtypeStruct(residual.shape, f32),
                jax.ShapeDtypeStruct((1, 3, cells, face), f32),
                jax.ShapeDtypeStruct((1, cells, face), f32),
            ],
            received,
            base,
            ends,
            upper,
            spots,
            choose,
            direction,
            multipliers,
            residual,
            viscosity,
            region_inverse,
            coarse_map,
            global_inverse,
        )
    )


def solution(mesh):
    sizes = (mesh.shape["region"], mesh.shape["sub"])
    whole = P(("region", "sub"))
    in_specs = (whole,) * 6 + (P("region", "sub"), whole, P())
    return jax.shard_map(
        functools.partial(body, sizes), mesh=mesh, in_specs=in_specs, out_specs=(whole,) * 4, check_vma=False
    )
```

time: 161 us -> 32.6 us (0.20)
  blocking collectives: 89.1 us -> 0 us
  other arithmetic: 30 us -> 0 us
  local copies, waits for them, and re-layouts: 27.3 us -> 3.84 us
  waiting for transfers between devices: 3.82 us -> 12.8 us
  Pallas kernels: 0 us -> 6.54 us
  starting transfers between devices: 6.06 us -> 8.4 us
  between operations: 2.82 us -> 0.73 us
    psum x2 -> x0, blocking collectives: 45.1 us -> none  [the longest x1 39.4 us: body(): lax.psum((jnp.sum(active * jump), squares), ('region', 'sub'))]
    all_gather x2 -> x0, blocking collectives: 44 us -> none  [the longest x1 25.9 us: body(): piece_share = lax.all_gather(share[None, :], 'sub', axis=0, tiled=True)]
    reshape x21 -> x0, local copies, waits for them, and re-layouts: 12.2 us -> none  [the longest x4 10.7 us: restrict(): array.reshape(lead + (depth // 2, 2, half, 2, half, 2))]
    all_to_all x0 -> x1, waiting for transfers between devices: none -> 10.6 us  [body(): received = lax.all_to_all(sent, ('region', 'sub'), 0, 0, tiled=True)]
    add x26 -> x0, other arithmetic: 10.1 us -> none  [the longest x17 7.44 us: relax(): field + damping * (source - operate(field, react, weight, cells)) / diagonal]
    pallas_call x0 -> x3, Pallas kernels: none -> 6.54 us  [call(): pl.pallas_call(kernel, out_shape=out_shape, in_specs=[vmem] * len(operand...]
    reduce_sum x9 -> x0, other arithmetic: 6.25 us -> none  [the longest x6 5 us: restrict(): array.reshape(lead + (depth // 2, 2, half, 2, half, 2))]
    scatter-add x2 -> x0, local copies, waits for them, and re-layouts: 4.6 us -> none  [the longest x1 4.26 us: body(): source = source.at[:, 0, :].add(-below_x)]
  transfers between devices with their start and end apart: 6 -> 4, of which waited for: 2 -> 2; matrix products, arithmetic and copies ran while one was open for 8% -> 0% of each run, Pallas kernels for 0% -> 2%
where the time goes in v1:
time: 32.6 us; the launch traced here: 32.3 us
  waiting for transfers between devices  12.8 us (39%)
  starting transfers between devices  8.4 us (26%)
  Pallas kernels  6.54 us (20%)
  local copies, waits for them, and re-layouts  3.84 us (12%)
  between operations  0.73 us (2%)
    all_to_all x1, waiting for transfers between devices, body(): received = lax.all_to_all(sent, ('region', 'sub'), 0, 0, tiled=True)  10.6 us
    pallas_call x3, Pallas kernels, call(): pl.pallas_call(kernel, out_shape=out_shape, in_specs=[vmem] * len(operand...  6.54 us
    ppermute x3, starting transfers between devices, shifted_2(): return lax.ppermute(x, axis, [(i, (i + by) % count) for i in range(count)])  5.69 us
    all_to_all x1, starting transfers between devices, body(): received = lax.all_to_all(sent, ('region', 'sub'), 0, 0, tiled=True)  2.71 us
    unnamed x23, local copies, waits for them, and re-layouts  2.62 us
    ppermute x3, waiting for transfers between devices, shifted_2(): return lax.ppermute(x, axis, [(i, (i + by) % count) for i in range(count)])  2.19 us
    pallas_call x2, local copies, waits for them, and re-layouts, call(): pl.pallas_call(kernel, out_shape=out_shape, in_specs=[vmem] * len(operand...  1.22 us
  transfers between devices with their start and end apart: 4, of which 2 were waited for; matrix products, arithmetic and copies ran while one was open for 0% of the time, Pallas kernels for 2%

profile of v1, /device:TPU:0, one launch (start us, length us, event | category | flops | bytes accessed | tf_op | source)
XLA Modules:
  0.0 32.3 jit_solution(1767607411281538095)
XLA Ops:
  0.6 0.7 %copy.13.direction = f32[1,3,3,256]{3,2,1,0:T(4,128)S(1)} copy(f32[1,3,3,256]{3,0,2,1:T(1,128)} %param.10) | data formatting | bytes 18432 | tf_op args[1]
  1.3 0.0 copy-start.8
  1.3 0.0 copy-start.6
  1.4 0.5 %collective-permute-start = (f32[3,256]{1,0:T(4,128)S(1)}, f32[3,256]{1,0:T(4,128)S(1)}, u32[]{:S(2)}, u32[]{:S(2)}) collective-permute-start(f32[3,256]{1,0:T(4,128)S(1)} %get-tuple-element.32), channel_id=1, source_target_pairs={{0,8},{8,16},{16,24},{24,0},{1,9},{9,17},{17,25},{25,1},{2,10},{10... | collective-permute-start | bytes 9224 | tf_op jit(solution)/shard_map/ppermute | solution.py:22
  1.9 3.7 %collective-permute-start.1 = (f32[3,256]{1,0:T(4,128)S(1)}, f32[3,256]{1,0:T(4,128)S(1)}, u32[]{:S(2)}, u32[]{:S(2)}) collective-permute-start(f32[3,256]{1,0:T(4,128)S(1)} %get-tuple-element.31), channel_id=1, source_target_pairs={{0,4},{1,5},{2,6},{3,7},{4,0},{5,1},{6,2},{7,3},{8,12},{9,13},{10,... | collective-permute-start | bytes 9224 | tf_op jit(solution)/shard_map/ppermute | solution.py:22
  5.5 0.0 copy-start.7
  5.5 1.5 %collective-permute-start.2 = (f32[3,256]{1,0:T(4,128)S(1)}, f32[3,256]{1,0:T(4,128)S(1)}, u32[]{:S(2)}, u32[]{:S(2)}) collective-permute-start(f32[3,256]{1,0:T(4,128)S(1)} %get-tuple-element.30), channel_id=1, source_target_pairs={{0,1},{1,2},{2,3},{3,4},{4,5},{5,6},{6,7},{7,0},{8,9},{9,10},{10,1... | collective-permute-start | bytes 9224 | tf_op jit(solution)/shard_map/ppermute | solution.py:22
  7.0 0.0 copy-done.8
  7.1 0.0 copy-done.6
  7.1 0.0 copy-done.7
  7.1 0.0 copy-start
  7.1 1.0 %copy-done = f32[1,96,768]{2,1,0:T(8,128)S(1)} copy-done((f32[1,96,768]{2,1,0:T(8,128)S(1)}, f32[1,96,768]{2,1,0:T(8,128)}, u32[]{:S(2)}) %copy-start) | copy-done | bytes 294936
  8.0 0.0 copy-start.2
  8.0 0.9 %copy-done.2 = f32[1,96,384]{2,1,0:T(8,128)S(1)} copy-done((f32[1,96,384]{2,1,0:T(8,128)S(1)}, f32[1,96,384]{2,1,0:T(8,128)}, u32[]{:S(2)}) %copy-start.2) | copy-done | bytes 147480
  8.9 0.7 %shard_map.120 = (f32[48,256]{1,0:T(8,128)S(1)}, f32[16,128]{1,0:T(8,128)S(1)}, f32[6,16,256]{2,1,0:T(8,128)S(1)}, bf16[512,256]{1,0:T(8,128)(2,1)S(1)}, bf16[51...) custom-call(f32[1,3,3,256]{3,2,1,0:T(4,128)S(1)} %copy.13.direction, ...), custom_call_target="tpu_custom_call" | custom-call | tf_op jit(solution)/shard_map/pallas_call | solution.py:432
  9.6 0.0 collective-permute-done.below_x
  9.6 0.0 collective-permute-done.1.below_y
  9.6 2.2 %collective-permute-done.2.below_z = f32[3,256]{1,0:T(4,128)S(1)} collective-permute-done((f32[3,256]{1,0:T(4,128)S(1)}, f32[3,256]{1,0:T(4,128)S(1)}, u32[]{:S(2)}, u32[]{:S(2)}) %collective-permute-start.2) | collective-permute-done | bytes 3104 | tf_op jit(solution)/shard_map/ppermute | solution.py:22
  11.8 0.0 copy-start.4
  11.8 4.4 %shard_map.121 = (f32[48,256]{1,0:T(8,128)S(1)}, f32[16,256]{1,0:T(8,128)S(1)}, f32[32,16,128]{2,1,0:T(8,128)}) custom-call(f32[48,256]{1,0:T(8,128)S(1)} %get-tuple-element.15.source_own, f32[3,256]{1,0:T(4,128)S(1)} %collective-permute-done.below_x, f32[3,256]{1,0:T(4,128)S(1)} %collective-permute-done.1.below_y, ...), custom_call_target="tpu_custom_call" | custom-call | tf_op jit(solution)/shard_map/pallas_call | solution.py:432
  16.3 0.0 copy-start.1
  16.3 2.7 %all-to-all-start = ((f32[32,16,128]{2,1,0:T(8,128)}), f32[32,16,128]{2,1,0:T(8,128)S(1)}, u32[]{:S(2)}, u32[]{:S(2)}) async-start(f32[32,16,128]{2,1,0:T(8,128)} %get-tuple-element.20), calls=%async_computation | async-start | bytes 524288 | tf_op jit(solution)/shard_map/all_to_all | solution.py:479
  19.0 0.0 copy-done.9
  19.0 0.0 copy-start.5
  19.0 10.6 %all-to-all-done.received = f32[32,16,128]{2,1,0:T(8,128)S(1)} async-done(((f32[32,16,128]{2,1,0:T(8,128)}), f32[32,16,128]{2,1,0:T(8,128)S(1)}, u32[]{:S(2)}, u32[]{:S(2)}) %all-to-all-start) | async-done | bytes 262176 | tf_op jit(solution)/shard_map/all_to_all | solution.py:479
  29.6 0.0 copy-done.4
  29.6 0.0 copy-done.1
  29.6 0.0 copy-done.3
  29.7 0.0 copy-done.5
  29.7 1.4 %shard_map.122 = (f32[1,3,3,256]{3,2,1,0:T(4,128)S(1)}, f32[1,3,3,256]{3,2,1,0:T(4,128)S(1)}, f32[1,3,16,256]{3,2,1,0:T(8,128)}, f32[1,16,256]{2,1,0:T(8,128)}) custom-call(f32[32,16,128]{2,1,0:T(8,128)S(1)} %all-to-all-done.received, f32[48,256]{1,0:T(8,128)S(1)} %get-tuple-element.21.base, f32[16,256]{1,0:T(8,128)S(1)} %get-tuple-element.22.ends, ...), custom_call_target="tpu_custom_call" | custom-call | tf_op jit(solution)/shard_map/pallas_call | solution.py:432
  31.1 0.6 %copy.21 = f32[1,3,3,256]{3,0,2,1:T(1,128)} copy(f32[1,3,3,256]{3,2,1,0:T(4,128)S(1)} %get-tuple-element.26) | data formatting | bytes 18432 | tf_op jit(solution)/shard_map/pallas_call | solution.py:432
  31.7 0.6 %copy.22 = f32[1,3,3,256]{3,0,2,1:T(1,128)} copy(f32[1,3,3,256]{3,2,1,0:T(4,128)S(1)} %get-tuple-element.27) | data formatting | bytes 18432 | tf_op jit(solution)/shard_map/pallas_call | solution.py:432
  (5 shorter events, 0.0 us)
Async XLA Ops:
  1.3 5.7 %copy-start.8 = (f32[1,3,3,256]{3,0,2,1:T(1,128)S(1)}, f32[1,3,3,256]{3,0,2,1:T(1,128)}, u32[]{:S(2)}) copy-start(f32[1,3,3,256]{3,0,2,1:T(1,128)} %param.11) | copy-start | bytes 27652
  1.3 5.7 %copy-start.6 = (f32[1,16,256]{2,1,0:T(8,128)S(1)}, f32[1,16,256]{2,1,0:T(8,128)}, u32[]{:S(2)}) copy-start(f32[1,16,256]{2,1,0:T(8,128)} %reaction.1) | copy-start | bytes 49156
  1.4 8.3 %collective-permute-start = (f32[3,256]{1,0:T(4,128)S(1)}, f32[3,256]{1,0:T(4,128)S(1)}, u32[]{:S(2)}, u32[]{:S(2)}) collective-permute-start(f32[3,256]{1,0:T(4,128)S(1)} %get-tuple-element.32), channel_id=1, source_target_pairs={{0,8},{8,16},{16,24},{24,0},{1,9},{9,17},{17,25},{25,1},{2,10},{10... | collective-permute-start | bytes 9224 | tf_op jit(solution)/shard_map/ppermute | solution.py:22
  1.9 7.8 %collective-permute-start.1 = (f32[3,256]{1,0:T(4,128)S(1)}, f32[3,256]{1,0:T(4,128)S(1)}, u32[]{:S(2)}, u32[]{:S(2)}) collective-permute-start(f32[3,256]{1,0:T(4,128)S(1)} %get-tuple-element.31), channel_id=1, source_target_pairs={{0,4},{1,5},{2,6},{3,7},{4,0},{5,1},{6,2},{7,3},{8,12},{9,13},{10,... | collective-permute-start | bytes 9224 | tf_op jit(solution)/shard_map/ppermute | solution.py:22
  5.5 1.5 %copy-start.7 = (s32[1,96]{1,0:T(1,128)S(1)}, s32[1,96]{1,0:T(1,128)}, u32[]{:S(2)}) copy-start(s32[1,96]{1,0:T(1,128)} %primal_index.1) | copy-start | bytes 1156
  5.5 6.3 %collective-permute-start.2 = (f32[3,256]{1,0:T(4,128)S(1)}, f32[3,256]{1,0:T(4,128)S(1)}, u32[]{:S(2)}, u32[]{:S(2)}) collective-permute-start(f32[3,256]{1,0:T(4,128)S(1)} %get-tuple-element.30), channel_id=1, source_target_pairs={{0,1},{1,2},{2,3},{3,4},{4,5},{5,6},{6,7},{7,0},{8,9},{9,10},{10,1... | collective-permute-start | bytes 9224 | tf_op jit(solution)/shard_map/ppermute | solution.py:22
  7.1 1.0 %copy-start = (f32[1,96,768]{2,1,0:T(8,128)S(1)}, f32[1,96,768]{2,1,0:T(8,128)}, u32[]{:S(2)}) copy-start(f32[1,96,768]{2,1,0:T(8,128)} %region_inverse.3) | copy-start | bytes 884740
  8.0 0.9 %copy-start.2 = (f32[1,96,384]{2,1,0:T(8,128)S(1)}, f32[1,96,384]{2,1,0:T(8,128)}, u32[]{:S(2)}) copy-start(f32[1,96,384]{2,1,0:T(8,128)} %coarse_map.3) | copy-start | bytes 442372
  11.8 17.8 %copy-start.4 = (f32[384,384]{1,0:T(8,128)S(1)}, f32[384,384]{1,0:T(8,128)}, u32[]{:S(2)}) copy-start(f32[384,384]{1,0:T(8,128)} %global_inverse.1) | copy-start | bytes 1769476
  16.3 13.4 %copy-start.1 = (f32[1,96,768]{2,1,0:T(8,128)S(1)}, f32[1,96,768]{2,1,0:T(8,128)}, u32[]{:S(2)}) copy-start(f32[1,96,768]{2,1,0:T(8,128)} %region_inverse.3) | copy-start | bytes 884740
  16.3 2.7 %copy-start.9 = (f32[1,3,3,256]{3,0,2,1:T(1,128)S(1)}, f32[1,3,3,256]{3,0,2,1:T(1,128)}, u32[]{:S(2)}) copy-start(f32[1,3,3,256]{3,0,2,1:T(1,128)} %param.9) | copy-start | bytes 27652
  16.3 13.4 %copy-start.3 = (f32[1,96,384]{2,1,0:T(8,128)S(1)}, f32[1,96,384]{2,1,0:T(8,128)}, u32[]{:S(2)}) copy-start(f32[1,96,384]{2,1,0:T(8,128)} %coarse_map.3) | copy-start | bytes 442372
  16.3 13.4 %all-to-all-start = ((f32[32,16,128]{2,1,0:T(8,128)}), f32[32,16,128]{2,1,0:T(8,128)S(1)}, u32[]{:S(2)}, u32[]{:S(2)}) async-start(f32[32,16,128]{2,1,0:T(8,128)} %get-tuple-element.20), calls=%async_computation | async-start | bytes 524288 | tf_op jit(solution)/shard_map/all_to_all | solution.py:479
  19.0 10.7 %copy-start.5 = (f32[1,16,256]{2,1,0:T(8,128)S(1)}, f32[1,16,256]{2,1,0:T(8,128)}, u32[]{:S(2)}) copy-start(f32[1,16,256]{2,1,0:T(8,128)} %viscosity.1) | copy-start | bytes 49156

commit v2 on v1

v2 whole, which is shorter than its diff:
```python
import functools

import jax
import jax.numpy as jnp
from jax import lax
from jax.experimental import pallas as pl
from jax.experimental.pallas import tpu as pltpu
from jax.sharding import PartitionSpec as P

DOM_Z = 4
LEVELS = 3
SWEEPS = 1
COARSE_SWEEPS = 8
VCYCLES = 2
LANES = 128

damping = 0.8


def shifted_2(x, axis, by):
    count = lax.axis_size(axis)
    return lax.ppermute(x, axis, [(i, (i + by) % count) for i in range(count)])


def iota(shape, dim):
    return lax.broadcasted_iota(jnp.int32, shape, dim)


def parts_of(x, count=3):
    result = []
    for step in range(count):
        piece = x.astype(jnp.bfloat16)
        result.append(piece)
        if step < count - 1:
            x = x - piece.astype(jnp.float32)
    return result


def times_choice(x, choice):
    rows = x.shape[0]
    stacked = jnp.concatenate(parts_of(x), axis=0)
    y = jnp.dot(stacked, choice, preferred_element_type=jnp.float32)
    return y[:rows] + y[rows : 2 * rows] + y[2 * rows :]


def choice_times(choice, x):
    width = x.shape[1]
    stacked = jnp.concatenate(parts_of(x), axis=1)
    y = jnp.dot(choice, stacked, preferred_element_type=jnp.float32)
    return y[:, :width] + y[:, width : 2 * width] + y[:, 2 * width :]


def one_hot(condition):
    return jnp.where(condition, 1.0, 0.0).astype(jnp.bfloat16)


def decode(picked, cells):
    face = cells * cells
    zero = jnp.zeros_like(picked)
    one = zero + 1
    block = jnp.where(picked >= 3 * face, one, zero) + jnp.where(picked >= 6 * face, one, zero)
    rest = picked - 3 * face * block
    component = jnp.where(rest >= face, one, zero) + jnp.where(rest >= 2 * face, one, zero)
    spot = rest - face * component
    first = lax.div(spot, zero + cells)
    second = spot - first * cells
    end = cells - 1
    x = jnp.where(block == 0, end, first)
    y = jnp.where(block == 0, first, jnp.where(block == 1, end, second))
    z = jnp.where(block == 2, end, second)
    return 3 * block + component, spot, component * cells + x, y * cells + z


def faces_of(rows):
    return [jnp.concatenate([rows[3 * d + c] for c in range(3)], axis=0) for d in range(3)]


def spread(faces, cells):
    face = cells * cells
    here = lax.div(iota((cells, face), 1), jnp.full((cells, face), cells, jnp.int32)) == iota((cells, face), 0)
    rows = [jnp.where(here, jnp.broadcast_to(faces[c : c + 1], (cells, face)), 0.0) for c in range(faces.shape[0])]
    return jnp.concatenate(rows, axis=0)


def mask_sum(x, cells):
    face = cells * cells
    here = lax.div(iota((cells, face), 1), jnp.full((cells, face), cells, jnp.int32)) == iota((cells, face), 0)
    rows = [
        jnp.sum(jnp.where(here, x[c * cells : (c + 1) * cells], 0.0), axis=0, keepdims=True)
        for c in range(x.shape[0] // cells)
    ]
    return jnp.concatenate(rows, axis=0)


def place_matrix(cells, upper):
    face = cells * cells
    row = iota((face, face), 0)
    column = iota((face, face), 1)
    second = row & (cells - 1)
    end = cells - 1 if upper else 0
    return jnp.concatenate(
        [one_hot(column == second + end * cells), one_hot(column == second * cells + end)], axis=0
    )


def pick_matrix(cells, upper):
    face = cells * cells
    row = iota((face, face), 0)
    column = iota((face, face), 1)
    second = column & (cells - 1)
    end = cells - 1 if upper else 0
    return jnp.concatenate(
        [one_hot(row == second + end * cells), one_hot(row == second * cells + end)], axis=1
    )


def face_ends(field, pick, cells, upper):
    face = cells * cells
    at = cells - 1 if upper else 0
    ends = times_choice(field, pick)
    on_x = [field[c * cells + at : c * cells + at + 1] for c in range(3)]
    return jnp.concatenate(on_x, axis=0), mask_sum(ends[:, :face], cells), mask_sum(ends[:, face:], cells)


def column_of(line):
    count = line.shape[1]
    wide = jnp.broadcast_to(line.astype(jnp.float32), (count, count))
    diagonal = iota((count, count), 0) == iota((count, count), 1)
    return jnp.sum(jnp.where(diagonal, wide, 0.0), axis=1, keepdims=True).astype(jnp.int32)


def shift(field, by, dim):
    size = field.shape[dim]
    return pltpu.roll(field, by % size, dim)


def pair_mean(field, cells, step, where_x, where_y, where_z):
    for position, dim, reach in ((where_z, 1, step), (where_y, 1, step * cells), (where_x, 0, step)):
        even = (position & step) == 0
        field = 0.5 * (field + jnp.where(even, shift(field, -reach, dim), shift(field, reach, dim)))
    return field


def positions(rows, cells):
    face = cells * cells
    shape = (rows, face)
    lane = iota(shape, 1)
    row = iota(shape, 0)
    where_x = row & (cells - 1)
    where_z = lane & (cells - 1)
    where_y = lax.shift_right_logical(lane, jnp.full(shape, cells.bit_length() - 1, jnp.int32))
    return where_x, where_y, where_z


def load(pairs, semaphores):
    copies = [pltpu.make_async_copy(a, b, semaphores.at[i]) for i, (a, b) in enumerate(pairs)]
    for copy in copies:
        copy.start()
    return copies


def before_kernel(
    cells,
    sizes,
    direction_in,
    residual_in,
    reaction_in,
    primal_index_in,
    region_inverse_in,
    coarse_map_in,
    direction,
    residual,
    source_out,
    front_out,
    inverse_out,
    lower_out,
    upper_out,
    pick_out,
    reaction,
    primal_index,
    region_inverse,
    coarse_map,
    semaphores,
):
    copies = load(
        [
            (direction_in, direction),
            (reaction_in, reaction),
            (primal_index_in, primal_index),
            (residual_in, residual),
            (coarse_map_in, coarse_map),
            (region_inverse_in, region_inverse),
        ],
        semaphores,
    )
    face = cells * cells
    n_sub = sizes[1]
    lower_out[...] = place_matrix(cells, False)
    upper = place_matrix(cells, True)
    upper_out[...] = upper
    pick_out[...] = pick_matrix(cells, False)
    for copy in copies:
        copy.wait()
    where_x, where_y, where_z = positions(cells, cells)
    react = reaction[0]
    for level in range(LEVELS):
        weight = 0.25**level
        diagonal = react + 6.0 * weight
        inverse_out[level] = damping / diagonal
        inverse_out[LEVELS + level] = diagonal
        if level < LEVELS - 1:
            react = pair_mean(react, cells, 2**level, where_x, where_y, where_z)
    faces = faces_of(direction)
    row_x = iota((cells, face), 0)
    source = times_choice(jnp.concatenate([spread(faces[1], cells), spread(faces[2], cells)], axis=1), upper)
    own_x = jnp.concatenate(
        [jnp.where(row_x == cells - 1, jnp.broadcast_to(faces[0][c : c + 1], (cells, face)), 0.0) for c in range(3)],
        axis=0,
    )
    source_out[...] = source + own_x
    count = primal_index.shape[1]
    group, spot, _, _ = decode(column_of(primal_index[...]), cells)
    nine = jnp.concatenate(faces + [jnp.zeros((7, face), jnp.float32)], axis=0)
    gathered = choice_times(one_hot(iota((count, 16), 1) == group), nine)
    primal = jnp.sum(jnp.where(iota((count, face), 1) == spot, gathered, 0.0), axis=1, keepdims=True)
    share = jnp.sum(primal * coarse_map[0], axis=0, keepdims=True)
    product = jnp.sum(primal * region_inverse[0], axis=0, keepdims=True)
    lane = iota((1, LANES), 1)
    line = jnp.sum(
        jnp.where(iota((count, LANES), 0) == iota((count, LANES), 1), primal, 0.0), axis=0, keepdims=True
    )
    blank = jnp.zeros((1, LANES - count), jnp.float32)
    blocks = jnp.concatenate(
        [jnp.concatenate([product[:, q * count : (q + 1) * count], blank], axis=1) for q in range(n_sub)], axis=0
    )
    me_sub = lax.axis_index("sub")
    own = jnp.sum(jnp.where(iota(blocks.shape, 0) == me_sub, blocks * line, 0.0))
    blocks = pltpu.roll(blocks, n_sub - 1 - me_sub, 0)
    half = n_sub // 2
    twice = jnp.where(iota((half, LANES), 0) == (half - 1 if n_sub % 2 == 0 else half), 1.0, 2.0)
    squares = jnp.sum(residual[...] * residual[...])
    line = jnp.where(lane == count, own, jnp.where(lane == count + 1, squares, line))
    front_out[...] = jnp.zeros_like(front_out)
    front_out[:half, :] = blocks[:half] * twice
    front_out[half : half + 1, :] = line
    for i in range(share.shape[1] // LANES):
        front_out[half + 1 + i : half + 2 + i, :] = share[:, i * LANES : (i + 1) * LANES]


def solve_kernel(
    cells,
    sizes,
    count,
    source_own,
    from_x,
    from_y,
    from_z,
    inverses,
    front,
    lower,
    base_out,
    send_out,
):
    face = cells * cells
    rows = 3 * cells
    below_x, below_y, below_z = [faces_of(ref)[d] for d, ref in enumerate((from_x, from_y, from_z))]
    n_region, n_sub = sizes
    row_x = iota((cells, face), 0)
    source = source_own[...] - times_choice(
        jnp.concatenate([spread(below_y, cells), spread(below_z, cells)], axis=1), lower[...]
    )
    source = source - jnp.concatenate(
        [jnp.where(row_x == 0, jnp.broadcast_to(below_x[c : c + 1], (cells, face)), 0.0) for c in range(3)],
        axis=0,
    )
    where_x, where_y, where_z = positions(rows, cells)

    def tall(x):
        return jnp.concatenate([x] * 3, axis=0)

    inverse = [tall(inverses[level]) for level in range(LEVELS)]
    diagonal = [tall(inverses[LEVELS + level]) for level in range(LEVELS)]

    def beside(field, level):
        step = 2**level
        last = cells - step
        total = jnp.where(where_x < last, shift(field, -step, 0), 0.0)
        total = total + jnp.where(where_x >= step, shift(field, step, 0), 0.0)
        total = total + jnp.where(where_y < last, shift(field, -step * cells, 1), 0.0)
        total = total + jnp.where(where_y >= step, shift(field, step * cells, 1), 0.0)
        total = total + jnp.where(where_z < last, shift(field, -step, 1), 0.0)
        return total + jnp.where(where_z >= step, shift(field, step, 1), 0.0)

    def relax(field, right, level, sweeps):
        weight = 0.25**level
        for _ in range(sweeps):
            if field is None:
                field = inverse[level] * right
            else:
                field = (1.0 - damping) * field + inverse[level] * (right + weight * beside(field, level))
        return field

    def vcycle(field, right, level):
        if level == LEVELS - 1:
            return relax(field, right, level, COARSE_SWEEPS)
        field = relax(field, right, level, SWEEPS)
        remain = right - diagonal[level] * field + 0.25**level * beside(field, level)
        remain = pair_mean(remain, cells, 2**level, where_x, where_y, where_z)
        field = field + vcycle(None, remain, level + 1)
        return relax(field, right, level, SWEEPS)

    field = None
    for _ in range(VCYCLES):
        field = vcycle(field, source, 0)
    base_out[...] = field
    energy = jnp.sum(source * field)
    message = front[...]
    at = (iota(message.shape, 0) == sizes[1] // 2) & (iota(message.shape, 1) == count)
    message = message + jnp.where(at, energy, 0.0)
    for device in range(sizes[0] * sizes[1]):
        send_out[device] = message


def ends_kernel(cells, base, pick, lower_x, lower_y, lower_z):
    lower_x[...], lower_y[...], lower_z[...] = face_ends(base[...], pick[...], cells, False)


def between_kernel(
    cells,
    base,
    primal_index_in,
    region_inverse_in,
    coarse_map_in,
    global_inverse_in,
    multipliers_in,
    viscosity_in,
    multipliers,
    viscosity,
    ends_out,
    region_out,
    through_out,
    global_out,
    spots_out,
    choose_out,
    primal_index,
    region_inverse,
    coarse_map,
    global_inverse,
    semaphores,
):
    copies = load(
        [
            (primal_index_in, primal_index),
            (region_inverse_in, region_inverse),
            (coarse_map_in, coarse_map),
            (global_inverse_in, global_inverse),
            (multipliers_in, multipliers),
            (viscosity_in, viscosity),
        ],
        semaphores,
    )
    face = cells * cells
    on_x, on_y, on_z = face_ends(base[...], pick_matrix(cells, True), cells, True)
    ends_out[...] = jnp.concatenate([on_x, on_y, on_z, jnp.zeros((7, face), jnp.float32)], axis=0)
    for copy in copies:
        copy.wait()
    count = primal_index.shape[1]
    group, _, place, _ = decode(primal_index[...], cells)
    choose_out[...] = jnp.concatenate(
        [one_hot(iota((3 * cells, count), 0) == place), one_hot(iota((16, count), 0) == group)], axis=0
    )
    _, spot, _, lane = decode(column_of(primal_index[...]), cells)
    at = iota((count, face), 1)
    spots_out[...] = jnp.concatenate([jnp.where(at == lane, 1.0, 0.0), jnp.where(at == spot, 1.0, 0.0)], axis=1)
    blank = jnp.zeros((count, LANES - count), jnp.float32)
    for q in range(region_out.shape[0]):
        region_out[q] = jnp.concatenate([region_inverse[0, :, q * count : (q + 1) * count], blank], axis=1)
    through_out[...] = jnp.dot(
        coarse_map[0], global_inverse[...], precision=lax.Precision.HIGHEST, preferred_element_type=jnp.float32
    )
    global_out[...] = jnp.concatenate(parts_of(global_inverse[...], 2), axis=1)


def after_kernel(
    cells,
    sizes,
    count,
    received,
    base,
    ends,
    after_x,
    after_y,
    after_z,
    upper,
    spots,
    choose,
    region_blocks,
    through,
    global_parts,
    direction,
    multipliers,
    residual,
    viscosity,
    multipliers_out,
    residual_out,
    velocity_out,
    pressure_out,
):
    face = cells * cells
    n_region, n_sub = sizes
    half = n_sub // 2
    columns = through.shape[1]
    me_region = lax.axis_index("region")
    everything = jnp.sum(received[...], axis=0)
    totals = [everything[half + 1 + i : half + 2 + i] for i in range(columns // LANES)]
    total = jnp.concatenate(totals, axis=1)
    added = jnp.zeros((count, LANES), jnp.float32)
    for i, part in enumerate(totals):
        added = added + through[:, i * LANES : (i + 1) * LANES] * part
    for q in range(n_sub):
        added = added + region_blocks[q] * received[me_region * n_sub + q, half : half + 1, :]
    lifted = jnp.sum(added, axis=1, keepdims=True)
    added = choice_times(choose[...], lifted * spots[...])
    velocity = base[...] + added[: 3 * cells, :face]
    upper_faces = ends[:9] + added[3 * cells : 3 * cells + 9, face:]
    for c in range(3):
        velocity_out[0, c] = velocity[c * cells : (c + 1) * cells]
    after = [after_x[...], after_y[...], after_z[...]]
    ahead = jnp.concatenate([spread(after[1][1:2], cells), spread(after[2][2:3], cells)], axis=1)
    ahead = times_choice(ahead, upper[...])
    where_x, where_y, where_z = positions(cells, cells)
    end = cells - 1
    field_x, field_y, field_z = [velocity[c * cells : (c + 1) * cells] for c in range(3)]
    step_x = jnp.where(where_x == end, jnp.broadcast_to(after[0][0:1], (cells, face)), shift(field_x, -1, 0))
    step_y = jnp.where(where_y == end, 0.0, shift(field_y, -cells, 1))
    step_z = jnp.where(where_z == end, 0.0, shift(field_z, -1, 1))
    step = (step_x - field_x) + (step_y - field_y) + (step_z - field_z) + ahead
    pressure_out[0] = -viscosity[0] * step
    piece = total.astype(jnp.bfloat16).astype(jnp.float32)
    row = iota((16, columns), 0)
    parts = jnp.where(row == 0, piece, jnp.where(row == 1, total - piece, 0.0)).astype(jnp.bfloat16)
    top = jnp.dot(parts, global_parts[...], preferred_element_type=jnp.float32)
    top = top[0:1, :columns] + top[1:2, :columns] + top[0:1, columns:]
    lines = received[:, half, :].reshape(n_region, n_sub, LANES)
    quadratic = jnp.zeros((n_region, n_sub, LANES), jnp.float32)
    for k in range(half):
        products = received[:, k, :].reshape(n_region, n_sub, LANES)
        quadratic = quadratic + products * pltpu.roll(lines, n_sub - 1 - k, 1)
    own_line = everything[half : half + 1]
    lane = iota((1, LANES), 1)
    quadratic = jnp.sum(quadratic.reshape(n_region * n_sub, LANES), axis=0, keepdims=True)
    curvature = quadratic + jnp.where(lane == count, own_line, 0.0)
    for i in range(columns // LANES):
        curvature = curvature + totals[i] * top[:, i * LANES : (i + 1) * LANES]
    curvature = jnp.sum(curvature, axis=1, keepdims=True)
    squares = jnp.sum(jnp.where(lane == count + 1, own_line, 0.0), axis=1, keepdims=True)
    alpha = squares / curvature
    for d in range(3):
        jump = upper_faces[3 * d : 3 * d + 3] - after[d]
        for c in range(3):
            residual_out[3 * d + c] = residual[3 * d + c] - alpha * jump[c : c + 1]
            multipliers_out[3 * d + c] = multipliers[3 * d + c] + alpha * direction[3 * d + c]


def body(
    sizes,
    multipliers,
    direction,
    residual,
    reaction,
    viscosity,
    primal_index,
    region_inverse,
    coarse_map,
    global_inverse,
):
    n_region, n_sub = sizes
    cells = reaction.shape[1]
    face = reaction.shape[2]
    count = primal_index.shape[1]
    columns = coarse_map.shape[2]
    height = -(-(n_sub // 2 + 1 + columns // LANES) // 8) * 8
    rows = 3 * cells
    shape = direction.shape
    lines = (9, 1, face)
    f32 = jnp.float32
    bf16 = jnp.bfloat16
    vmem = pl.BlockSpec(memory_space=pltpu.VMEM)
    hbm = pl.BlockSpec(memory_space=pltpu.HBM)

    def like(shape, kind=f32):
        return jax.ShapeDtypeStruct(shape, kind)

    def call(kernel, out_shape, operands, in_hbm=(), scratch=()):
        return pl.pallas_call(
            kernel,
            out_shape=out_shape,
            in_specs=[vmem] * len(operands) + [hbm] * len(in_hbm),
            out_specs=[vmem] * len(out_shape),
            scratch_shapes=[pltpu.VMEM(x.shape, x.dtype) for x in scratch]
            + ([pltpu.SemaphoreType.DMA((len(in_hbm),))] if in_hbm else []),
            compiler_params=pltpu.CompilerParams(vmem_limit_bytes=32 * 1024 * 1024),
        )(*operands, *[pltpu.with_memory_space_constraint(x, pltpu.HBM) for x in in_hbm])

    below_x = shifted_2(direction, "region", 1).reshape(lines)
    below_y = shifted_2(direction, "sub", DOM_Z).reshape(lines)
    below_z = shifted_2(direction, "sub", 1).reshape(lines)
    multipliers, direction, residual = [x.reshape(lines) for x in (multipliers, direction, residual)]
    direction, residual, source, front, inverses, lower, upper, pick = call(
        functools.partial(before_kernel, cells, sizes),
        [
            like(lines),
            like(lines),
            like((rows, face)),
            like((height, LANES)),
            like((2 * LEVELS, cells, face)),
            like((2 * face, face), bf16),
            like((2 * face, face), bf16),
            like((face, 2 * face), bf16),
        ],
        [],
        [direction, residual, reaction, primal_index, region_inverse, coarse_map],
        [reaction, primal_index, region_inverse, coarse_map],
    )
    base, sent = call(
        functools.partial(solve_kernel, cells, sizes, count),
        [like((rows, face)), like((n_region * n_sub, height, LANES))],
        [source, below_x, below_y, below_z, inverses, front, lower],
    )
    received = lax.all_to_all(sent, ("region", "sub"), 0, 0, tiled=True)
    lower_x, lower_y, lower_z = call(
        functools.partial(ends_kernel, cells), [like((3, face))] * 3, [base, pick]
    )
    after_x = shifted_2(lower_x, "region", -1)
    after_y = shifted_2(lower_y, "sub", -DOM_Z)
    after_z = shifted_2(lower_z, "sub", -1)
    multipliers, viscosity, ends, region_blocks, through, global_parts, spots, choose = call(
        functools.partial(between_kernel, cells),
        [
            like(lines),
            like(viscosity.shape),
            like((16, face)),
            like((n_sub, count, LANES)),
            like((count, columns)),
            like((columns, 2 * columns), bf16),
            like((count, 2 * face)),
            like((rows + 16, count), bf16),
        ],
        [base],
        [primal_index, region_inverse, coarse_map, global_inverse, multipliers, viscosity],
        [primal_index, region_inverse, coarse_map, global_inverse],
    )
    new_multipliers, new_residual, velocity, pressure = call(
        functools.partial(after_kernel, cells, sizes, count),
        [like(lines), like(lines), like((1, 3, cells, face)), like((1, cells, face))],
        [
            received,
            base,
            ends,
            after_x,
            after_y,
            after_z,
            upper,
            spots,
            choose,
            region_blocks,
            through,
            global_parts,
            direction,
            multipliers,
            residual,
            viscosity,
        ],
    )
    return new_multipliers.reshape(shape), new_residual.reshape(shape), velocity, pressure


def solution(mesh):
    sizes = (mesh.shape["region"], mesh.shape["sub"])
    whole = P(("region", "sub"))
    in_specs = (whole,) * 6 + (P("region", "sub"), whole, P())
    return jax.shard_map(
        functools.partial(body, sizes), mesh=mesh, in_specs=in_specs, out_specs=(whole,) * 4, check_vma=False
    )
```

time: 32.6 us -> 27.4 us (0.84)
  waiting for transfers between devices: 12.8 us -> 0.56 us
  starting transfers between devices: 8.4 us -> 16.8 us
  local copies, waits for them, and re-layouts: 3.84 us -> 0 us
  Pallas kernels: 6.54 us -> 9.14 us
    all_to_all x1, waiting for transfers between devices: 10.6 us -> 0.01 us  [body(): received = lax.all_to_all(sent, ('region', 'sub'), 0, 0, tiled=True)]
    ppermute x3 -> x6, starting transfers between devices: 5.69 us -> 12 us  [shifted_2(): return lax.ppermute(x, axis, [(i, (i + by) % count) for i in range(count)])]
    unnamed x23 -> x0, local copies, waits for them, and re-layouts: 2.62 us -> none
    pallas_call x3 -> x5, Pallas kernels: 6.54 us -> 9.14 us  [call(): pl.pallas_call(kernel, out_shape=out_shape, in_specs=[vmem] * len(operand...]
    all_to_all x1, starting transfers between devices: 2.71 us -> 4.78 us  [body(): received = lax.all_to_all(sent, ('region', 'sub'), 0, 0, tiled=True)]
    ppermute x3 -> x6, waiting for transfers between devices: 2.19 us -> 0.56 us  [shifted_2(): return lax.ppermute(x, axis, [(i, (i + by) % count) for i in range(count)])]
    pallas_call x2 -> x0, local copies, waits for them, and re-layouts: 1.22 us -> none  [call(): pl.pallas_call(kernel, out_shape=out_shape, in_specs=[vmem] * len(operand...]
  transfers between devices with their start and end apart: 4 -> 7, of which waited for: 2 -> 1; matrix products, arithmetic and copies ran while one was open for 0% -> 0% of each run, Pallas kernels for 2% -> 14%
where the time goes in v2:
time: 27.4 us; the launch traced here: 27.2 us
  starting transfers between devices  16.8 us (61%)
  Pallas kernels  9.14 us (33%)
  between operations  0.71 us (3%)
  waiting for transfers between devices  0.56 us (2%)
    ppermute x6, starting transfers between devices, shifted_2(): return lax.ppermute(x, axis, [(i, (i + by) % count) for i in range(count)])  12 us
    pallas_call x5, Pallas kernels, call(): pl.pallas_call(kernel, out_shape=out_shape, in_specs=[vmem] * len(operand...  9.14 us
    all_to_all x1, starting transfers between devices, body(): received = lax.all_to_all(sent, ('region', 'sub'), 0, 0, tiled=True)  4.78 us
    ppermute x6, waiting for transfers between devices, shifted_2(): return lax.ppermute(x, axis, [(i, (i + by) % count) for i in range(count)])  0.56 us
  transfers between devices with their start and end apart: 7, of which 1 were waited for; matrix products, arithmetic and copies ran while one was open for 0% of the time, Pallas kernels for 14%

profile of v2, /device:TPU:0, one launch (start us, length us, event | category | flops | bytes accessed | tf_op | source)
XLA Modules:
  0.0 27.2 jit_solution(17386332673681557107)
XLA Ops:
  0.6 0.5 %collective-permute-start = (f32[1,3,3,256]{3,0,2,1:T(1,128)}, f32[1,3,3,256]{3,0,2,1:T(1,128)S(1)}, u32[]{:S(2)}, u32[]{:S(2)}) collective-permute-start(f32[1,3,3,256]{3,0,2,1:T(1,128)} %param.10), channel_id=1, source_target_pairs={{0,8},{8,16},{16,24},{24,0},{1,9},{9,17},{17,25},{25,1},{2,10},{10... | collective-permute-start | bytes 27656 | tf_op jit(solution)/shard_map/ppermute | solution.py:22
  1.1 2.6 %collective-permute-start.2 = (f32[1,3,3,256]{3,0,2,1:T(1,128)}, f32[1,3,3,256]{3,0,2,1:T(1,128)S(1)}, u32[]{:S(2)}, u32[]{:S(2)}) collective-permute-start(f32[1,3,3,256]{3,0,2,1:T(1,128)} %param.10), channel_id=1, source_target_pairs={{0,1},{1,2},{2,3},{3,4},{4,5},{5,6},{6,7},{7,0},{8,9},{9,10},{10,1... | collective-permute-start | bytes 27656 | tf_op jit(solution)/shard_map/ppermute | solution.py:22
  3.7 2.6 %collective-permute-start.1 = (f32[1,3,3,256]{3,0,2,1:T(1,128)}, f32[1,3,3,256]{3,0,2,1:T(1,128)S(1)}, u32[]{:S(2)}, u32[]{:S(2)}) collective-permute-start(f32[1,3,3,256]{3,0,2,1:T(1,128)} %param.10), channel_id=1, source_target_pairs={{0,4},{1,5},{2,6},{3,7},{4,0},{5,1},{6,2},{7,3},{8,12},{9,13},{10,... | collective-permute-start | bytes 27656 | tf_op jit(solution)/shard_map/ppermute | solution.py:22
  6.3 1.7 %shard_map.120 = (f32[9,1,256]{2,1,0:T(1,128)S(1)}, f32[9,1,256]{2,1,0:T(1,128)S(1)}, f32[48,256]{1,0:T(8,128)S(1)}, f32[8,128]{1,0:T(8,128)S(1)}, f32[6,16,256]...) custom-call(f32[9,1,256]{2,1,0:T(1,128)} %bitcast.13, ...), custom_call_target="tpu_custom_call" | custom-call | tf_op jit(solution)/shard_map/pallas_call | solution.py:495
  8.0 0.0 collective-permute-done
  8.1 0.5 %collective-permute-done.2 = f32[1,3,3,256]{3,0,2,1:T(1,128)S(1)} collective-permute-done((f32[1,3,3,256]{3,0,2,1:T(1,128)}, f32[1,3,3,256]{3,0,2,1:T(1,128)S(1)}, u32[]{:S(2)}, u32[]{:S(2)}) %collective-permute-start.2) | collective-permute-done | bytes 9248 | tf_op jit(solution)/shard_map/ppermute | solution.py:22
  8.6 0.0 collective-permute-done.1
  8.6 4.1 %shard_map.121 = (f32[48,256]{1,0:T(8,128)S(1)}, f32[32,8,128]{2,1,0:T(8,128)}) custom-call(f32[48,256]{1,0:T(8,128)S(1)} %get-tuple-element.29.source_own, f32[9,1,256]{2,1,0:T(1,128)S(1)} %bitcast.8, f32[9,1,256]{2,1,0:T(1,128)S(1)} %bitcast.10, f32[9,1,256]{2,1,0:T(1,128)S(1)} %bitcast.9, f32[6,16,256]{2,1,0:T(8,128)S(1)} %get-tuple-element.30.inverses, ...), custom_call_target="tpu_custom_call" | custom-call | tf_op jit(solution)/shard_map/pallas_call | solution.py:495
  12.7 4.8 %all-to-all-start = ((f32[32,8,128]{2,1,0:T(8,128)}), f32[32,8,128]{2,1,0:T(8,128)S(1)}, u32[]{:S(2)}, u32[]{:S(2)}) async-start(f32[32,8,128]{2,1,0:T(8,128)} %get-tuple-element.33), calls=%async_computation | async-start | bytes 262144 | tf_op jit(solution)/shard_map/all_to_all | solution.py:530
  17.5 0.2 shard_map.123
  17.7 1.6 %collective-permute-start.3 = (f32[3,256]{1,0:T(4,128)S(1)}, f32[3,256]{1,0:T(4,128)S(1)}, u32[]{:S(2)}, u32[]{:S(2)}) collective-permute-start(f32[3,256]{1,0:T(4,128)S(1)} %get-tuple-element.37), channel_id=1, source_target_pairs={{0,24},{8,0},{16,8},{24,16},{1,25},{9,1},{17,9},{25,17},{2,26},{10... | collective-permute-start | bytes 9224 | tf_op jit(solution)/shard_map/ppermute | solution.py:22
  19.2 2.4 %collective-permute-start.4 = (f32[3,256]{1,0:T(4,128)S(1)}, f32[3,256]{1,0:T(4,128)S(1)}, u32[]{:S(2)}, u32[]{:S(2)}) collective-permute-start(f32[3,256]{1,0:T(4,128)S(1)} %get-tuple-element.38), channel_id=1, source_target_pairs={{0,4},{1,5},{2,6},{3,7},{4,0},{5,1},{6,2},{7,3},{8,12},{9,13},{10,... | collective-permute-start | bytes 9224 | tf_op jit(solution)/shard_map/ppermute | solution.py:22
  21.6 2.4 %collective-permute-start.5 = (f32[3,256]{1,0:T(4,128)S(1)}, f32[3,256]{1,0:T(4,128)S(1)}, u32[]{:S(2)}, u32[]{:S(2)}) collective-permute-start(f32[3,256]{1,0:T(4,128)S(1)} %get-tuple-element.39), channel_id=1, source_target_pairs={{0,7},{1,0},{2,1},{3,2},{4,3},{5,4},{6,5},{7,6},{8,15},{9,8},{10,9... | collective-permute-start | bytes 9224 | tf_op jit(solution)/shard_map/ppermute | solution.py:22
  24.0 2.0 %shard_map.122 = (f32[9,1,256]{2,1,0:T(1,128)S(1)}, f32[1,16,256]{2,1,0:T(8,128)S(1)}, f32[16,256]{1,0:T(8,128)S(1)}, f32[8,96,128]{2,1,0:T(8,128)S(1)}, f32[96,...) custom-call(f32[48,256]{1,0:T(8,128)S(1)} %get-tuple-element.34.base, ...), custom_call_target="tpu_custom_call" | custom-call | tf_op jit(solution)/shard_map/pallas_call | solution.py:495
  26.0 0.0 collective-permute-done.3.after_x
  26.0 0.0 collective-permute-done.4.after_y
  26.0 0.0 collective-permute-done.5.after_z
  26.0 0.0 all-to-all-done.received
  26.0 1.2 %shard_map.124 = (f32[9,1,256]{2,1,0:T(1,128)}, f32[9,1,256]{2,1,0:T(1,128)}, f32[1,3,16,256]{3,2,1,0:T(8,128)}, f32[1,16,256]{2,1,0:T(8,128)}) custom-call(f32[32,8,128]{2,1,0:T(8,128)S(1)} %all-to-all-done.received, f32[48,256]{1,0:T(8,128)S(1)} %get-tuple-element.34.base, f32[16,256]{1,0:T(8,128)S(1)} %get-tuple-element.35.ends, ...), custom_call_target="tpu_custom_call" | custom-call | tf_op jit(solution)/shard_map/pallas_call | solution.py:495
Async XLA Ops:
  0.6 7.4 %collective-permute-start = (f32[1,3,3,256]{3,0,2,1:T(1,128)}, f32[1,3,3,256]{3,0,2,1:T(1,128)S(1)}, u32[]{:S(2)}, u32[]{:S(2)}) collective-permute-start(f32[1,3,3,256]{3,0,2,1:T(1,128)} %param.10), channel_id=1, source_target_pairs={{0,8},{8,16},{16,24},{24,0},{1,9},{9,17},{17,25},{25,1},{2,10},{10... | collective-permute-start | bytes 27656 | tf_op jit(solution)/shard_map/ppermute | solution.py:22
  1.1 7.5 %collective-permute-start.2 = (f32[1,3,3,256]{3,0,2,1:T(1,128)}, f32[1,3,3,256]{3,0,2,1:T(1,128)S(1)}, u32[]{:S(2)}, u32[]{:S(2)}) collective-permute-start(f32[1,3,3,256]{3,0,2,1:T(1,128)} %param.10), channel_id=1, source_target_pairs={{0,1},{1,2},{2,3},{3,4},{4,5},{5,6},{6,7},{7,0},{8,9},{9,10},{10,1... | collective-permute-start | bytes 27656 | tf_op jit(solution)/shard_map/ppermute | solution.py:22
  3.7 4.9 %collective-permute-start.1 = (f32[1,3,3,256]{3,0,2,1:T(1,128)}, f32[1,3,3,256]{3,0,2,1:T(1,128)S(1)}, u32[]{:S(2)}, u32[]{:S(2)}) collective-permute-start(f32[1,3,3,256]{3,0,2,1:T(1,128)} %param.10), channel_id=1, source_target_pairs={{0,4},{1,5},{2,6},{3,7},{4,0},{5,1},{6,2},{7,3},{8,12},{9,13},{10,... | collective-permute-start | bytes 27656 | tf_op jit(solution)/shard_map/ppermute | solution.py:22
  12.7 13.3 %all-to-all-start = ((f32[32,8,128]{2,1,0:T(8,128)}), f32[32,8,128]{2,1,0:T(8,128)S(1)}, u32[]{:S(2)}, u32[]{:S(2)}) async-start(f32[32,8,128]{2,1,0:T(8,128)} %get-tuple-element.33), calls=%async_computation | async-start | bytes 262144 | tf_op jit(solution)/shard_map/all_to_all | solution.py:530
  17.7 8.3 %collective-permute-start.3 = (f32[3,256]{1,0:T(4,128)S(1)}, f32[3,256]{1,0:T(4,128)S(1)}, u32[]{:S(2)}, u32[]{:S(2)}) collective-permute-start(f32[3,256]{1,0:T(4,128)S(1)} %get-tuple-element.37), channel_id=1, source_target_pairs={{0,24},{8,0},{16,8},{24,16},{1,25},{9,1},{17,9},{25,17},{2,26},{10... | collective-permute-start | bytes 9224 | tf_op jit(solution)/shard_map/ppermute | solution.py:22
  19.2 6.7 %collective-permute-start.4 = (f32[3,256]{1,0:T(4,128)S(1)}, f32[3,256]{1,0:T(4,128)S(1)}, u32[]{:S(2)}, u32[]{:S(2)}) collective-permute-start(f32[3,256]{1,0:T(4,128)S(1)} %get-tuple-element.38), channel_id=1, source_target_pairs={{0,4},{1,5},{2,6},{3,7},{4,0},{5,1},{6,2},{7,3},{8,12},{9,13},{10,... | collective-permute-start | bytes 9224 | tf_op jit(solution)/shard_map/ppermute | solution.py:22
  21.6 4.4 %collective-permute-start.5 = (f32[3,256]{1,0:T(4,128)S(1)}, f32[3,256]{1,0:T(4,128)S(1)}, u32[]{:S(2)}, u32[]{:S(2)}) collective-permute-start(f32[3,256]{1,0:T(4,128)S(1)} %get-tuple-element.39), channel_id=1, source_target_pairs={{0,7},{1,0},{2,1},{3,2},{4,3},{5,4},{6,5},{7,6},{8,15},{9,8},{10,9... | collective-permute-start | bytes 9224 | tf_op jit(solution)/shard_map/ppermute | solution.py:22

commit v3 on v2

--- a/solution.py
+++ b/solution.py
@@ -36,18 +36,29 @@
     return result
 
 
-def times_choice(x, choice):
+def times_choice(x, choice, count=2):
     rows = x.shape[0]
-    stacked = jnp.concatenate(parts_of(x), axis=0)
+    stacked = jnp.concatenate(parts_of(x, count), axis=0)
     y = jnp.dot(stacked, choice, preferred_element_type=jnp.float32)
-    return y[:rows] + y[rows : 2 * rows] + y[2 * rows :]
-
-
-def choice_times(choice, x):
+    return functools.reduce(lambda a, b: a + b, [y[i * rows : (i + 1) * rows] for i in range(count)])
+
+
+def times_parts(x, both):
+    rows = x.shape[0]
+    width = both.shape[1] // 2
+    y = jnp.dot(jnp.concatenate(parts_of(x, 2), axis=0), both, preferred_element_type=jnp.float32)
+    return y[:rows, :width] + (y[rows:, :width] + y[:rows, width:])
+
+
+def both_parts(w):
+    return jnp.concatenate(parts_of(w, 2), axis=1)
+
+
+def choice_times(choice, x, count=2):
     width = x.shape[1]
-    stacked = jnp.concatenate(parts_of(x), axis=1)
+    stacked = jnp.concatenate(parts_of(x, count), axis=1)
     y = jnp.dot(choice, stacked, preferred_element_type=jnp.float32)
-    return y[:, :width] + y[:, width : 2 * width] + y[:, 2 * width :]
+    return functools.reduce(lambda a, b: a + b, [y[:, i * width : (i + 1) * width] for i in range(count)])
 
 
 def one_hot(condition):
@@ -134,22 +145,74 @@
     return pltpu.roll(field, by % size, dim)
 
 
-def pair_mean(field, cells, step, where_x, where_y, where_z):
-    for position, dim, reach in ((where_z, 1, step), (where_y, 1, step * cells), (where_x, 0, step)):
-        even = (position & step) == 0
-        field = 0.5 * (field + jnp.where(even, shift(field, -reach, dim), shift(field, reach, dim)))
-    return field
-
-
 def positions(rows, cells):
-    face = cells * cells
-    shape = (rows, face)
-    lane = iota(shape, 1)
-    row = iota(shape, 0)
-    where_x = row & (cells - 1)
-    where_z = lane & (cells - 1)
-    where_y = lax.shift_right_logical(lane, jnp.full(shape, cells.bit_length() - 1, jnp.int32))
-    return where_x, where_y, where_z
+    shape = (rows, cells * cells)
+    return (iota(shape, 0) & (cells - 1), *split_index(iota(shape, 1), cells, 2))
+
+
+def bits(cells):
+    return cells.bit_length() - 1
+
+
+def split_index(flat, cells, dims):
+    return [(flat >> (bits(cells) * (dims - 1 - i))) & (cells - 1) for i in range(dims)]
+
+
+def gather_matrix(cells, columns_first):
+    face, half = cells * cells, cells // 2
+    shape = (half**3, face) if columns_first else (face, half**3)
+    y, z = split_index(iota(shape, 1 if columns_first else 0), cells, 2)
+    _, half_y, half_z = split_index(iota(shape, 0 if columns_first else 1), half, 3)
+    return one_hot(((y >> 1) == half_y) & ((z >> 1) == half_z))
+
+
+def coarsen_matrix(cells, columns_first):
+    half = cells // 2
+    shape = (half**3, cells**3) if columns_first else (cells**3, half**3)
+    fine = split_index(iota(shape, 1 if columns_first else 0), cells, 3)
+    coarse = split_index(iota(shape, 0 if columns_first else 1), half, 3)
+    same = [(f >> 1) == c for f, c in zip(fine, coarse)]
+    return one_hot(same[0] & same[1] & same[2])
+
+
+def own_half(cells):
+    half = cells // 2
+    shape = (cells, half**3)
+    return split_index(iota(shape, 1), half, 3)[0] == (iota(shape, 0) >> 1)
+
+
+def plane_restrict(field, gather, cells, count):
+    spread_out = times_choice(field, gather)
+    here = own_half(cells)
+    rows = [
+        jnp.sum(jnp.where(here, spread_out[c * cells : (c + 1) * cells], 0.0), axis=0, keepdims=True)
+        for c in range(count)
+    ]
+    return 0.125 * (rows[0] if count == 1 else jnp.concatenate(rows, axis=0))
+
+
+def plane_prolong(coarse, scatter, cells, count):
+    here = own_half(cells)
+    wide = [
+        jnp.where(here, jnp.broadcast_to(coarse[c : c + 1], (cells, coarse.shape[1])), 0.0) for c in range(count)
+    ]
+    return times_choice(jnp.concatenate(wide, axis=0), scatter)
+
+
+def sweeps_matrix(scale, cells, weight):
+    size = cells**3
+    shape = (size, size)
+    here = split_index(iota(shape, 0), cells, 3)
+    there = split_index(iota(shape, 1), cells, 3)
+    distance = functools.reduce(lambda a, b: a + b, [jnp.abs(a - b) for a, b in zip(here, there)])
+    power = jnp.where(distance == 0, 1.0 - damping, 0.0) + jnp.where(distance == 1, weight * scale, 0.0)
+    total = jnp.where(distance == 0, 1.0, 0.0) + power
+    done = 2
+    while done < COARSE_SWEEPS:
+        power = times_parts(power, both_parts(power))
+        total = total + times_parts(total, both_parts(power))
+        done *= 2
+    return total
 
 
 def load(pairs, semaphores):
@@ -176,6 +239,12 @@
     lower_out,
     upper_out,
     pick_out,
+    half_out,
+    quarter_out,
+    gather_out,
+    scatter_out,
+    coarsen_out,
+    sweeps_out,
     reaction,
     primal_index,
     region_inverse,
@@ -199,17 +268,27 @@
     upper = place_matrix(cells, True)
     upper_out[...] = upper
     pick_out[...] = pick_matrix(cells, False)
+    half = cells // 2
+    gather = gather_matrix(cells, False)
+    gather_out[...] = gather
+    scatter_out[...] = gather_matrix(cells, True)
+    coarsen = coarsen_matrix(half, False)
+    coarsen_out[...] = coarsen
     for copy in copies:
         copy.wait()
-    where_x, where_y, where_z = positions(cells, cells)
     react = reaction[0]
-    for level in range(LEVELS):
-        weight = 0.25**level
-        diagonal = react + 6.0 * weight
-        inverse_out[level] = damping / diagonal
-        inverse_out[LEVELS + level] = diagonal
-        if level < LEVELS - 1:
-            react = pair_mean(react, cells, 2**level, where_x, where_y, where_z)
+    diagonal = react + 6.0
+    inverse_out[0] = damping / diagonal
+    inverse_out[1] = diagonal
+    react = plane_restrict(react, gather, cells, 1)
+    diagonal = react + 6.0 * 0.25
+    half_out[0:1, :] = damping / diagonal
+    half_out[1:2, :] = diagonal
+    react = 0.125 * times_choice(jnp.broadcast_to(react, (8, half**3)), coarsen)[:1]
+    scale = damping / (react + 6.0 * 0.0625)
+    quarter_out[...] = 0.125 * scale
+    sweeps = sweeps_matrix(scale, half // 2, 0.0625)
+    sweeps_out[...] = both_parts(times_choice(sweeps, coarsen_matrix(half, True)))
     faces = faces_of(direction)
     row_x = iota((cells, face), 0)
     source = times_choice(jnp.concatenate([spread(faces[1], cells), spread(faces[2], cells)], axis=1), upper)
@@ -258,6 +337,12 @@
     inverses,
     front,
     lower,
+    halves,
+    quarter,
+    gather,
+    scatter,
+    coarsen,
+    sweeps,
     base_out,
     send_out,
 ):
@@ -274,46 +359,56 @@
         axis=0,
     )
     where_x, where_y, where_z = positions(rows, cells)
+    last = cells - 1
 
     def tall(x):
         return jnp.concatenate([x] * 3, axis=0)
 
-    inverse = [tall(inverses[level]) for level in range(LEVELS)]
-    diagonal = [tall(inverses[LEVELS + level]) for level in range(LEVELS)]
-
-    def beside(field, level):
-        step = 2**level
-        last = cells - step
-        total = jnp.where(where_x < last, shift(field, -step, 0), 0.0)
-        total = total + jnp.where(where_x >= step, shift(field, step, 0), 0.0)
-        total = total + jnp.where(where_y < last, shift(field, -step * cells, 1), 0.0)
-        total = total + jnp.where(where_y >= step, shift(field, step * cells, 1), 0.0)
-        total = total + jnp.where(where_z < last, shift(field, -step, 1), 0.0)
-        return total + jnp.where(where_z >= step, shift(field, step, 1), 0.0)
-
-    def relax(field, right, level, sweeps):
-        weight = 0.25**level
-        for _ in range(sweeps):
-            if field is None:
-                field = inverse[level] * right
-            else:
-                field = (1.0 - damping) * field + inverse[level] * (right + weight * beside(field, level))
-        return field
-
-    def vcycle(field, right, level):
-        if level == LEVELS - 1:
-            return relax(field, right, level, COARSE_SWEEPS)
-        field = relax(field, right, level, SWEEPS)
-        remain = right - diagonal[level] * field + 0.25**level * beside(field, level)
-        remain = pair_mean(remain, cells, 2**level, where_x, where_y, where_z)
-        field = field + vcycle(None, remain, level + 1)
-        return relax(field, right, level, SWEEPS)
-
-    field = None
-    for _ in range(VCYCLES):
-        field = vcycle(field, source, 0)
+    inverse = tall(inverses[0])
+    diagonal = tall(inverses[1])
+
+    def beside(field):
+        total = jnp.where(where_x < last, shift(field, -1, 0), 0.0)
+        total = total + jnp.where(where_x > 0, shift(field, 1, 0), 0.0)
+        total = total + jnp.where(where_y < last, shift(field, -cells, 1), 0.0)
+        total = total + jnp.where(where_y > 0, shift(field, cells, 1), 0.0)
+        total = total + jnp.where(where_z < last, shift(field, -1, 1), 0.0)
+        return total + jnp.where(where_z > 0, shift(field, 1, 1), 0.0)
+
+    half = cells // 2
+    lane = iota((8, half**3), 1)
+    half_at = split_index(lane, half, 3)
+    half_inverse = halves[0:1, :]
+    half_diagonal = halves[1:2, :]
+
+    def half_beside(field):
+        total = jnp.zeros_like(field)
+        for position, reach in zip(half_at, (half * half, half, 1)):
+            total = total + jnp.where(position < half - 1, shift(field, -reach, 1), 0.0)
+            total = total + jnp.where(position > 0, shift(field, reach, 1), 0.0)
+        return total
+
+    def half_cycle(right):
+        field = half_inverse * right
+        remain = right - half_diagonal * field + 0.25 * half_beside(field)
+        remain = times_choice(remain, coarsen[...])
+        field = field + times_parts(remain * quarter[...], sweeps[...])
+        return (1.0 - damping) * field + half_inverse * (right + 0.25 * half_beside(field))
+
+    def relax(field, right):
+        return (1.0 - damping) * field + inverse * (right + beside(field))
+
+    field = inverse * source
+    for cycle in range(VCYCLES):
+        if cycle:
+            field = relax(field, source)
+        remain = source - diagonal * field + beside(field)
+        right = plane_restrict(remain, gather[...], cells, 3)
+        right = jnp.concatenate([right, jnp.zeros((5, half**3), jnp.float32)], axis=0)
+        field = field + plane_prolong(half_cycle(right), scatter[...], cells, 3)
+        field = relax(field, source)
     base_out[...] = field
-    energy = jnp.sum(source * field)
+    energy = jnp.sum(jnp.sum(source * field, axis=0, keepdims=True), axis=1, keepdims=True)
     message = front[...]
     at = (iota(message.shape, 0) == sizes[1] // 2) & (iota(message.shape, 1) == count)
     message = message + jnp.where(at, energy, 0.0)
@@ -328,42 +423,20 @@
 def between_kernel(
     cells,
     base,
-    primal_index_in,
-    region_inverse_in,
-    coarse_map_in,
-    global_inverse_in,
-    multipliers_in,
-    viscosity_in,
-    multipliers,
-    viscosity,
+    primal_index,
+    region_inverse,
+    coarse_map,
+    global_inverse,
     ends_out,
     region_out,
     through_out,
     global_out,
     spots_out,
     choose_out,
-    primal_index,
-    region_inverse,
-    coarse_map,
-    global_inverse,
-    semaphores,
 ):
-    copies = load(
-        [
-            (primal_index_in, primal_index),
-            (region_inverse_in, region_inverse),
-            (coarse_map_in, coarse_map),
-            (global_inverse_in, global_inverse),
-            (multipliers_in, multipliers),
-            (viscosity_in, viscosity),
-        ],
-        semaphores,
-    )
     face = cells * cells
     on_x, on_y, on_z = face_ends(base[...], pick_matrix(cells, True), cells, True)
     ends_out[...] = jnp.concatenate([on_x, on_y, on_z, jnp.zeros((7, face), jnp.float32)], axis=0)
-    for copy in copies:
-        copy.wait()
     count = primal_index.shape[1]
     group, _, place, _ = decode(primal_index[...], cells)
     choose_out[...] = jnp.concatenate(
@@ -375,10 +448,9 @@
     blank = jnp.zeros((count, LANES - count), jnp.float32)
     for q in range(region_out.shape[0]):
         region_out[q] = jnp.concatenate([region_inverse[0, :, q * count : (q + 1) * count], blank], axis=1)
-    through_out[...] = jnp.dot(
-        coarse_map[0], global_inverse[...], precision=lax.Precision.HIGHEST, preferred_element_type=jnp.float32
-    )
-    global_out[...] = jnp.concatenate(parts_of(global_inverse[...], 2), axis=1)
+    both = both_parts(global_inverse[...])
+    global_out[...] = both
+    through_out[...] = times_parts(coarse_map[0], both)
 
 
 def after_kernel(
@@ -506,17 +578,26 @@
     below_y = shifted_2(direction, "sub", DOM_Z).reshape(lines)
     below_z = shifted_2(direction, "sub", 1).reshape(lines)
     multipliers, direction, residual = [x.reshape(lines) for x in (multipliers, direction, residual)]
-    direction, residual, source, front, inverses, lower, upper, pick = call(
+    half_cells = (cells // 2) ** 3
+    (
+        direction, residual, source, front, inverses, lower, upper, pick, halves, quarter, gather, scatter, coarsen, sweeps
+    ) = call(
         functools.partial(before_kernel, cells, sizes),
         [
             like(lines),
             like(lines),
             like((rows, face)),
             like((height, LANES)),
-            like((2 * LEVELS, cells, face)),
+            like((2, cells, face)),
             like((2 * face, face), bf16),
             like((2 * face, face), bf16),
             like((face, 2 * face), bf16),
+            like((2, half_cells)),
+            like((1, half_cells // 8)),
+            like((face, half_cells), bf16),
+            like((half_cells, face), bf16),
+            like((half_cells, half_cells // 8), bf16),
+            like((half_cells // 8, 2 * half_cells), bf16),
         ],
         [],
         [direction, residual, reaction, primal_index, region_inverse, coarse_map],
@@ -525,7 +606,7 @@
     base, sent = call(
         functools.partial(solve_kernel, cells, sizes, count),
         [like((rows, face)), like((n_region * n_sub, height, LANES))],
-        [source, below_x, below_y, below_z, inverses, front, lower],
+        [source, below_x, below_y, below_z, inverses, front, lower, halves, quarter, gather, scatter, coarsen, sweeps],
     )
     received = lax.all_to_all(sent, ("region", "sub"), 0, 0, tiled=True)
     lower_x, lower_y, lower_z = call(
@@ -534,11 +615,9 @@
     after_x = shifted_2(lower_x, "region", -1)
     after_y = shifted_2(lower_y, "sub", -DOM_Z)
     after_z = shifted_2(lower_z, "sub", -1)
-    multipliers, viscosity, ends, region_blocks, through, global_parts, spots, choose = call(
+    ends, region_blocks, through, global_parts, spots, choose = call(
         functools.partial(between_kernel, cells),
         [
-            like(lines),
-            like(viscosity.shape),
             like((16, face)),
             like((n_sub, count, LANES)),
             like((count, columns)),
@@ -546,9 +625,7 @@
             like((count, 2 * face)),
             like((rows + 16, count), bf16),
         ],
-        [base],
-        [primal_index, region_inverse, coarse_map, global_inverse, multipliers, viscosity],
-        [primal_index, region_inverse, coarse_map, global_inverse],
+        [base, primal_index, region_inverse, coarse_map, global_inverse],
     )
     new_multipliers, new_residual, velocity, pressure = call(
         functools.partial(after_kernel, cells, sizes, count),

time: 27.4 us -> 25.6 us (0.934)
  Pallas kernels: 9.14 us -> 7.47 us
  starting transfers between devices: 16.8 us -> 16.2 us
  waiting for transfers between devices: 0.56 us -> 0.89 us
    pallas_call x5, Pallas kernels: 9.14 us -> 7.47 us  [call(): pl.pallas_call(kernel, out_shape=out_shape, in_specs=[vmem] * len(operand...]
    all_to_all x1, starting transfers between devices: 4.78 us -> 4.26 us  [body(): received = lax.all_to_all(sent, ('region', 'sub'), 0, 0, tiled=True)]
    ppermute x6, waiting for transfers between devices: 0.56 us -> 0.89 us  [shifted_2(): return lax.ppermute(x, axis, [(i, (i + by) % count) for i in range(count)])]
  transfers between devices with their start and end apart: 7 -> 7, of which waited for: 1 -> 1; matrix products, arithmetic and copies ran while one was open for 0% -> 0% of each run, Pallas kernels for 14% -> 13%
where the time goes in v3:
time: 25.6 us; the launch traced here: 25.4 us
  starting transfers between devices  16.2 us (63%)
  Pallas kernels  7.47 us (29%)
  waiting for transfers between devices  0.89 us (3%)
  between operations  0.74 us (3%)
    ppermute x6, starting transfers between devices, shifted_2(): return lax.ppermute(x, axis, [(i, (i + by) % count) for i in range(count)])  12 us
    pallas_call x5, Pallas kernels, call(): pl.pallas_call(kernel, out_shape=out_shape, in_specs=[vmem] * len(operand...  7.47 us
    all_to_all x1, starting transfers between devices, body(): received = lax.all_to_all(sent, ('region', 'sub'), 0, 0, tiled=True)  4.26 us
    ppermute x6, waiting for transfers between devices, shifted_2(): return lax.ppermute(x, axis, [(i, (i + by) % count) for i in range(count)])  0.89 us
  transfers between devices with their start and end apart: 7, of which 1 were waited for; matrix products, arithmetic and copies ran while one was open for 0% of the time, Pallas kernels for 13%

profile of v3, /device:TPU:0, one launch (start us, length us, event | category | flops | bytes accessed | tf_op | source)
XLA Modules:
  0.0 25.4 jit_solution(6249702168921983658)
XLA Ops:
  0.6 0.5 %collective-permute-start = (f32[1,3,3,256]{3,0,2,1:T(1,128)}, f32[1,3,3,256]{3,0,2,1:T(1,128)S(1)}, u32[]{:S(2)}, u32[]{:S(2)}) collective-permute-start(f32[1,3,3,256]{3,0,2,1:T(1,128)} %param.10), channel_id=1, source_target_pairs={{0,8},{8,16},{16,24},{24,0},{1,9},{9,17},{17,25},{25,1},{2,10},{10... | collective-permute-start | bytes 27656 | tf_op jit(solution)/shard_map/ppermute | solution.py:22
  1.1 2.6 %collective-permute-start.2 = (f32[1,3,3,256]{3,0,2,1:T(1,128)}, f32[1,3,3,256]{3,0,2,1:T(1,128)S(1)}, u32[]{:S(2)}, u32[]{:S(2)}) collective-permute-start(f32[1,3,3,256]{3,0,2,1:T(1,128)} %param.10), channel_id=1, source_target_pairs={{0,1},{1,2},{2,3},{3,4},{4,5},{5,6},{6,7},{7,0},{8,9},{9,10},{10,1... | collective-permute-start | bytes 27656 | tf_op jit(solution)/shard_map/ppermute | solution.py:22
  3.7 2.6 %collective-permute-start.1 = (f32[1,3,3,256]{3,0,2,1:T(1,128)}, f32[1,3,3,256]{3,0,2,1:T(1,128)S(1)}, u32[]{:S(2)}, u32[]{:S(2)}) collective-permute-start(f32[1,3,3,256]{3,0,2,1:T(1,128)} %param.10), channel_id=1, source_target_pairs={{0,4},{1,5},{2,6},{3,7},{4,0},{5,1},{6,2},{7,3},{8,12},{9,13},{10,... | collective-permute-start | bytes 27656 | tf_op jit(solution)/shard_map/ppermute | solution.py:22
  6.3 2.8 %shard_map.120 = (f32[9,1,256]{2,1,0:T(1,128)S(1)}, f32[9,1,256]{2,1,0:T(1,128)S(1)}, f32[48,256]{1,0:T(8,128)S(1)}, f32[8,128]{1,0:T(8,128)S(1)}, f32[2,16,256]...) custom-call(f32[9,1,256]{2,1,0:T(1,128)} %bitcast.13, ...), custom_call_target="tpu_custom_call" | custom-call | tf_op jit(solution)/shard_map/pallas_call | solution.py:567
  9.1 0.0 collective-permute-done
  9.1 0.0 collective-permute-done.2
  9.1 0.0 collective-permute-done.1
  9.1 0.0 copy-start.1
  9.1 3.0 %shard_map.121 = (f32[48,256]{1,0:T(8,128)S(1)}, f32[32,8,128]{2,1,0:T(8,128)}) custom-call(f32[48,256]{1,0:T(8,128)S(1)} %get-tuple-element.33.source_own, f32[9,1,256]{2,1,0:T(1,128)S(1)} %bitcast.9, f32[9,1,256]{2,1,0:T(1,128)S(1)} %bitcast.11, f32[9,1,256]{2,1,0:T(1,128)S(1)} %bitcast.10, f32[2,16,256]{2,1,0:T(8,128)S(1)} %get-tuple-element.34.inverses, ...), custom_call_target="tpu_custom_call" | custom-call | tf_op jit(solution)/shard_map/pallas_call | solution.py:567
  12.1 0.0 copy-start
  12.1 4.3 %all-to-all-start = ((f32[32,8,128]{2,1,0:T(8,128)}), f32[32,8,128]{2,1,0:T(8,128)S(1)}, u32[]{:S(2)}, u32[]{:S(2)}) async-start(f32[32,8,128]{2,1,0:T(8,128)} %get-tuple-element.43), calls=%async_computation | async-start | bytes 262144 | tf_op jit(solution)/shard_map/all_to_all | solution.py:611
  16.4 0.0 copy-start.2
  16.4 0.2 shard_map.123
  16.6 1.6 %collective-permute-start.3 = (f32[3,256]{1,0:T(4,128)S(1)}, f32[3,256]{1,0:T(4,128)S(1)}, u32[]{:S(2)}, u32[]{:S(2)}) collective-permute-start(f32[3,256]{1,0:T(4,128)S(1)} %get-tuple-element.47), channel_id=1, source_target_pairs={{0,24},{8,0},{16,8},{24,16},{1,25},{9,1},{17,9},{25,17},{2,26},{10... | collective-permute-start | bytes 9224 | tf_op jit(solution)/shard_map/ppermute | solution.py:22
  18.2 0.0 copy-start.5
  18.2 2.4 %collective-permute-start.4 = (f32[3,256]{1,0:T(4,128)S(1)}, f32[3,256]{1,0:T(4,128)S(1)}, u32[]{:S(2)}, u32[]{:S(2)}) collective-permute-start(f32[3,256]{1,0:T(4,128)S(1)} %get-tuple-element.48), channel_id=1, source_target_pairs={{0,4},{1,5},{2,6},{3,7},{4,0},{5,1},{6,2},{7,3},{8,12},{9,13},{10,... | collective-permute-start | bytes 9224 | tf_op jit(solution)/shard_map/ppermute | solution.py:22
  20.5 2.4 %collective-permute-start.5 = (f32[3,256]{1,0:T(4,128)S(1)}, f32[3,256]{1,0:T(4,128)S(1)}, u32[]{:S(2)}, u32[]{:S(2)}) collective-permute-start(f32[3,256]{1,0:T(4,128)S(1)} %get-tuple-element.49), channel_id=1, source_target_pairs={{0,7},{1,0},{2,1},{3,2},{4,3},{5,4},{6,5},{7,6},{8,15},{9,8},{10,9... | collective-permute-start | bytes 9224 | tf_op jit(solution)/shard_map/ppermute | solution.py:22
  22.9 0.0 copy-done.1
  22.9 0.0 copy-done
  22.9 0.0 copy-done.2
  22.9 0.0 copy-done.5
  22.9 0.0 copy-start.4
  22.9 0.4 %shard_map.122 = (f32[16,256]{1,0:T(8,128)S(1)}, f32[8,96,128]{2,1,0:T(8,128)S(1)}, f32[96,384]{1,0:T(8,128)S(1)}, bf16[384,768]{1,0:T(8,128)(2,1)S(1)}, f32[96,...) custom-call(f32[48,256]{1,0:T(8,128)S(1)} %get-tuple-element.44.base, s32[1,96]{1,0:T(1,128)S(1)} %copy-done.5, ...), custom_call_target="tpu_custom_call" | custom-call | tf_op jit(solution)/shard_map/pallas_call | solution.py:567
  23.3 0.0 copy-start.3
  23.3 0.0 collective-permute-done.3.after_x
  23.3 0.0 collective-permute-done.4.after_y
  23.4 0.9 %collective-permute-done.5.after_z = f32[3,256]{1,0:T(4,128)S(1)} collective-permute-done((f32[3,256]{1,0:T(4,128)S(1)}, f32[3,256]{1,0:T(4,128)S(1)}, u32[]{:S(2)}, u32[]{:S(2)}) %collective-permute-start.5) | collective-permute-done | bytes 3104 | tf_op jit(solution)/shard_map/ppermute | solution.py:22
  24.2 0.0 all-to-all-done.received
  24.2 0.0 copy-done.4
  24.2 0.0 copy-done.3
  24.2 1.1 %shard_map.124 = (f32[9,1,256]{2,1,0:T(1,128)}, f32[9,1,256]{2,1,0:T(1,128)}, f32[1,3,16,256]{3,2,1,0:T(8,128)}, f32[1,16,256]{2,1,0:T(8,128)}) custom-call(f32[32,8,128]{2,1,0:T(8,128)S(1)} %all-to-all-done.received, f32[48,256]{1,0:T(8,128)S(1)} %get-tuple-element.44.base, f32[16,256]{1,0:T(8,128)S(1)} %get-tuple-element.45.ends, ...), custom_call_target="tpu_custom_call" | custom-call | tf_op jit(solution)/shard_map/pallas_call | solution.py:567
Async XLA Ops:
  0.6 8.4 %collective-permute-start = (f32[1,3,3,256]{3,0,2,1:T(1,128)}, f32[1,3,3,256]{3,0,2,1:T(1,128)S(1)}, u32[]{:S(2)}, u32[]{:S(2)}) collective-permute-start(f32[1,3,3,256]{3,0,2,1:T(1,128)} %param.10), channel_id=1, source_target_pairs={{0,8},{8,16},{16,24},{24,0},{1,9},{9,17},{17,25},{25,1},{2,10},{10... | collective-permute-start | bytes 27656 | tf_op jit(solution)/shard_map/ppermute | solution.py:22
  1.1 8.0 %collective-permute-start.2 = (f32[1,3,3,256]{3,0,2,1:T(1,128)}, f32[1,3,3,256]{3,0,2,1:T(1,128)S(1)}, u32[]{:S(2)}, u32[]{:S(2)}) collective-permute-start(f32[1,3,3,256]{3,0,2,1:T(1,128)} %param.10), channel_id=1, source_target_pairs={{0,1},{1,2},{2,3},{3,4},{4,5},{5,6},{6,7},{7,0},{8,9},{9,10},{10,1... | collective-permute-start | bytes 27656 | tf_op jit(solution)/shard_map/ppermute | solution.py:22
  3.7 5.4 %collective-permute-start.1 = (f32[1,3,3,256]{3,0,2,1:T(1,128)}, f32[1,3,3,256]{3,0,2,1:T(1,128)S(1)}, u32[]{:S(2)}, u32[]{:S(2)}) collective-permute-start(f32[1,3,3,256]{3,0,2,1:T(1,128)} %param.10), channel_id=1, source_target_pairs={{0,4},{1,5},{2,6},{3,7},{4,0},{5,1},{6,2},{7,3},{8,12},{9,13},{10,... | collective-permute-start | bytes 27656 | tf_op jit(solution)/shard_map/ppermute | solution.py:22
  9.1 13.8 %copy-start.1 = (f32[384,384]{1,0:T(8,128)S(1)}, f32[384,384]{1,0:T(8,128)}, u32[]{:S(2)}) copy-start(f32[384,384]{1,0:T(8,128)} %global_inverse.1) | copy-start | bytes 1769476
  12.1 10.8 %copy-start = (f32[1,96,768]{2,1,0:T(8,128)S(1)}, f32[1,96,768]{2,1,0:T(8,128)}, u32[]{:S(2)}) copy-start(f32[1,96,768]{2,1,0:T(8,128)} %region_inverse.1) | copy-start | bytes 884740
  12.1 12.1 %all-to-all-start = ((f32[32,8,128]{2,1,0:T(8,128)}), f32[32,8,128]{2,1,0:T(8,128)S(1)}, u32[]{:S(2)}, u32[]{:S(2)}) async-start(f32[32,8,128]{2,1,0:T(8,128)} %get-tuple-element.43), calls=%async_computation | async-start | bytes 262144 | tf_op jit(solution)/shard_map/all_to_all | solution.py:611
  16.4 6.5 %copy-start.2 = (f32[1,96,384]{2,1,0:T(8,128)S(1)}, f32[1,96,384]{2,1,0:T(8,128)}, u32[]{:S(2)}) copy-start(f32[1,96,384]{2,1,0:T(8,128)} %coarse_map.1) | copy-start | bytes 442372
  16.6 6.7 %collective-permute-start.3 = (f32[3,256]{1,0:T(4,128)S(1)}, f32[3,256]{1,0:T(4,128)S(1)}, u32[]{:S(2)}, u32[]{:S(2)}) collective-permute-start(f32[3,256]{1,0:T(4,128)S(1)} %get-tuple-element.47), channel_id=1, source_target_pairs={{0,24},{8,0},{16,8},{24,16},{1,25},{9,1},{17,9},{25,17},{2,26},{10... | collective-permute-start | bytes 9224 | tf_op jit(solution)/shard_map/ppermute | solution.py:22
  18.2 4.7 %copy-start.5 = (s32[1,96]{1,0:T(1,128)S(1)}, s32[1,96]{1,0:T(1,128)}, u32[]{:S(2)}) copy-start(s32[1,96]{1,0:T(1,128)} %primal_index.1) | copy-start | bytes 1156
  18.2 5.2 %collective-permute-start.4 = (f32[3,256]{1,0:T(4,128)S(1)}, f32[3,256]{1,0:T(4,128)S(1)}, u32[]{:S(2)}, u32[]{:S(2)}) collective-permute-start(f32[3,256]{1,0:T(4,128)S(1)} %get-tuple-element.48), channel_id=1, source_target_pairs={{0,4},{1,5},{2,6},{3,7},{4,0},{5,1},{6,2},{7,3},{8,12},{9,13},{10,... | collective-permute-start | bytes 9224 | tf_op jit(solution)/shard_map/ppermute | solution.py:22
  20.5 3.7 %collective-permute-start.5 = (f32[3,256]{1,0:T(4,128)S(1)}, f32[3,256]{1,0:T(4,128)S(1)}, u32[]{:S(2)}, u32[]{:S(2)}) collective-permute-start(f32[3,256]{1,0:T(4,128)S(1)} %get-tuple-element.49), channel_id=1, source_target_pairs={{0,7},{1,0},{2,1},{3,2},{4,3},{5,4},{6,5},{7,6},{8,15},{9,8},{10,9... | collective-permute-start | bytes 9224 | tf_op jit(solution)/shard_map/ppermute | solution.py:22
  22.9 1.3 %copy-start.4 = (f32[1,3,3,256]{3,0,2,1:T(1,128)S(1)}, f32[1,3,3,256]{3,0,2,1:T(1,128)}, u32[]{:S(2)}) copy-start(f32[1,3,3,256]{3,0,2,1:T(1,128)} %param.9) | copy-start | bytes 27652
  23.3 0.9 %copy-start.3 = (f32[1,16,256]{2,1,0:T(8,128)S(1)}, f32[1,16,256]{2,1,0:T(8,128)}, u32[]{:S(2)}) copy-start(f32[1,16,256]{2,1,0:T(8,128)} %viscosity.1) | copy-start | bytes 49156

commit v4 on v3

--- a/solution.py
+++ b/solution.py
@@ -104,25 +104,22 @@
 
 
 def place_matrix(cells, upper):
-    face = cells * cells
-    row = iota((face, face), 0)
-    column = iota((face, face), 1)
-    second = row & (cells - 1)
+    row = iota((cells, cells * cells), 0)
+    column = iota((cells, cells * cells), 1)
     end = cells - 1 if upper else 0
-    return jnp.concatenate(
-        [one_hot(column == second + end * cells), one_hot(column == second * cells + end)], axis=0
-    )
+    on_y = one_hot(column == row + end * cells)
+    on_z = one_hot(column == row * cells + end)
+    return jnp.concatenate([on_y] * cells + [on_z] * cells, axis=0)
 
 
 def pick_matrix(cells, upper):
     face = cells * cells
-    row = iota((face, face), 0)
-    column = iota((face, face), 1)
-    second = column & (cells - 1)
+    row = iota((face, LANES), 0)
+    second = iota((face, LANES), 1) & (cells - 1)
     end = cells - 1 if upper else 0
-    return jnp.concatenate(
-        [one_hot(row == second + end * cells), one_hot(row == second * cells + end)], axis=1
-    )
+    on_y = one_hot(row == second + end * cells)
+    on_z = one_hot(row == second * cells + end)
+    return jnp.concatenate([on_y] * (face // LANES) + [on_z] * (face // LANES), axis=1)
 
 
 def face_ends(field, pick, cells, upper):
@@ -158,60 +155,84 @@
     return [(flat >> (bits(cells) * (dims - 1 - i))) & (cells - 1) for i in range(dims)]
 
 
-def gather_matrix(cells, columns_first):
-    face, half = cells * cells, cells // 2
-    shape = (half**3, face) if columns_first else (face, half**3)
-    y, z = split_index(iota(shape, 1 if columns_first else 0), cells, 2)
-    _, half_y, half_z = split_index(iota(shape, 0 if columns_first else 1), half, 3)
-    return one_hot(((y >> 1) == half_y) & ((z >> 1) == half_z))
-
-
-def coarsen_matrix(cells, columns_first):
+def gather_matrix(cells, steps=1):
+    size = cells >> steps
+    width = min(size**3, LANES)
+    shape = (cells * cells, width)
+    y, z = split_index(iota(shape, 0), cells, 2)
+    _, far_y, far_z = split_index(iota(shape, 1), size, 3)
+    return jnp.concatenate([one_hot(((y >> steps) == far_y) & ((z >> steps) == far_z))] * (size**3 // width), axis=1)
+
+
+def scatter_matrix(cells):
     half = cells // 2
-    shape = (half**3, cells**3) if columns_first else (cells**3, half**3)
-    fine = split_index(iota(shape, 1 if columns_first else 0), cells, 3)
-    coarse = split_index(iota(shape, 0 if columns_first else 1), half, 3)
-    same = [(f >> 1) == c for f, c in zip(fine, coarse)]
-    return one_hot(same[0] & same[1] & same[2])
-
-
-def own_half(cells):
+    shape = (half * half, cells * cells)
+    y, z = split_index(iota(shape, 1), cells, 2)
+    half_y, half_z = split_index(iota(shape, 0), half, 2)
+    return jnp.concatenate([one_hot(((y >> 1) == half_y) & ((z >> 1) == half_z))] * half, axis=0)
+
+
+def block_matrices(cells, blocks_first):
     half = cells // 2
-    shape = (cells, half**3)
-    return split_index(iota(shape, 1), half, 3)[0] == (iota(shape, 0) >> 1)
-
-
-def plane_restrict(field, gather, cells, count):
+    shape = (half**3, cells**3) if blocks_first else (cells**3, half**3)
+    fine = split_index(iota(shape, 1 if blocks_first else 0), cells, 3)
+    block = split_index(iota(shape, 0 if blocks_first else 1), half, 3)
+    inside = [(f >> 1) == b for f, b in zip(fine, block)]
+    nearby = [(f >> 1) + 2 * (f & 1) - 1 == b for f, b in zip(fine, block)]
+    same = inside[0] & inside[1] & inside[2]
+    near = (
+        (nearby[0] & inside[1] & inside[2])
+        | (inside[0] & nearby[1] & inside[2])
+        | (inside[0] & inside[1] & nearby[2])
+    )
+    return one_hot(same), jnp.where(same, 3.0, jnp.where(near, 1.0, 0.0)).astype(jnp.bfloat16)
+
+
+def own_part(cells, steps=1):
+    size = cells >> steps
+    shape = (cells, size**3)
+    return split_index(iota(shape, 1), size, 3)[0] == (iota(shape, 0) >> steps)
+
+
+def plane_restrict(field, gather, cells, count, steps=1):
     spread_out = times_choice(field, gather)
-    here = own_half(cells)
+    here = own_part(cells, steps)
     rows = [
         jnp.sum(jnp.where(here, spread_out[c * cells : (c + 1) * cells], 0.0), axis=0, keepdims=True)
         for c in range(count)
     ]
-    return 0.125 * (rows[0] if count == 1 else jnp.concatenate(rows, axis=0))
+    return 0.125**steps * (rows[0] if count == 1 else jnp.concatenate(rows, axis=0))
 
 
 def plane_prolong(coarse, scatter, cells, count):
-    here = own_half(cells)
+    here = own_part(cells)
     wide = [
         jnp.where(here, jnp.broadcast_to(coarse[c : c + 1], (cells, coarse.shape[1])), 0.0) for c in range(count)
     ]
     return times_choice(jnp.concatenate(wide, axis=0), scatter)
 
 
-def sweeps_matrix(scale, cells, weight):
+def sweep_power(scale, cells, weight):
     size = cells**3
     shape = (size, size)
     here = split_index(iota(shape, 0), cells, 3)
     there = split_index(iota(shape, 1), cells, 3)
     distance = functools.reduce(lambda a, b: a + b, [jnp.abs(a - b) for a, b in zip(here, there)])
-    power = jnp.where(distance == 0, 1.0 - damping, 0.0) + jnp.where(distance == 1, weight * scale, 0.0)
-    total = jnp.where(distance == 0, 1.0, 0.0) + power
+    one = jnp.where(distance == 0, 1.0, 0.0)
+    return (1.0 - damping) * one + jnp.where(distance == 1, weight * scale, 0.0), one
+
+
+def square(power):
+    return times_parts(power, both_parts(power))
+
+
+def powers_sum(total, power):
     done = 2
     while done < COARSE_SWEEPS:
-        power = times_parts(power, both_parts(power))
         total = total + times_parts(total, both_parts(power))
         done *= 2
+        if done < COARSE_SWEEPS:
+            power = square(power)
     return total
 
 
@@ -269,27 +290,41 @@
     upper_out[...] = upper
     pick_out[...] = pick_matrix(cells, False)
     half = cells // 2
-    gather = gather_matrix(cells, False)
+    gather = gather_matrix(cells)
     gather_out[...] = gather
-    scatter_out[...] = gather_matrix(cells, True)
-    coarsen = coarsen_matrix(half, False)
-    coarsen_out[...] = coarsen
-    for copy in copies:
+    quarter_gather = gather_matrix(cells, 2)
+    scatter_out[...] = scatter_matrix(cells)
+    coarsen, coarsen_near = block_matrices(half, False)
+    coarsen_out[...] = jnp.concatenate([coarsen, coarsen_near], axis=0)
+    refine = jnp.concatenate(block_matrices(half, True), axis=1)
+    for copy in copies[:3]:
         copy.wait()
     react = reaction[0]
+    scale = damping / (plane_restrict(react, quarter_gather, cells, 1, 2) + 6.0 * 0.0625)
+    quarter_out[...] = 0.125 * scale
+    power, one = sweep_power(scale, half // 2, 0.0625)
+    second_power = square(power)
     diagonal = react + 6.0
     inverse_out[0] = damping / diagonal
     inverse_out[1] = diagonal
-    react = plane_restrict(react, gather, cells, 1)
-    diagonal = react + 6.0 * 0.25
-    half_out[0:1, :] = damping / diagonal
-    half_out[1:2, :] = diagonal
-    react = 0.125 * times_choice(jnp.broadcast_to(react, (8, half**3)), coarsen)[:1]
-    scale = damping / (react + 6.0 * 0.0625)
-    quarter_out[...] = 0.125 * scale
-    sweeps = sweeps_matrix(scale, half // 2, 0.0625)
-    sweeps_out[...] = both_parts(times_choice(sweeps, coarsen_matrix(half, True)))
+    half_scale = damping / (plane_restrict(react, gather, cells, 1) + 6.0 * 0.25)
+    half_out[...] = half_scale
     faces = faces_of(direction)
+    count = primal_index.shape[1]
+    group, spot, _, _ = decode(column_of(primal_index[...]), cells)
+    nine = jnp.concatenate(faces + [jnp.zeros((7, face), jnp.float32)], axis=0)
+    gathered = choice_times(one_hot(iota((count, 16), 1) == group), nine)
+    primal = jnp.sum(jnp.where(iota((count, face), 1) == spot, gathered, 0.0), axis=1, keepdims=True)
+    lane = iota((1, LANES), 1)
+    line = jnp.sum(
+        jnp.where(iota((count, LANES), 0) == iota((count, LANES), 1), primal, 0.0), axis=0, keepdims=True
+    )
+    for copy in copies[3:]:
+        copy.wait()
+    refined = times_choice(powers_sum(one + power, second_power), refine)
+    sweeps_out[...] = both_parts(
+        (1.0 - damping) * refined[:, : half**3] + 0.25 * half_scale * refined[:, half**3 :]
+    )
     row_x = iota((cells, face), 0)
     source = times_choice(jnp.concatenate([spread(faces[1], cells), spread(faces[2], cells)], axis=1), upper)
     own_x = jnp.concatenate(
@@ -297,33 +332,26 @@
         axis=0,
     )
     source_out[...] = source + own_x
-    count = primal_index.shape[1]
-    group, spot, _, _ = decode(column_of(primal_index[...]), cells)
-    nine = jnp.concatenate(faces + [jnp.zeros((7, face), jnp.float32)], axis=0)
-    gathered = choice_times(one_hot(iota((count, 16), 1) == group), nine)
-    primal = jnp.sum(jnp.where(iota((count, face), 1) == spot, gathered, 0.0), axis=1, keepdims=True)
     share = jnp.sum(primal * coarse_map[0], axis=0, keepdims=True)
     product = jnp.sum(primal * region_inverse[0], axis=0, keepdims=True)
-    lane = iota((1, LANES), 1)
-    line = jnp.sum(
-        jnp.where(iota((count, LANES), 0) == iota((count, LANES), 1), primal, 0.0), axis=0, keepdims=True
-    )
     blank = jnp.zeros((1, LANES - count), jnp.float32)
     blocks = jnp.concatenate(
         [jnp.concatenate([product[:, q * count : (q + 1) * count], blank], axis=1) for q in range(n_sub)], axis=0
     )
     me_sub = lax.axis_index("sub")
-    own = jnp.sum(jnp.where(iota(blocks.shape, 0) == me_sub, blocks * line, 0.0))
+    own = jnp.sum(jnp.where(iota(blocks.shape, 0) == me_sub, blocks, 0.0), axis=0, keepdims=True)
+    own = jnp.sum(own * line, axis=1, keepdims=True)
     blocks = pltpu.roll(blocks, n_sub - 1 - me_sub, 0)
-    half = n_sub // 2
-    twice = jnp.where(iota((half, LANES), 0) == (half - 1 if n_sub % 2 == 0 else half), 1.0, 2.0)
-    squares = jnp.sum(residual[...] * residual[...])
+    opposite = n_sub // 2
+    twice = jnp.where(iota((opposite, LANES), 0) == (opposite - 1 if n_sub % 2 == 0 else opposite), 1.0, 2.0)
+    squares = jnp.concatenate([residual[i] for i in range(9)], axis=0)
+    squares = jnp.sum(jnp.sum(squares * squares, axis=0, keepdims=True), axis=1, keepdims=True)
     line = jnp.where(lane == count, own, jnp.where(lane == count + 1, squares, line))
     front_out[...] = jnp.zeros_like(front_out)
-    front_out[:half, :] = blocks[:half] * twice
-    front_out[half : half + 1, :] = line
+    front_out[:opposite, :] = blocks[:opposite] * twice
+    front_out[opposite : opposite + 1, :] = line
     for i in range(share.shape[1] // LANES):
-        front_out[half + 1 + i : half + 2 + i, :] = share[:, i * LANES : (i + 1) * LANES]
+        front_out[opposite + 1 + i : opposite + 2 + i, :] = share[:, i * LANES : (i + 1) * LANES]
 
 
 def solve_kernel(
@@ -378,8 +406,7 @@
     half = cells // 2
     lane = iota((8, half**3), 1)
     half_at = split_index(lane, half, 3)
-    half_inverse = halves[0:1, :]
-    half_diagonal = halves[1:2, :]
+    half_scale = halves[...]
 
     def half_beside(field):
         total = jnp.zeros_like(field)
@@ -389,11 +416,10 @@
         return total
 
     def half_cycle(right):
-        field = half_inverse * right
-        remain = right - half_diagonal * field + 0.25 * half_beside(field)
-        remain = times_choice(remain, coarsen[...])
-        field = field + times_parts(remain * quarter[...], sweeps[...])
-        return (1.0 - damping) * field + half_inverse * (right + 0.25 * half_beside(field))
+        swept = half_scale * right
+        remain = times_choice(jnp.concatenate([(1.0 - damping) * right, 0.25 * swept], axis=1), coarsen[...])
+        local = (2.0 - damping) * swept + 0.25 * half_scale * half_beside(swept)
+        return local + times_parts(remain * quarter[...], sweeps[...])
 
     def relax(field, right):
         return (1.0 - damping) * field + inverse * (right + beside(field))
@@ -592,11 +618,11 @@
             like((2 * face, face), bf16),
             like((2 * face, face), bf16),
             like((face, 2 * face), bf16),
-            like((2, half_cells)),
+            like((1, half_cells)),
             like((1, half_cells // 8)),
             like((face, half_cells), bf16),
             like((half_cells, face), bf16),
-            like((half_cells, half_cells // 8), bf16),
+            like((2 * half_cells, half_cells // 8), bf16),
             like((half_cells // 8, 2 * half_cells), bf16),
         ],
         [],

time: 25.6 us -> 25.3 us (0.988)
  Pallas kernels: 7.47 us -> 6.5 us
  starting transfers between devices: 16.2 us -> 16.7 us
    pallas_call x5, Pallas kernels: 7.47 us -> 6.5 us  [call(): pl.pallas_call(kernel, out_shape=out_shape, in_specs=[vmem] * len(operand...]
    all_to_all x1, starting transfers between devices: 4.26 us -> 4.77 us  [body(): received = lax.all_to_all(sent, ('region', 'sub'), 0, 0, tiled=True)]
  transfers between devices with their start and end apart: 7 -> 7, of which waited for: 1 -> 2; matrix products, arithmetic and copies ran while one was open for 0% -> 0% of each run, Pallas kernels for 13% -> 11%
where the time goes in v4:
time: 25.3 us; the launch traced here: 25.1 us
  starting transfers between devices  16.7 us (66%)
  Pallas kernels  6.5 us (26%)
  waiting for transfers between devices  1.07 us (4%)
  between operations  0.72 us (3%)
    ppermute x6, starting transfers between devices, shifted_2(): return lax.ppermute(x, axis, [(i, (i + by) % count) for i in range(count)])  12 us
    pallas_call x5, Pallas kernels, call(): pl.pallas_call(kernel, out_shape=out_shape, in_specs=[vmem] * len(operand...  6.5 us
    all_to_all x1, starting transfers between devices, body(): received = lax.all_to_all(sent, ('region', 'sub'), 0, 0, tiled=True)  4.77 us
    ppermute x6, waiting for transfers between devices, shifted_2(): return lax.ppermute(x, axis, [(i, (i + by) % count) for i in range(count)])  1.06 us
  transfers between devices with their start and end apart: 7, of which 2 were waited for; matrix products, arithmetic and copies ran while one was open for 0% of the time, Pallas kernels for 11%

profile of v4, /device:TPU:0, one launch (start us, length us, event | category | flops | bytes accessed | tf_op | source)
XLA Modules:
  0.0 25.1 jit_solution(13282644223356521314)
XLA Ops:
  0.6 0.5 %collective-permute-start = (f32[1,3,3,256]{3,0,2,1:T(1,128)}, f32[1,3,3,256]{3,0,2,1:T(1,128)S(1)}, u32[]{:S(2)}, u32[]{:S(2)}) collective-permute-start(f32[1,3,3,256]{3,0,2,1:T(1,128)} %param.10), channel_id=1, source_target_pairs={{0,8},{8,16},{16,24},{24,0},{1,9},{9,17},{17,25},{25,1},{2,10},{10... | collective-permute-start | bytes 27656 | tf_op jit(solution)/shard_map/ppermute | solution.py:22
  1.1 2.6 %collective-permute-start.2 = (f32[1,3,3,256]{3,0,2,1:T(1,128)}, f32[1,3,3,256]{3,0,2,1:T(1,128)S(1)}, u32[]{:S(2)}, u32[]{:S(2)}) collective-permute-start(f32[1,3,3,256]{3,0,2,1:T(1,128)} %param.10), channel_id=1, source_target_pairs={{0,1},{1,2},{2,3},{3,4},{4,5},{5,6},{6,7},{7,0},{8,9},{9,10},{10,1... | collective-permute-start | bytes 27656 | tf_op jit(solution)/shard_map/ppermute | solution.py:22
  3.7 2.6 %collective-permute-start.1 = (f32[1,3,3,256]{3,0,2,1:T(1,128)}, f32[1,3,3,256]{3,0,2,1:T(1,128)S(1)}, u32[]{:S(2)}, u32[]{:S(2)}) collective-permute-start(f32[1,3,3,256]{3,0,2,1:T(1,128)} %param.10), channel_id=1, source_target_pairs={{0,4},{1,5},{2,6},{3,7},{4,0},{5,1},{6,2},{7,3},{8,12},{9,13},{10,... | collective-permute-start | bytes 27656 | tf_op jit(solution)/shard_map/ppermute | solution.py:22
  6.3 2.1 %shard_map.120 = (f32[9,1,256]{2,1,0:T(1,128)S(1)}, f32[9,1,256]{2,1,0:T(1,128)S(1)}, f32[48,256]{1,0:T(8,128)S(1)}, f32[8,128]{1,0:T(8,128)S(1)}, f32[2,16,256]...) custom-call(f32[9,1,256]{2,1,0:T(1,128)} %bitcast.13, ...), custom_call_target="tpu_custom_call" | custom-call | tf_op jit(solution)/shard_map/pallas_call | solution.py:593
  8.4 0.0 collective-permute-done
  8.4 0.2 collective-permute-done.2
  8.6 0.0 collective-permute-done.1
  8.6 0.0 copy-start.1
  8.6 2.7 %shard_map.121 = (f32[48,256]{1,0:T(8,128)S(1)}, f32[32,8,128]{2,1,0:T(8,128)}) custom-call(f32[48,256]{1,0:T(8,128)S(1)} %get-tuple-element.33.source_own, f32[9,1,256]{2,1,0:T(1,128)S(1)} %bitcast.9, f32[9,1,256]{2,1,0:T(1,128)S(1)} %bitcast.11, f32[9,1,256]{2,1,0:T(1,128)S(1)} %bitcast.10, f32[2,16,256]{2,1,0:T(8,128)S(1)} %get-tuple-element.34.inverses, ...), custom_call_target="tpu_custom_call" | custom-call | tf_op jit(solution)/shard_map/pallas_call | solution.py:593
  11.3 0.0 copy-start
  11.3 4.8 %all-to-all-start = ((f32[32,8,128]{2,1,0:T(8,128)}), f32[32,8,128]{2,1,0:T(8,128)S(1)}, u32[]{:S(2)}, u32[]{:S(2)}) async-start(f32[32,8,128]{2,1,0:T(8,128)} %get-tuple-element.43), calls=%async_computation | async-start | bytes 262144 | tf_op jit(solution)/shard_map/all_to_all | solution.py:637
  16.1 0.0 copy-start.2
  16.1 0.2 shard_map.123
  16.3 1.6 %collective-permute-start.3 = (f32[3,256]{1,0:T(4,128)S(1)}, f32[3,256]{1,0:T(4,128)S(1)}, u32[]{:S(2)}, u32[]{:S(2)}) collective-permute-start(f32[3,256]{1,0:T(4,128)S(1)} %get-tuple-element.47), channel_id=1, source_target_pairs={{0,24},{8,0},{16,8},{24,16},{1,25},{9,1},{17,9},{25,17},{2,26},{10... | collective-permute-start | bytes 9224 | tf_op jit(solution)/shard_map/ppermute | solution.py:22
  17.9 0.0 copy-start.5
  17.9 2.4 %collective-permute-start.4 = (f32[3,256]{1,0:T(4,128)S(1)}, f32[3,256]{1,0:T(4,128)S(1)}, u32[]{:S(2)}, u32[]{:S(2)}) collective-permute-start(f32[3,256]{1,0:T(4,128)S(1)} %get-tuple-element.48), channel_id=1, source_target_pairs={{0,4},{1,5},{2,6},{3,7},{4,0},{5,1},{6,2},{7,3},{8,12},{9,13},{10,... | collective-permute-start | bytes 9224 | tf_op jit(solution)/shard_map/ppermute | solution.py:22
  20.2 2.4 %collective-permute-start.5 = (f32[3,256]{1,0:T(4,128)S(1)}, f32[3,256]{1,0:T(4,128)S(1)}, u32[]{:S(2)}, u32[]{:S(2)}) collective-permute-start(f32[3,256]{1,0:T(4,128)S(1)} %get-tuple-element.49), channel_id=1, source_target_pairs={{0,7},{1,0},{2,1},{3,2},{4,3},{5,4},{6,5},{7,6},{8,15},{9,8},{10,9... | collective-permute-start | bytes 9224 | tf_op jit(solution)/shard_map/ppermute | solution.py:22
  22.6 0.0 copy-done.1
  22.6 0.0 copy-done
  22.6 0.0 copy-done.2
  22.6 0.0 copy-done.5
  22.6 0.0 copy-start.4
  22.6 0.4 %shard_map.122 = (f32[16,256]{1,0:T(8,128)S(1)}, f32[8,96,128]{2,1,0:T(8,128)S(1)}, f32[96,384]{1,0:T(8,128)S(1)}, bf16[384,768]{1,0:T(8,128)(2,1)S(1)}, f32[96,...) custom-call(f32[48,256]{1,0:T(8,128)S(1)} %get-tuple-element.44.base, s32[1,96]{1,0:T(1,128)S(1)} %copy-done.5, ...), custom_call_target="tpu_custom_call" | custom-call | tf_op jit(solution)/shard_map/pallas_call | solution.py:593
  23.0 0.0 copy-start.3
  23.0 0.0 collective-permute-done.3.after_x
  23.0 0.0 collective-permute-done.4.after_y
  23.0 0.9 %collective-permute-done.5.after_z = f32[3,256]{1,0:T(4,128)S(1)} collective-permute-done((f32[3,256]{1,0:T(4,128)S(1)}, f32[3,256]{1,0:T(4,128)S(1)}, u32[]{:S(2)}, u32[]{:S(2)}) %collective-permute-start.5) | collective-permute-done | bytes 3104 | tf_op jit(solution)/shard_map/ppermute | solution.py:22
  23.9 0.0 all-to-all-done.received
  23.9 0.0 copy-done.4
  23.9 0.0 copy-done.3
  23.9 1.1 %shard_map.124 = (f32[9,1,256]{2,1,0:T(1,128)}, f32[9,1,256]{2,1,0:T(1,128)}, f32[1,3,16,256]{3,2,1,0:T(8,128)}, f32[1,16,256]{2,1,0:T(8,128)}) custom-call(f32[32,8,128]{2,1,0:T(8,128)S(1)} %all-to-all-done.received, f32[48,256]{1,0:T(8,128)S(1)} %get-tuple-element.44.base, f32[16,256]{1,0:T(8,128)S(1)} %get-tuple-element.45.ends, ...), custom_call_target="tpu_custom_call" | custom-call | tf_op jit(solution)/shard_map/pallas_call | solution.py:593
Async XLA Ops:
  0.6 7.8 %collective-permute-start = (f32[1,3,3,256]{3,0,2,1:T(1,128)}, f32[1,3,3,256]{3,0,2,1:T(1,128)S(1)}, u32[]{:S(2)}, u32[]{:S(2)}) collective-permute-start(f32[1,3,3,256]{3,0,2,1:T(1,128)} %param.10), channel_id=1, source_target_pairs={{0,8},{8,16},{16,24},{24,0},{1,9},{9,17},{17,25},{25,1},{2,10},{10... | collective-permute-start | bytes 27656 | tf_op jit(solution)/shard_map/ppermute | solution.py:22
  1.1 7.5 %collective-permute-start.2 = (f32[1,3,3,256]{3,0,2,1:T(1,128)}, f32[1,3,3,256]{3,0,2,1:T(1,128)S(1)}, u32[]{:S(2)}, u32[]{:S(2)}) collective-permute-start(f32[1,3,3,256]{3,0,2,1:T(1,128)} %param.10), channel_id=1, source_target_pairs={{0,1},{1,2},{2,3},{3,4},{4,5},{5,6},{6,7},{7,0},{8,9},{9,10},{10,1... | collective-permute-start | bytes 27656 | tf_op jit(solution)/shard_map/ppermute | solution.py:22
  3.7 4.9 %collective-permute-start.1 = (f32[1,3,3,256]{3,0,2,1:T(1,128)}, f32[1,3,3,256]{3,0,2,1:T(1,128)S(1)}, u32[]{:S(2)}, u32[]{:S(2)}) collective-permute-start(f32[1,3,3,256]{3,0,2,1:T(1,128)} %param.10), channel_id=1, source_target_pairs={{0,4},{1,5},{2,6},{3,7},{4,0},{5,1},{6,2},{7,3},{8,12},{9,13},{10,... | collective-permute-start | bytes 27656 | tf_op jit(solution)/shard_map/ppermute | solution.py:22
  8.6 14.0 %copy-start.1 = (f32[384,384]{1,0:T(8,128)S(1)}, f32[384,384]{1,0:T(8,128)}, u32[]{:S(2)}) copy-start(f32[384,384]{1,0:T(8,128)} %global_inverse.1) | copy-start | bytes 1769476
  11.3 11.3 %copy-start = (f32[1,96,768]{2,1,0:T(8,128)S(1)}, f32[1,96,768]{2,1,0:T(8,128)}, u32[]{:S(2)}) copy-start(f32[1,96,768]{2,1,0:T(8,128)} %region_inverse.1) | copy-start | bytes 884740
  11.3 12.6 %all-to-all-start = ((f32[32,8,128]{2,1,0:T(8,128)}), f32[32,8,128]{2,1,0:T(8,128)S(1)}, u32[]{:S(2)}, u32[]{:S(2)}) async-start(f32[32,8,128]{2,1,0:T(8,128)} %get-tuple-element.43), calls=%async_computation | async-start | bytes 262144 | tf_op jit(solution)/shard_map/all_to_all | solution.py:637
  16.1 6.5 %copy-start.2 = (f32[1,96,384]{2,1,0:T(8,128)S(1)}, f32[1,96,384]{2,1,0:T(8,128)}, u32[]{:S(2)}) copy-start(f32[1,96,384]{2,1,0:T(8,128)} %coarse_map.1) | copy-start | bytes 442372
  16.3 6.7 %collective-permute-start.3 = (f32[3,256]{1,0:T(4,128)S(1)}, f32[3,256]{1,0:T(4,128)S(1)}, u32[]{:S(2)}, u32[]{:S(2)}) collective-permute-start(f32[3,256]{1,0:T(4,128)S(1)} %get-tuple-element.47), channel_id=1, source_target_pairs={{0,24},{8,0},{16,8},{24,16},{1,25},{9,1},{17,9},{25,17},{2,26},{10... | collective-permute-start | bytes 9224 | tf_op jit(solution)/shard_map/ppermute | solution.py:22
  17.9 4.7 %copy-start.5 = (s32[1,96]{1,0:T(1,128)S(1)}, s32[1,96]{1,0:T(1,128)}, u32[]{:S(2)}) copy-start(s32[1,96]{1,0:T(1,128)} %primal_index.1) | copy-start | bytes 1156
  17.9 5.2 %collective-permute-start.4 = (f32[3,256]{1,0:T(4,128)S(1)}, f32[3,256]{1,0:T(4,128)S(1)}, u32[]{:S(2)}, u32[]{:S(2)}) collective-permute-start(f32[3,256]{1,0:T(4,128)S(1)} %get-tuple-element.48), channel_id=1, source_target_pairs={{0,4},{1,5},{2,6},{3,7},{4,0},{5,1},{6,2},{7,3},{8,12},{9,13},{10,... | collective-permute-start | bytes 9224 | tf_op jit(solution)/shard_map/ppermute | solution.py:22
  20.2 3.7 %collective-permute-start.5 = (f32[3,256]{1,0:T(4,128)S(1)}, f32[3,256]{1,0:T(4,128)S(1)}, u32[]{:S(2)}, u32[]{:S(2)}) collective-permute-start(f32[3,256]{1,0:T(4,128)S(1)} %get-tuple-element.49), channel_id=1, source_target_pairs={{0,7},{1,0},{2,1},{3,2},{4,3},{5,4},{6,5},{7,6},{8,15},{9,8},{10,9... | collective-permute-start | bytes 9224 | tf_op jit(solution)/shard_map/ppermute | solution.py:22
  22.6 1.3 %copy-start.4 = (f32[1,3,3,256]{3,0,2,1:T(1,128)S(1)}, f32[1,3,3,256]{3,0,2,1:T(1,128)}, u32[]{:S(2)}) copy-start(f32[1,3,3,256]{3,0,2,1:T(1,128)} %param.9) | copy-start | bytes 27652
  23.0 0.9 %copy-start.3 = (f32[1,16,256]{2,1,0:T(8,128)S(1)}, f32[1,16,256]{2,1,0:T(8,128)}, u32[]{:S(2)}) copy-start(f32[1,16,256]{2,1,0:T(8,128)} %viscosity.1) | copy-start | bytes 49156

commit v5 on v4

--- a/solution.py
+++ b/solution.py
@@ -155,13 +155,23 @@
     return [(flat >> (bits(cells) * (dims - 1 - i))) & (cells - 1) for i in range(dims)]
 
 
+def plane_blocks(y, z, far_y, far_z, steps=1):
+    inside = [(y >> steps) == far_y, (z >> steps) == far_z]
+    nearby = [(f >> 1) + 2 * (f & 1) - 1 == b for f, b in ((y, far_y), (z, far_z))]
+    same = inside[0] & inside[1]
+    near = (nearby[0] & inside[1]) | (inside[0] & nearby[1])
+    return one_hot(same), jnp.where(same, 2.0, jnp.where(near, 1.0, 0.0)).astype(jnp.bfloat16)
+
+
 def gather_matrix(cells, steps=1):
     size = cells >> steps
     width = min(size**3, LANES)
     shape = (cells * cells, width)
     y, z = split_index(iota(shape, 0), cells, 2)
     _, far_y, far_z = split_index(iota(shape, 1), size, 3)
-    return jnp.concatenate([one_hot(((y >> steps) == far_y) & ((z >> steps) == far_z))] * (size**3 // width), axis=1)
+    return [
+        jnp.concatenate([x] * (size**3 // width), axis=1) for x in plane_blocks(y, z, far_y, far_z, steps)
+    ]
 
 
 def scatter_matrix(cells):
@@ -169,7 +179,7 @@
     shape = (half * half, cells * cells)
     y, z = split_index(iota(shape, 1), cells, 2)
     half_y, half_z = split_index(iota(shape, 0), half, 2)
-    return jnp.concatenate([one_hot(((y >> 1) == half_y) & ((z >> 1) == half_z))] * half, axis=0)
+    return jnp.concatenate([jnp.concatenate(plane_blocks(y, z, half_y, half_z), axis=1)] * half, axis=0)
 
 
 def block_matrices(cells, blocks_first):
@@ -209,7 +219,9 @@
     wide = [
         jnp.where(here, jnp.broadcast_to(coarse[c : c + 1], (cells, coarse.shape[1])), 0.0) for c in range(count)
     ]
-    return times_choice(jnp.concatenate(wide, axis=0), scatter)
+    fine = times_choice(jnp.concatenate(wide, axis=0), scatter)
+    face = cells * cells
+    return fine[:, :face], fine[:, face:]
 
 
 def sweep_power(scale, cells, weight):
@@ -290,9 +302,9 @@
     upper_out[...] = upper
     pick_out[...] = pick_matrix(cells, False)
     half = cells // 2
-    gather = gather_matrix(cells)
-    gather_out[...] = gather
-    quarter_gather = gather_matrix(cells, 2)
+    gather, gather_near = gather_matrix(cells)
+    gather_out[...] = jnp.concatenate([gather, gather_near], axis=0)
+    quarter_gather = gather_matrix(cells, 2)[0]
     scatter_out[...] = scatter_matrix(cells)
     coarsen, coarsen_near = block_matrices(half, False)
     coarsen_out[...] = jnp.concatenate([coarsen, coarsen_near], axis=0)
@@ -373,6 +385,8 @@
     sweeps,
     base_out,
     send_out,
+    buffer,
+    semaphores,
 ):
     face = cells * cells
     rows = 3 * cells
@@ -395,13 +409,16 @@
     inverse = tall(inverses[0])
     diagonal = tall(inverses[1])
 
+    def beside_x(field):
+        total = jnp.where(where_x < last, shift(field, -1, 0), 0.0)
+        return total + jnp.where(where_x > 0, shift(field, 1, 0), 0.0)
+
     def beside(field):
-        total = jnp.where(where_x < last, shift(field, -1, 0), 0.0)
-        total = total + jnp.where(where_x > 0, shift(field, 1, 0), 0.0)
-        total = total + jnp.where(where_y < last, shift(field, -cells, 1), 0.0)
+        total = jnp.where(where_y < last, shift(field, -cells, 1), 0.0)
         total = total + jnp.where(where_y > 0, shift(field, cells, 1), 0.0)
         total = total + jnp.where(where_z < last, shift(field, -1, 1), 0.0)
-        return total + jnp.where(where_z > 0, shift(field, 1, 1), 0.0)
+        total = total + jnp.where(where_z > 0, shift(field, 1, 1), 0.0)
+        return beside_x(field) + total
 
     half = cells // 2
     lane = iota((8, half**3), 1)
@@ -421,25 +438,43 @@
         local = (2.0 - damping) * swept + 0.25 * half_scale * half_beside(swept)
         return local + times_parts(remain * quarter[...], sweeps[...])
 
-    def relax(field, right):
-        return (1.0 - damping) * field + inverse * (right + beside(field))
-
-    field = inverse * source
+    scaled = inverse * source
+
+    def relax(field, neighbours):
+        return (1.0 - damping) * field + scaled + inverse * neighbours
+
+    def restrict(field):
+        remain = jnp.concatenate([source - diagonal * field + beside_x(field), field], axis=1)
+        remain = plane_restrict(remain, gather[...], cells, 3)
+        return jnp.concatenate([remain, jnp.zeros((5, half**3), jnp.float32)], axis=0)
+
+    field = scaled
+    first = None
     for cycle in range(VCYCLES):
         if cycle:
-            field = relax(field, source)
-        remain = source - diagonal * field + beside(field)
-        right = plane_restrict(remain, gather[...], cells, 3)
-        right = jnp.concatenate([right, jnp.zeros((5, half**3), jnp.float32)], axis=0)
-        field = field + plane_prolong(half_cycle(right), scatter[...], cells, 3)
-        field = relax(field, source)
+            field = relax(field, beside(field))
+        neighbours = beside(field)
+        right = restrict(field)
+        if first is None:
+            first = right
+            residual = (1.0 - damping) * source + neighbours
+        coarse = half_cycle(right)
+        if cycle == VCYCLES - 1:
+            energy = jnp.sum(source * scaled + residual * field, axis=0, keepdims=True)
+            coarse_energy = 8.0 * jnp.sum(first * coarse, axis=0, keepdims=True)
+            pieces = [energy[:, i * LANES : (i + 1) * LANES] for i in range(face // LANES)]
+            pieces += [coarse_energy[:, i * LANES : (i + 1) * LANES] for i in range(half**3 // LANES)]
+            energy = jnp.sum(functools.reduce(lambda a, b: a + b, pieces), axis=1, keepdims=True)
+            message = front[...]
+            at = (iota(message.shape, 0) == sizes[1] // 2) & (iota(message.shape, 1) == count)
+            message = message + jnp.where(at, energy, 0.0)
+            for device in range(sizes[0] * sizes[1]):
+                buffer[device] = message
+            (copy,) = load([(buffer, send_out)], semaphores)
+        correction, nearby = plane_prolong(coarse, scatter[...], cells, 3)
+        field = relax(field + correction, neighbours + beside_x(correction) + nearby)
     base_out[...] = field
-    energy = jnp.sum(jnp.sum(source * field, axis=0, keepdims=True), axis=1, keepdims=True)
-    message = front[...]
-    at = (iota(message.shape, 0) == sizes[1] // 2) & (iota(message.shape, 1) == count)
-    message = message + jnp.where(at, energy, 0.0)
-    for device in range(sizes[0] * sizes[1]):
-        send_out[device] = message
+    copy.wait()
 
 
 def ends_kernel(cells, base, pick, lower_x, lower_y, lower_z):
@@ -589,14 +624,14 @@
     def like(shape, kind=f32):
         return jax.ShapeDtypeStruct(shape, kind)
 
-    def call(kernel, out_shape, operands, in_hbm=(), scratch=()):
+    def call(kernel, out_shape, operands, in_hbm=(), scratch=(), out_hbm=0):
         return pl.pallas_call(
             kernel,
             out_shape=out_shape,
             in_specs=[vmem] * len(operands) + [hbm] * len(in_hbm),
-            out_specs=[vmem] * len(out_shape),
+            out_specs=[vmem] * (len(out_shape) - out_hbm) + [hbm] * out_hbm,
             scratch_shapes=[pltpu.VMEM(x.shape, x.dtype) for x in scratch]
-            + ([pltpu.SemaphoreType.DMA((len(in_hbm),))] if in_hbm else []),
+            + ([pltpu.SemaphoreType.DMA((len(in_hbm) + out_hbm,))] if in_hbm or out_hbm else []),
             compiler_params=pltpu.CompilerParams(vmem_limit_bytes=32 * 1024 * 1024),
         )(*operands, *[pltpu.with_memory_space_constraint(x, pltpu.HBM) for x in in_hbm])
 
@@ -620,8 +655,8 @@
             like((face, 2 * face), bf16),
             like((1, half_cells)),
             like((1, half_cells // 8)),
-            like((face, half_cells), bf16),
-            like((half_cells, face), bf16),
+            like((2 * face, half_cells), bf16),
+            like((half_cells, 2 * face), bf16),
             like((2 * half_cells, half_cells // 8), bf16),
             like((half_cells // 8, 2 * half_cells), bf16),
         ],
@@ -633,6 +668,8 @@
         functools.partial(solve_kernel, cells, sizes, count),
         [like((rows, face)), like((n_region * n_sub, height, LANES))],
         [source, below_x, below_y, below_z, inverses, front, lower, halves, quarter, gather, scatter, coarsen, sweeps],
+        scratch=[like((n_region * n_sub, height, LANES))],
+        out_hbm=1,
     )
     received = lax.all_to_all(sent, ("region", "sub"), 0, 0, tiled=True)
     lower_x, lower_y, lower_z = call(

time: 25.3 us -> 24.9 us (0.984)
  transfers between devices with their start and end apart: 7 -> 7, of which waited for: 2 -> 1; matrix products, arithmetic and copies ran while one was open for 0% -> 0% of each run, Pallas kernels for 11% -> 12%
where the time goes in v5:
time: 24.9 us; the launch traced here: 24.7 us
  starting transfers between devices  16.7 us (67%)
  Pallas kernels  6.29 us (25%)
  waiting for transfers between devices  0.9 us (4%)
  between operations  0.76 us (3%)
    ppermute x6, starting transfers between devices, shifted_2(): return lax.ppermute(x, axis, [(i, (i + by) % count) for i in range(count)])  12 us
    pallas_call x5, Pallas kernels, call(): pl.pallas_call(kernel, out_shape=out_shape, in_specs=[vmem] * len(operand...  6.29 us
    all_to_all x1, starting transfers between devices, body(): received = lax.all_to_all(sent, ('region', 'sub'), 0, 0, tiled=True)  4.74 us
    ppermute x6, waiting for transfers between devices, shifted_2(): return lax.ppermute(x, axis, [(i, (i + by) % count) for i in range(count)])  0.89 us
  transfers between devices with their start and end apart: 7, of which 1 were waited for; matrix products, arithmetic and copies ran while one was open for 0% of the time, Pallas kernels for 12%

profile of v5, /device:TPU:0, one launch (start us, length us, event | category | flops | bytes accessed | tf_op | source)
XLA Modules:
  0.0 24.7 jit_solution(16231456228514687409)
XLA Ops:
  0.6 0.5 %collective-permute-start = (f32[1,3,3,256]{3,0,2,1:T(1,128)}, f32[1,3,3,256]{3,0,2,1:T(1,128)S(1)}, u32[]{:S(2)}, u32[]{:S(2)}) collective-permute-start(f32[1,3,3,256]{3,0,2,1:T(1,128)} %param.10), channel_id=1, source_target_pairs={{0,8},{8,16},{16,24},{24,0},{1,9},{9,17},{17,25},{25,1},{2,10},{10... | collective-permute-start | bytes 27656 | tf_op jit(solution)/shard_map/ppermute | solution.py:22
  1.1 2.6 %collective-permute-start.2 = (f32[1,3,3,256]{3,0,2,1:T(1,128)}, f32[1,3,3,256]{3,0,2,1:T(1,128)S(1)}, u32[]{:S(2)}, u32[]{:S(2)}) collective-permute-start(f32[1,3,3,256]{3,0,2,1:T(1,128)} %param.10), channel_id=1, source_target_pairs={{0,1},{1,2},{2,3},{3,4},{4,5},{5,6},{6,7},{7,0},{8,9},{9,10},{10,1... | collective-permute-start | bytes 27656 | tf_op jit(solution)/shard_map/ppermute | solution.py:22
  3.7 2.6 %collective-permute-start.1 = (f32[1,3,3,256]{3,0,2,1:T(1,128)}, f32[1,3,3,256]{3,0,2,1:T(1,128)S(1)}, u32[]{:S(2)}, u32[]{:S(2)}) collective-permute-start(f32[1,3,3,256]{3,0,2,1:T(1,128)} %param.10), channel_id=1, source_target_pairs={{0,4},{1,5},{2,6},{3,7},{4,0},{5,1},{6,2},{7,3},{8,12},{9,13},{10,... | collective-permute-start | bytes 27656 | tf_op jit(solution)/shard_map/ppermute | solution.py:22
  6.3 2.3 %shard_map.120 = (f32[9,1,256]{2,1,0:T(1,128)S(1)}, f32[9,1,256]{2,1,0:T(1,128)S(1)}, f32[48,256]{1,0:T(8,128)S(1)}, f32[8,128]{1,0:T(8,128)S(1)}, f32[2,16,256]...) custom-call(f32[9,1,256]{2,1,0:T(1,128)} %bitcast.13, ...), custom_call_target="tpu_custom_call" | custom-call | tf_op jit(solution)/shard_map/pallas_call | solution.py:628
  8.6 0.0 collective-permute-done
  8.6 0.0 collective-permute-done.2
  8.6 0.0 collective-permute-done.1
  8.6 0.0 copy-start.1
  8.6 2.3 %shard_map.121 = (f32[48,256]{1,0:T(8,128)S(1)}, f32[32,8,128]{2,1,0:T(8,128)}) custom-call(f32[48,256]{1,0:T(8,128)S(1)} %get-tuple-element.33.source_own, f32[9,1,256]{2,1,0:T(1,128)S(1)} %bitcast.9, f32[9,1,256]{2,1,0:T(1,128)S(1)} %bitcast.11, f32[9,1,256]{2,1,0:T(1,128)S(1)} %bitcast.10, f32[2,16,256]{2,1,0:T(8,128)S(1)} %get-tuple-element.34.inverses, ...), custom_call_target="tpu_custom_call" | custom-call | tf_op jit(solution)/shard_map/pallas_call | solution.py:628
  11.0 0.0 copy-start
  11.0 4.7 %all-to-all-start = ((f32[32,8,128]{2,1,0:T(8,128)}), f32[32,8,128]{2,1,0:T(8,128)S(1)}, u32[]{:S(2)}, u32[]{:S(2)}) async-start(f32[32,8,128]{2,1,0:T(8,128)} %get-tuple-element.43), calls=%async_computation | async-start | bytes 262144 | tf_op jit(solution)/shard_map/all_to_all | solution.py:674
  15.7 0.0 copy-start.2
  15.7 0.2 shard_map.123
  15.9 1.6 %collective-permute-start.3 = (f32[3,256]{1,0:T(4,128)S(1)}, f32[3,256]{1,0:T(4,128)S(1)}, u32[]{:S(2)}, u32[]{:S(2)}) collective-permute-start(f32[3,256]{1,0:T(4,128)S(1)} %get-tuple-element.47), channel_id=1, source_target_pairs={{0,24},{8,0},{16,8},{24,16},{1,25},{9,1},{17,9},{25,17},{2,26},{10... | collective-permute-start | bytes 9224 | tf_op jit(solution)/shard_map/ppermute | solution.py:22
  17.5 0.0 copy-start.5
  17.5 2.4 %collective-permute-start.4 = (f32[3,256]{1,0:T(4,128)S(1)}, f32[3,256]{1,0:T(4,128)S(1)}, u32[]{:S(2)}, u32[]{:S(2)}) collective-permute-start(f32[3,256]{1,0:T(4,128)S(1)} %get-tuple-element.48), channel_id=1, source_target_pairs={{0,4},{1,5},{2,6},{3,7},{4,0},{5,1},{6,2},{7,3},{8,12},{9,13},{10,... | collective-permute-start | bytes 9224 | tf_op jit(solution)/shard_map/ppermute | solution.py:22
  19.9 2.4 %collective-permute-start.5 = (f32[3,256]{1,0:T(4,128)S(1)}, f32[3,256]{1,0:T(4,128)S(1)}, u32[]{:S(2)}, u32[]{:S(2)}) collective-permute-start(f32[3,256]{1,0:T(4,128)S(1)} %get-tuple-element.49), channel_id=1, source_target_pairs={{0,7},{1,0},{2,1},{3,2},{4,3},{5,4},{6,5},{7,6},{8,15},{9,8},{10,9... | collective-permute-start | bytes 9224 | tf_op jit(solution)/shard_map/ppermute | solution.py:22
  22.2 0.0 copy-done.1
  22.2 0.0 copy-done
  22.2 0.0 copy-done.2
  22.2 0.0 copy-done.5
  22.2 0.0 copy-start.4
  22.2 0.4 %shard_map.122 = (f32[16,256]{1,0:T(8,128)S(1)}, f32[8,96,128]{2,1,0:T(8,128)S(1)}, f32[96,384]{1,0:T(8,128)S(1)}, bf16[384,768]{1,0:T(8,128)(2,1)S(1)}, f32[96,...) custom-call(f32[48,256]{1,0:T(8,128)S(1)} %get-tuple-element.44.base, s32[1,96]{1,0:T(1,128)S(1)} %copy-done.5, ...), custom_call_target="tpu_custom_call" | custom-call | tf_op jit(solution)/shard_map/pallas_call | solution.py:628
  22.6 0.0 copy-start.3
  22.6 0.0 collective-permute-done.3.after_x
  22.7 0.0 collective-permute-done.4.after_y
  22.7 0.9 %collective-permute-done.5.after_z = f32[3,256]{1,0:T(4,128)S(1)} collective-permute-done((f32[3,256]{1,0:T(4,128)S(1)}, f32[3,256]{1,0:T(4,128)S(1)}, u32[]{:S(2)}, u32[]{:S(2)}) %collective-permute-start.5) | collective-permute-done | bytes 3104 | tf_op jit(solution)/shard_map/ppermute | solution.py:22
  23.6 0.0 all-to-all-done.received
  23.6 0.0 copy-done.4
  23.6 0.0 copy-done.3
  23.6 1.1 %shard_map.124 = (f32[9,1,256]{2,1,0:T(1,128)}, f32[9,1,256]{2,1,0:T(1,128)}, f32[1,3,16,256]{3,2,1,0:T(8,128)}, f32[1,16,256]{2,1,0:T(8,128)}) custom-call(f32[32,8,128]{2,1,0:T(8,128)S(1)} %all-to-all-done.received, f32[48,256]{1,0:T(8,128)S(1)} %get-tuple-element.44.base, f32[16,256]{1,0:T(8,128)S(1)} %get-tuple-element.45.ends, ...), custom_call_target="tpu_custom_call" | custom-call | tf_op jit(solution)/shard_map/pallas_call | solution.py:628
Async XLA Ops:
  0.6 8.0 %collective-permute-start = (f32[1,3,3,256]{3,0,2,1:T(1,128)}, f32[1,3,3,256]{3,0,2,1:T(1,128)S(1)}, u32[]{:S(2)}, u32[]{:S(2)}) collective-permute-start(f32[1,3,3,256]{3,0,2,1:T(1,128)} %param.10), channel_id=1, source_target_pairs={{0,8},{8,16},{16,24},{24,0},{1,9},{9,17},{17,25},{25,1},{2,10},{10... | collective-permute-start | bytes 27656 | tf_op jit(solution)/shard_map/ppermute | solution.py:22
  1.1 7.5 %collective-permute-start.2 = (f32[1,3,3,256]{3,0,2,1:T(1,128)}, f32[1,3,3,256]{3,0,2,1:T(1,128)S(1)}, u32[]{:S(2)}, u32[]{:S(2)}) collective-permute-start(f32[1,3,3,256]{3,0,2,1:T(1,128)} %param.10), channel_id=1, source_target_pairs={{0,1},{1,2},{2,3},{3,4},{4,5},{5,6},{6,7},{7,0},{8,9},{9,10},{10,1... | collective-permute-start | bytes 27656 | tf_op jit(solution)/shard_map/ppermute | solution.py:22
  3.7 4.9 %collective-permute-start.1 = (f32[1,3,3,256]{3,0,2,1:T(1,128)}, f32[1,3,3,256]{3,0,2,1:T(1,128)S(1)}, u32[]{:S(2)}, u32[]{:S(2)}) collective-permute-start(f32[1,3,3,256]{3,0,2,1:T(1,128)} %param.10), channel_id=1, source_target_pairs={{0,4},{1,5},{2,6},{3,7},{4,0},{5,1},{6,2},{7,3},{8,12},{9,13},{10,... | collective-permute-start | bytes 27656 | tf_op jit(solution)/shard_map/ppermute | solution.py:22
  8.6 13.6 %copy-start.1 = (f32[384,384]{1,0:T(8,128)S(1)}, f32[384,384]{1,0:T(8,128)}, u32[]{:S(2)}) copy-start(f32[384,384]{1,0:T(8,128)} %global_inverse.1) | copy-start | bytes 1769476
  11.0 11.3 %copy-start = (f32[1,96,768]{2,1,0:T(8,128)S(1)}, f32[1,96,768]{2,1,0:T(8,128)}, u32[]{:S(2)}) copy-start(f32[1,96,768]{2,1,0:T(8,128)} %region_inverse.1) | copy-start | bytes 884740
  11.0 12.6 %all-to-all-start = ((f32[32,8,128]{2,1,0:T(8,128)}), f32[32,8,128]{2,1,0:T(8,128)S(1)}, u32[]{:S(2)}, u32[]{:S(2)}) async-start(f32[32,8,128]{2,1,0:T(8,128)} %get-tuple-element.43), calls=%async_computation | async-start | bytes 262144 | tf_op jit(solution)/shard_map/all_to_all | solution.py:674
  15.7 6.5 %copy-start.2 = (f32[1,96,384]{2,1,0:T(8,128)S(1)}, f32[1,96,384]{2,1,0:T(8,128)}, u32[]{:S(2)}) copy-start(f32[1,96,384]{2,1,0:T(8,128)} %coarse_map.1) | copy-start | bytes 442372
  15.9 6.7 %collective-permute-start.3 = (f32[3,256]{1,0:T(4,128)S(1)}, f32[3,256]{1,0:T(4,128)S(1)}, u32[]{:S(2)}, u32[]{:S(2)}) collective-permute-start(f32[3,256]{1,0:T(4,128)S(1)} %get-tuple-element.47), channel_id=1, source_target_pairs={{0,24},{8,0},{16,8},{24,16},{1,25},{9,1},{17,9},{25,17},{2,26},{10... | collective-permute-start | bytes 9224 | tf_op jit(solution)/shard_map/ppermute | solution.py:22
  17.5 4.7 %copy-start.5 = (s32[1,96]{1,0:T(1,128)S(1)}, s32[1,96]{1,0:T(1,128)}, u32[]{:S(2)}) copy-start(s32[1,96]{1,0:T(1,128)} %primal_index.1) | copy-start | bytes 1156
  17.5 5.2 %collective-permute-start.4 = (f32[3,256]{1,0:T(4,128)S(1)}, f32[3,256]{1,0:T(4,128)S(1)}, u32[]{:S(2)}, u32[]{:S(2)}) collective-permute-start(f32[3,256]{1,0:T(4,128)S(1)} %get-tuple-element.48), channel_id=1, source_target_pairs={{0,4},{1,5},{2,6},{3,7},{4,0},{5,1},{6,2},{7,3},{8,12},{9,13},{10,... | collective-permute-start | bytes 9224 | tf_op jit(solution)/shard_map/ppermute | solution.py:22
  19.9 3.7 %collective-permute-start.5 = (f32[3,256]{1,0:T(4,128)S(1)}, f32[3,256]{1,0:T(4,128)S(1)}, u32[]{:S(2)}, u32[]{:S(2)}) collective-permute-start(f32[3,256]{1,0:T(4,128)S(1)} %get-tuple-element.49), channel_id=1, source_target_pairs={{0,7},{1,0},{2,1},{3,2},{4,3},{5,4},{6,5},{7,6},{8,15},{9,8},{10,9... | collective-permute-start | bytes 9224 | tf_op jit(solution)/shard_map/ppermute | solution.py:22
  22.2 1.3 %copy-start.4 = (f32[1,3,3,256]{3,0,2,1:T(1,128)S(1)}, f32[1,3,3,256]{3,0,2,1:T(1,128)}, u32[]{:S(2)}) copy-start(f32[1,3,3,256]{3,0,2,1:T(1,128)} %param.9) | copy-start | bytes 27652
  22.6 0.9 %copy-start.3 = (f32[1,16,256]{2,1,0:T(8,128)S(1)}, f32[1,16,256]{2,1,0:T(8,128)}, u32[]{:S(2)}) copy-start(f32[1,16,256]{2,1,0:T(8,128)} %viscosity.1) | copy-start | bytes 49156

commit v6 on v5

--- a/solution.py
+++ b/solution.py
@@ -8,10 +8,7 @@
 from jax.sharding import PartitionSpec as P
 
 DOM_Z = 4
-LEVELS = 3
-SWEEPS = 1
 COARSE_SWEEPS = 8
-VCYCLES = 2
 LANES = 128
 
 damping = 0.8
@@ -86,48 +83,66 @@
     return [jnp.concatenate([rows[3 * d + c] for c in range(3)], axis=0) for d in range(3)]
 
 
-def spread(faces, cells):
+def lane_gather(x, lanes):
+    return jnp.take_along_axis(x, lanes, axis=1, mode="promise_in_bounds")
+
+
+def grid(cells, count, tile):
+    shape = (count * cells, LANES)
+    y, z = split_index(iota(shape, 1) + tile * LANES, cells, 2)
+    return iota(shape, 0) & (cells - 1), y, z
+
+
+def rows_of_tiles(x, rows):
+    count, width = x.shape
+    tiles = width // LANES
+    return jnp.concatenate(
+        [
+            jnp.broadcast_to(x[c : c + 1, i * LANES : (i + 1) * LANES], (rows // tiles, LANES))
+            for c in range(count)
+            for i in range(tiles)
+        ],
+        axis=0,
+    )
+
+
+def unfold(on_y, on_z, cells, upper):
+    count, face = on_y.shape
+    end = cells - 1 if upper else 0
+    wide_y = rows_of_tiles(on_y, cells)
+    wide_z = rows_of_tiles(on_z, cells)
+    tiles = []
+    for tile in range(face // LANES):
+        x, y, z = grid(cells, count, tile)
+        start = (x * cells) & (LANES - 1)
+        field = jnp.where(z == end, lane_gather(wide_z, start + y), 0.0)
+        if end * cells // LANES == tile:
+            field = field + jnp.where(y == end, lane_gather(wide_y, start + z), 0.0)
+        tiles.append(field)
+    return jnp.concatenate(tiles, axis=1)
+
+
+def fold(field, cells, upper):
     face = cells * cells
-    here = lax.div(iota((cells, face), 1), jnp.full((cells, face), cells, jnp.int32)) == iota((cells, face), 0)
-    rows = [jnp.where(here, jnp.broadcast_to(faces[c : c + 1], (cells, face)), 0.0) for c in range(faces.shape[0])]
-    return jnp.concatenate(rows, axis=0)
-
-
-def mask_sum(x, cells):
-    face = cells * cells
-    here = lax.div(iota((cells, face), 1), jnp.full((cells, face), cells, jnp.int32)) == iota((cells, face), 0)
-    rows = [
-        jnp.sum(jnp.where(here, x[c * cells : (c + 1) * cells], 0.0), axis=0, keepdims=True)
-        for c in range(x.shape[0] // cells)
-    ]
-    return jnp.concatenate(rows, axis=0)
-
-
-def place_matrix(cells, upper):
-    row = iota((cells, cells * cells), 0)
-    column = iota((cells, cells * cells), 1)
     end = cells - 1 if upper else 0
-    on_y = one_hot(column == row + end * cells)
-    on_z = one_hot(column == row * cells + end)
-    return jnp.concatenate([on_y] * cells + [on_z] * cells, axis=0)
-
-
-def pick_matrix(cells, upper):
-    face = cells * cells
-    row = iota((face, LANES), 0)
-    second = iota((face, LANES), 1) & (cells - 1)
-    end = cells - 1 if upper else 0
-    on_y = one_hot(row == second + end * cells)
-    on_z = one_hot(row == second * cells + end)
-    return jnp.concatenate([on_y] * (face // LANES) + [on_z] * (face // LANES), axis=1)
-
-
-def face_ends(field, pick, cells, upper):
-    face = cells * cells
-    at = cells - 1 if upper else 0
-    ends = times_choice(field, pick)
-    on_x = [field[c * cells + at : c * cells + at + 1] for c in range(3)]
-    return jnp.concatenate(on_x, axis=0), mask_sum(ends[:, :face], cells), mask_sum(ends[:, face:], cells)
+    rows = LANES // cells
+    tiles = [field[:, i * LANES : (i + 1) * LANES] for i in range(face // LANES)]
+    x, first, second = grid(cells, 3, 0)
+    on_y = lane_gather(tiles[end * cells // LANES], ((end * cells) & (LANES - 1)) + second)
+    on_z = jnp.zeros_like(on_y)
+    for i, tile in enumerate(tiles):
+        values = lane_gather(tile, ((second * cells) & (LANES - 1)) + end)
+        on_z = jnp.where(second // rows == i, values, on_z)
+    here = first == (x & (rows - 1))
+    faces = [jnp.concatenate([field[c * cells + end : c * cells + end + 1] for c in range(3)], axis=0)]
+    for values in (on_y, on_z):
+        values = jnp.where(here, values, 0.0)
+        sums = [jnp.sum(values[i * rows : (i + 1) * rows], axis=0, keepdims=True) for i in range(3 * cells // rows)]
+        per = face // LANES
+        faces.append(
+            jnp.concatenate([jnp.concatenate(sums[c * per : (c + 1) * per], axis=1) for c in range(3)], axis=0)
+        )
+    return faces
 
 
 def column_of(line):
@@ -165,21 +180,10 @@
 
 def gather_matrix(cells, steps=1):
     size = cells >> steps
-    width = min(size**3, LANES)
-    shape = (cells * cells, width)
+    shape = (cells * cells, min(size**3, LANES))
     y, z = split_index(iota(shape, 0), cells, 2)
     _, far_y, far_z = split_index(iota(shape, 1), size, 3)
-    return [
-        jnp.concatenate([x] * (size**3 // width), axis=1) for x in plane_blocks(y, z, far_y, far_z, steps)
-    ]
-
-
-def scatter_matrix(cells):
-    half = cells // 2
-    shape = (half * half, cells * cells)
-    y, z = split_index(iota(shape, 1), cells, 2)
-    half_y, half_z = split_index(iota(shape, 0), half, 2)
-    return jnp.concatenate([jnp.concatenate(plane_blocks(y, z, half_y, half_z), axis=1)] * half, axis=0)
+    return plane_blocks(y, z, far_y, far_z, steps)
 
 
 def block_matrices(cells, blocks_first):
@@ -198,30 +202,40 @@
     return one_hot(same), jnp.where(same, 3.0, jnp.where(near, 1.0, 0.0)).astype(jnp.bfloat16)
 
 
-def own_part(cells, steps=1):
+def plane_restrict(field, gather, cells, count, steps=1):
     size = cells >> steps
-    shape = (cells, size**3)
-    return split_index(iota(shape, 1), size, 3)[0] == (iota(shape, 0) >> steps)
-
-
-def plane_restrict(field, gather, cells, count, steps=1):
+    width = gather.shape[1]
+    per = width // (size * size) << steps
     spread_out = times_choice(field, gather)
-    here = own_part(cells, steps)
-    rows = [
-        jnp.sum(jnp.where(here, spread_out[c * cells : (c + 1) * cells], 0.0), axis=0, keepdims=True)
-        for c in range(count)
-    ]
+    shape = (cells, width)
+    own = split_index(iota(shape, 1), size, 3)[0] == ((iota(shape, 0) & (per - 1)) >> steps)
+    group = iota(shape, 0) // per
+    rows = []
+    for c in range(count):
+        values = jnp.where(own, spread_out[c * cells : (c + 1) * cells], 0.0)
+        tiles = [
+            jnp.sum(jnp.where(group == i, values, 0.0), axis=0, keepdims=True) for i in range(cells // per)
+        ]
+        rows.append(tiles[0] if len(tiles) == 1 else jnp.concatenate(tiles, axis=1))
     return 0.125**steps * (rows[0] if count == 1 else jnp.concatenate(rows, axis=0))
 
 
-def plane_prolong(coarse, scatter, cells, count):
-    here = own_part(cells)
-    wide = [
-        jnp.where(here, jnp.broadcast_to(coarse[c : c + 1], (cells, coarse.shape[1])), 0.0) for c in range(count)
-    ]
-    fine = times_choice(jnp.concatenate(wide, axis=0), scatter)
-    face = cells * cells
-    return fine[:, :face], fine[:, face:]
+def plane_prolong(coarse, cells, count):
+    half = cells // 2
+    wide = rows_of_tiles(coarse[:count], cells)
+    fine, nearby = [], []
+    for tile in range(cells * cells // LANES):
+        x, y, z = grid(cells, count, tile)
+        start = ((x >> 1) * half * half) & (LANES - 1)
+        half_y, half_z = y >> 1, z >> 1
+        other_y, other_z = half_y + 2 * (y & 1) - 1, half_z + 2 * (z & 1) - 1
+        inside_y, inside_z = (other_y & (half - 1)) == other_y, (other_z & (half - 1)) == other_z
+        values = lane_gather(wide, start + half_y * half + half_z)
+        beside_y = lane_gather(wide, start + (other_y & (half - 1)) * half + half_z)
+        beside_z = lane_gather(wide, start + half_y * half + (other_z & (half - 1)))
+        fine.append(values)
+        nearby.append(2.0 * values + jnp.where(inside_y, beside_y, 0.0) + jnp.where(inside_z, beside_z, 0.0))
+    return jnp.concatenate(fine, axis=1), jnp.concatenate(nearby, axis=1)
 
 
 def sweep_power(scale, cells, weight):
@@ -269,13 +283,9 @@
     source_out,
     front_out,
     inverse_out,
-    lower_out,
-    upper_out,
-    pick_out,
     half_out,
     quarter_out,
     gather_out,
-    scatter_out,
     coarsen_out,
     sweeps_out,
     reaction,
@@ -297,15 +307,10 @@
     )
     face = cells * cells
     n_sub = sizes[1]
-    lower_out[...] = place_matrix(cells, False)
-    upper = place_matrix(cells, True)
-    upper_out[...] = upper
-    pick_out[...] = pick_matrix(cells, False)
     half = cells // 2
     gather, gather_near = gather_matrix(cells)
     gather_out[...] = jnp.concatenate([gather, gather_near], axis=0)
     quarter_gather = gather_matrix(cells, 2)[0]
-    scatter_out[...] = scatter_matrix(cells)
     coarsen, coarsen_near = block_matrices(half, False)
     coarsen_out[...] = jnp.concatenate([coarsen, coarsen_near], axis=0)
     refine = jnp.concatenate(block_matrices(half, True), axis=1)
@@ -338,7 +343,7 @@
         (1.0 - damping) * refined[:, : half**3] + 0.25 * half_scale * refined[:, half**3 :]
     )
     row_x = iota((cells, face), 0)
-    source = times_choice(jnp.concatenate([spread(faces[1], cells), spread(faces[2], cells)], axis=1), upper)
+    source = unfold(faces[1], faces[2], cells, True)
     own_x = jnp.concatenate(
         [jnp.where(row_x == cells - 1, jnp.broadcast_to(faces[0][c : c + 1], (cells, face)), 0.0) for c in range(3)],
         axis=0,
@@ -376,11 +381,9 @@
     from_z,
     inverses,
     front,
-    lower,
     halves,
     quarter,
     gather,
-    scatter,
     coarsen,
     sweeps,
     base_out,
@@ -393,9 +396,7 @@
     below_x, below_y, below_z = [faces_of(ref)[d] for d, ref in enumerate((from_x, from_y, from_z))]
     n_region, n_sub = sizes
     row_x = iota((cells, face), 0)
-    source = source_own[...] - times_choice(
-        jnp.concatenate([spread(below_y, cells), spread(below_z, cells)], axis=1), lower[...]
-    )
+    source = source_own[...] - unfold(below_y, below_z, cells, False)
     source = source - jnp.concatenate(
         [jnp.where(row_x == 0, jnp.broadcast_to(below_x[c : c + 1], (cells, face)), 0.0) for c in range(3)],
         axis=0,
@@ -438,47 +439,37 @@
         local = (2.0 - damping) * swept + 0.25 * half_scale * half_beside(swept)
         return local + times_parts(remain * quarter[...], sweeps[...])
 
-    scaled = inverse * source
-
-    def relax(field, neighbours):
-        return (1.0 - damping) * field + scaled + inverse * neighbours
-
-    def restrict(field):
-        remain = jnp.concatenate([source - diagonal * field + beside_x(field), field], axis=1)
-        remain = plane_restrict(remain, gather[...], cells, 3)
-        return jnp.concatenate([remain, jnp.zeros((5, half**3), jnp.float32)], axis=0)
-
-    field = scaled
-    first = None
-    for cycle in range(VCYCLES):
-        if cycle:
-            field = relax(field, beside(field))
-        neighbours = beside(field)
-        right = restrict(field)
-        if first is None:
-            first = right
-            residual = (1.0 - damping) * source + neighbours
-        coarse = half_cycle(right)
-        if cycle == VCYCLES - 1:
-            energy = jnp.sum(source * scaled + residual * field, axis=0, keepdims=True)
-            coarse_energy = 8.0 * jnp.sum(first * coarse, axis=0, keepdims=True)
-            pieces = [energy[:, i * LANES : (i + 1) * LANES] for i in range(face // LANES)]
-            pieces += [coarse_energy[:, i * LANES : (i + 1) * LANES] for i in range(half**3 // LANES)]
-            energy = jnp.sum(functools.reduce(lambda a, b: a + b, pieces), axis=1, keepdims=True)
-            message = front[...]
-            at = (iota(message.shape, 0) == sizes[1] // 2) & (iota(message.shape, 1) == count)
-            message = message + jnp.where(at, energy, 0.0)
-            for device in range(sizes[0] * sizes[1]):
-                buffer[device] = message
-            (copy,) = load([(buffer, send_out)], semaphores)
-        correction, nearby = plane_prolong(coarse, scatter[...], cells, 3)
-        field = relax(field + correction, neighbours + beside_x(correction) + nearby)
-    base_out[...] = field
+    def correct(residual):
+        swept = inverse * residual
+        remain = (1.0 - damping) * residual
+        right = plane_restrict(
+            jnp.concatenate([remain + beside_x(swept), swept], axis=1), gather[...], cells, 3
+        )
+        right = jnp.concatenate([right, jnp.zeros((5, half**3), jnp.float32)], axis=0)
+        remain = remain + beside(swept)
+        correction, nearby = plane_prolong(half_cycle(right), cells, 3)
+        return swept + correction, remain - diagonal * correction + beside_x(correction) + nearby
+
+    field, residual = correct(source)
+    swept = inverse * residual
+    then = (1.0 - damping) * residual + beside(swept)
+    energy = jnp.sum((source + residual) * field + swept * (residual + then), axis=0, keepdims=True)
+    energy = functools.reduce(lambda a, b: a + b, [energy[:, i * LANES : (i + 1) * LANES] for i in range(face // LANES)])
+    energy = jnp.sum(energy, axis=1, keepdims=True)
+    message = front[...]
+    at = (iota(message.shape, 0) == sizes[1] // 2) & (iota(message.shape, 1) == count)
+    message = message + jnp.where(at, energy, 0.0)
+    for device in range(sizes[0] * sizes[1]):
+        buffer[device] = message
+    (copy,) = load([(buffer, send_out)], semaphores)
+    field = field + swept
+    more, residual = correct(then)
+    base_out[...] = field + more + inverse * residual
     copy.wait()
 
 
-def ends_kernel(cells, base, pick, lower_x, lower_y, lower_z):
-    lower_x[...], lower_y[...], lower_z[...] = face_ends(base[...], pick[...], cells, False)
+def ends_kernel(cells, base, lower_x, lower_y, lower_z):
+    lower_x[...], lower_y[...], lower_z[...] = fold(base[...], cells, False)
 
 
 def between_kernel(
@@ -496,8 +487,7 @@
     choose_out,
 ):
     face = cells * cells
-    on_x, on_y, on_z = face_ends(base[...], pick_matrix(cells, True), cells, True)
-    ends_out[...] = jnp.concatenate([on_x, on_y, on_z, jnp.zeros((7, face), jnp.float32)], axis=0)
+    ends_out[...] = jnp.concatenate(fold(base[...], cells, True) + [jnp.zeros((7, face), jnp.float32)], axis=0)
     count = primal_index.shape[1]
     group, _, place, _ = decode(primal_index[...], cells)
     choose_out[...] = jnp.concatenate(
@@ -524,7 +514,6 @@
     after_x,
     after_y,
     after_z,
-    upper,
     spots,
     choose,
     region_blocks,
@@ -559,8 +548,7 @@
     for c in range(3):
         velocity_out[0, c] = velocity[c * cells : (c + 1) * cells]
     after = [after_x[...], after_y[...], after_z[...]]
-    ahead = jnp.concatenate([spread(after[1][1:2], cells), spread(after[2][2:3], cells)], axis=1)
-    ahead = times_choice(ahead, upper[...])
+    ahead = unfold(after[1][1:2], after[2][2:3], cells, True)
     where_x, where_y, where_z = positions(cells, cells)
     end = cells - 1
     field_x, field_y, field_z = [velocity[c * cells : (c + 1) * cells] for c in range(3)]
@@ -640,9 +628,7 @@
     below_z = shifted_2(direction, "sub", 1).reshape(lines)
     multipliers, direction, residual = [x.reshape(lines) for x in (multipliers, direction, residual)]
     half_cells = (cells // 2) ** 3
-    (
-        direction, residual, source, front, inverses, lower, upper, pick, halves, quarter, gather, scatter, coarsen, sweeps
-    ) = call(
+    direction, residual, source, front, inverses, halves, quarter, gather, coarsen, sweeps = call(
         functools.partial(before_kernel, cells, sizes),
         [
             like(lines),
@@ -650,13 +636,9 @@
             like((rows, face)),
             like((height, LANES)),
             like((2, cells, face)),
-            like((2 * face, face), bf16),
-            like((2 * face, face), bf16),
-            like((face, 2 * face), bf16),
             like((1, half_cells)),
             like((1, half_cells // 8)),
-            like((2 * face, half_cells), bf16),
-            like((half_cells, 2 * face), bf16),
+            like((2 * face, min(half_cells, LANES)), bf16),
             like((2 * half_cells, half_cells // 8), bf16),
             like((half_cells // 8, 2 * half_cells), bf16),
         ],
@@ -667,13 +649,13 @@
     base, sent = call(
         functools.partial(solve_kernel, cells, sizes, count),
         [like((rows, face)), like((n_region * n_sub, height, LANES))],
-        [source, below_x, below_y, below_z, inverses, front, lower, halves, quarter, gather, scatter, coarsen, sweeps],
+        [source, below_x, below_y, below_z, inverses, front, halves, quarter, gather, coarsen, sweeps],
         scratch=[like((n_region * n_sub, height, LANES))],
         out_hbm=1,
     )
     received = lax.all_to_all(sent, ("region", "sub"), 0, 0, tiled=True)
     lower_x, lower_y, lower_z = call(
-        functools.partial(ends_kernel, cells), [like((3, face))] * 3, [base, pick]
+        functools.partial(ends_kernel, cells), [like((3, face))] * 3, [base]
     )
     after_x = shifted_2(lower_x, "region", -1)
     after_y = shifted_2(lower_y, "sub", -DOM_Z)
@@ -700,7 +682,6 @@
             after_x,
             after_y,
             after_z,
-            upper,
             spots,
             choose,
             region_blocks,

time: 24.9 us -> 24.2 us (0.972)
  Pallas kernels: 6.29 us -> 5.35 us
    pallas_call x5, Pallas kernels: 6.29 us -> 5.35 us  [call(): pl.pallas_call(kernel, out_shape=out_shape, in_specs=[vmem] * len(operand...]
  transfers between devices with their start and end apart: 7 -> 7, of which waited for: 1 -> 2; matrix products, arithmetic and copies ran while one was open for 0% -> 0% of each run, Pallas kernels for 12% -> 11%
where the time goes in v6:
time: 24.2 us; the launch traced here: 24 us
  starting transfers between devices  16.8 us (69%)
  Pallas kernels  5.35 us (22%)
  waiting for transfers between devices  1.09 us (5%)
  between operations  0.74 us (3%)
    ppermute x6, starting transfers between devices, shifted_2(): return lax.ppermute(x, axis, [(i, (i + by) % count) for i in range(count)])  12 us
    pallas_call x5, Pallas kernels, call(): pl.pallas_call(kernel, out_shape=out_shape, in_specs=[vmem] * len(operand...  5.35 us
    all_to_all x1, starting transfers between devices, body(): received = lax.all_to_all(sent, ('region', 'sub'), 0, 0, tiled=True)  4.78 us
    ppermute x6, waiting for transfers between devices, shifted_2(): return lax.ppermute(x, axis, [(i, (i + by) % count) for i in range(count)])  1.09 us
  transfers between devices with their start and end apart: 7, of which 2 were waited for; matrix products, arithmetic and copies ran while one was open for 0% of the time, Pallas kernels for 11%

profile of v6, /device:TPU:0, one launch (start us, length us, event | category | flops | bytes accessed | tf_op | source)
XLA Modules:
  0.0 24.0 jit_solution(1289906352091257732)
XLA Ops:
  0.6 0.5 %collective-permute-start = (f32[1,3,3,256]{3,0,2,1:T(1,128)}, f32[1,3,3,256]{3,0,2,1:T(1,128)S(1)}, u32[]{:S(2)}, u32[]{:S(2)}) collective-permute-start(f32[1,3,3,256]{3,0,2,1:T(1,128)} %param.10), channel_id=1, source_target_pairs={{0,8},{8,16},{16,24},{24,0},{1,9},{9,17},{17,25},{25,1},{2,10},{10... | collective-permute-start | bytes 27656 | tf_op jit(solution)/shard_map/ppermute | solution.py:19
  1.1 2.6 %collective-permute-start.2 = (f32[1,3,3,256]{3,0,2,1:T(1,128)}, f32[1,3,3,256]{3,0,2,1:T(1,128)S(1)}, u32[]{:S(2)}, u32[]{:S(2)}) collective-permute-start(f32[1,3,3,256]{3,0,2,1:T(1,128)} %param.10), channel_id=1, source_target_pairs={{0,1},{1,2},{2,3},{3,4},{4,5},{5,6},{6,7},{7,0},{8,9},{9,10},{10,1... | collective-permute-start | bytes 27656 | tf_op jit(solution)/shard_map/ppermute | solution.py:19
  3.7 2.6 %collective-permute-start.1 = (f32[1,3,3,256]{3,0,2,1:T(1,128)}, f32[1,3,3,256]{3,0,2,1:T(1,128)S(1)}, u32[]{:S(2)}, u32[]{:S(2)}) collective-permute-start(f32[1,3,3,256]{3,0,2,1:T(1,128)} %param.10), channel_id=1, source_target_pairs={{0,4},{1,5},{2,6},{3,7},{4,0},{5,1},{6,2},{7,3},{8,12},{9,13},{10,... | collective-permute-start | bytes 27656 | tf_op jit(solution)/shard_map/ppermute | solution.py:19
  6.3 0.0 copy-start.2
  6.3 2.1 %shard_map.120 = (f32[9,1,256]{2,1,0:T(1,128)S(1)}, f32[9,1,256]{2,1,0:T(1,128)S(1)}, f32[48,256]{1,0:T(8,128)S(1)}, f32[8,128]{1,0:T(8,128)S(1)}, f32[2,16,256]...) custom-call(f32[9,1,256]{2,1,0:T(1,128)} %bitcast.13, ...), custom_call_target="tpu_custom_call" | custom-call | tf_op jit(solution)/shard_map/pallas_call | solution.py:616
  8.4 0.0 copy-start.1
  8.5 0.0 collective-permute-done
  8.5 0.1 collective-permute-done.2
  8.6 0.0 collective-permute-done.1
  8.6 1.7 %shard_map.121 = (f32[48,256]{1,0:T(8,128)S(1)}, f32[32,8,128]{2,1,0:T(8,128)}) custom-call(f32[48,256]{1,0:T(8,128)S(1)} %get-tuple-element.29.source_own, f32[9,1,256]{2,1,0:T(1,128)S(1)} %bitcast.8, f32[9,1,256]{2,1,0:T(1,128)S(1)} %bitcast.10, f32[9,1,256]{2,1,0:T(1,128)S(1)} %bitcast.9, f32[2,16,256]{2,1,0:T(8,128)S(1)} %get-tuple-element.30.inverses, ...), custom_call_target="tpu_custom_call" | custom-call | tf_op jit(solution)/shard_map/pallas_call | solution.py:616
  10.3 0.0 copy-start
  10.3 4.8 %all-to-all-start = ((f32[32,8,128]{2,1,0:T(8,128)}), f32[32,8,128]{2,1,0:T(8,128)S(1)}, u32[]{:S(2)}, u32[]{:S(2)}) async-start(f32[32,8,128]{2,1,0:T(8,128)} %get-tuple-element.37), calls=%async_computation | async-start | bytes 262144 | tf_op jit(solution)/shard_map/all_to_all | solution.py:656
  15.1 0.1 shard_map.123
  15.2 1.6 %collective-permute-start.3 = (f32[3,256]{1,0:T(4,128)S(1)}, f32[3,256]{1,0:T(4,128)S(1)}, u32[]{:S(2)}, u32[]{:S(2)}) collective-permute-start(f32[3,256]{1,0:T(4,128)S(1)} %get-tuple-element.40), channel_id=1, source_target_pairs={{0,24},{8,0},{16,8},{24,16},{1,25},{9,1},{17,9},{25,17},{2,26},{10... | collective-permute-start | bytes 9224 | tf_op jit(solution)/shard_map/ppermute | solution.py:19
  16.8 0.0 copy-start.5
  16.8 2.4 %collective-permute-start.4 = (f32[3,256]{1,0:T(4,128)S(1)}, f32[3,256]{1,0:T(4,128)S(1)}, u32[]{:S(2)}, u32[]{:S(2)}) collective-permute-start(f32[3,256]{1,0:T(4,128)S(1)} %get-tuple-element.41), channel_id=1, source_target_pairs={{0,4},{1,5},{2,6},{3,7},{4,0},{5,1},{6,2},{7,3},{8,12},{9,13},{10,... | collective-permute-start | bytes 9224 | tf_op jit(solution)/shard_map/ppermute | solution.py:19
  19.2 2.4 %collective-permute-start.5 = (f32[3,256]{1,0:T(4,128)S(1)}, f32[3,256]{1,0:T(4,128)S(1)}, u32[]{:S(2)}, u32[]{:S(2)}) collective-permute-start(f32[3,256]{1,0:T(4,128)S(1)} %get-tuple-element.42), channel_id=1, source_target_pairs={{0,7},{1,0},{2,1},{3,2},{4,3},{5,4},{6,5},{7,6},{8,15},{9,8},{10,9... | collective-permute-start | bytes 9224 | tf_op jit(solution)/shard_map/ppermute | solution.py:19
  21.5 0.0 copy-done.2
  21.5 0.0 copy-done.1
  21.5 0.0 copy-done
  21.5 0.0 copy-done.5
  21.5 0.0 copy-start.4
  21.6 0.3 %shard_map.122 = (f32[16,256]{1,0:T(8,128)S(1)}, f32[8,96,128]{2,1,0:T(8,128)S(1)}, f32[96,384]{1,0:T(8,128)S(1)}, bf16[384,768]{1,0:T(8,128)(2,1)S(1)}, f32[96,...) custom-call(f32[48,256]{1,0:T(8,128)S(1)} %get-tuple-element.38.base, s32[1,96]{1,0:T(1,128)S(1)} %copy-done.5, ...), custom_call_target="tpu_custom_call" | custom-call | tf_op jit(solution)/shard_map/pallas_call | solution.py:616
  21.9 0.0 copy-start.3
  21.9 0.0 collective-permute-done.3.after_x
  21.9 0.0 collective-permute-done.4.after_y
  21.9 0.9 %collective-permute-done.5.after_z = f32[3,256]{1,0:T(4,128)S(1)} collective-permute-done((f32[3,256]{1,0:T(4,128)S(1)}, f32[3,256]{1,0:T(4,128)S(1)}, u32[]{:S(2)}, u32[]{:S(2)}) %collective-permute-start.5) | collective-permute-done | bytes 3104 | tf_op jit(solution)/shard_map/ppermute | solution.py:19
  22.9 0.0 all-to-all-done.received
  22.9 0.0 copy-done.4
  22.9 0.0 copy-done.3
  22.9 1.1 %shard_map.124 = (f32[9,1,256]{2,1,0:T(1,128)}, f32[9,1,256]{2,1,0:T(1,128)}, f32[1,3,16,256]{3,2,1,0:T(8,128)}, f32[1,16,256]{2,1,0:T(8,128)}) custom-call(f32[32,8,128]{2,1,0:T(8,128)S(1)} %all-to-all-done.received, f32[48,256]{1,0:T(8,128)S(1)} %get-tuple-element.38.base, f32[16,256]{1,0:T(8,128)S(1)} %get-tuple-element.39.ends, ...), custom_call_target="tpu_custom_call" | custom-call | tf_op jit(solution)/shard_map/pallas_call | solution.py:616
Async XLA Ops:
  0.6 7.8 %collective-permute-start = (f32[1,3,3,256]{3,0,2,1:T(1,128)}, f32[1,3,3,256]{3,0,2,1:T(1,128)S(1)}, u32[]{:S(2)}, u32[]{:S(2)}) collective-permute-start(f32[1,3,3,256]{3,0,2,1:T(1,128)} %param.10), channel_id=1, source_target_pairs={{0,8},{8,16},{16,24},{24,0},{1,9},{9,17},{17,25},{25,1},{2,10},{10... | collective-permute-start | bytes 27656 | tf_op jit(solution)/shard_map/ppermute | solution.py:19
  1.1 7.5 %collective-permute-start.2 = (f32[1,3,3,256]{3,0,2,1:T(1,128)}, f32[1,3,3,256]{3,0,2,1:T(1,128)S(1)}, u32[]{:S(2)}, u32[]{:S(2)}) collective-permute-start(f32[1,3,3,256]{3,0,2,1:T(1,128)} %param.10), channel_id=1, source_target_pairs={{0,1},{1,2},{2,3},{3,4},{4,5},{5,6},{6,7},{7,0},{8,9},{9,10},{10,1... | collective-permute-start | bytes 27656 | tf_op jit(solution)/shard_map/ppermute | solution.py:19
  3.7 4.9 %collective-permute-start.1 = (f32[1,3,3,256]{3,0,2,1:T(1,128)}, f32[1,3,3,256]{3,0,2,1:T(1,128)S(1)}, u32[]{:S(2)}, u32[]{:S(2)}) collective-permute-start(f32[1,3,3,256]{3,0,2,1:T(1,128)} %param.10), channel_id=1, source_target_pairs={{0,4},{1,5},{2,6},{3,7},{4,0},{5,1},{6,2},{7,3},{8,12},{9,13},{10,... | collective-permute-start | bytes 27656 | tf_op jit(solution)/shard_map/ppermute | solution.py:19
  6.3 15.2 %copy-start.2 = (f32[1,96,384]{2,1,0:T(8,128)S(1)}, f32[1,96,384]{2,1,0:T(8,128)}, u32[]{:S(2)}) copy-start(f32[1,96,384]{2,1,0:T(8,128)} %coarse_map.1) | copy-start | bytes 442372
  8.4 13.1 %copy-start.1 = (f32[384,384]{1,0:T(8,128)S(1)}, f32[384,384]{1,0:T(8,128)}, u32[]{:S(2)}) copy-start(f32[384,384]{1,0:T(8,128)} %global_inverse.1) | copy-start | bytes 1769476
  10.3 11.2 %copy-start = (f32[1,96,768]{2,1,0:T(8,128)S(1)}, f32[1,96,768]{2,1,0:T(8,128)}, u32[]{:S(2)}) copy-start(f32[1,96,768]{2,1,0:T(8,128)} %region_inverse.1) | copy-start | bytes 884740
  10.3 12.5 %all-to-all-start = ((f32[32,8,128]{2,1,0:T(8,128)}), f32[32,8,128]{2,1,0:T(8,128)S(1)}, u32[]{:S(2)}, u32[]{:S(2)}) async-start(f32[32,8,128]{2,1,0:T(8,128)} %get-tuple-element.37), calls=%async_computation | async-start | bytes 262144 | tf_op jit(solution)/shard_map/all_to_all | solution.py:656
  15.2 6.7 %collective-permute-start.3 = (f32[3,256]{1,0:T(4,128)S(1)}, f32[3,256]{1,0:T(4,128)S(1)}, u32[]{:S(2)}, u32[]{:S(2)}) collective-permute-start(f32[3,256]{1,0:T(4,128)S(1)} %get-tuple-element.40), channel_id=1, source_target_pairs={{0,24},{8,0},{16,8},{24,16},{1,25},{9,1},{17,9},{25,17},{2,26},{10... | collective-permute-start | bytes 9224 | tf_op jit(solution)/shard_map/ppermute | solution.py:19
  16.8 4.7 %copy-start.5 = (s32[1,96]{1,0:T(1,128)S(1)}, s32[1,96]{1,0:T(1,128)}, u32[]{:S(2)}) copy-start(s32[1,96]{1,0:T(1,128)} %primal_index.1) | copy-start | bytes 1156
  16.8 5.1 %collective-permute-start.4 = (f32[3,256]{1,0:T(4,128)S(1)}, f32[3,256]{1,0:T(4,128)S(1)}, u32[]{:S(2)}, u32[]{:S(2)}) collective-permute-start(f32[3,256]{1,0:T(4,128)S(1)} %get-tuple-element.41), channel_id=1, source_target_pairs={{0,4},{1,5},{2,6},{3,7},{4,0},{5,1},{6,2},{7,3},{8,12},{9,13},{10,... | collective-permute-start | bytes 9224 | tf_op jit(solution)/shard_map/ppermute | solution.py:19
  19.2 3.7 %collective-permute-start.5 = (f32[3,256]{1,0:T(4,128)S(1)}, f32[3,256]{1,0:T(4,128)S(1)}, u32[]{:S(2)}, u32[]{:S(2)}) collective-permute-start(f32[3,256]{1,0:T(4,128)S(1)} %get-tuple-element.42), channel_id=1, source_target_pairs={{0,7},{1,0},{2,1},{3,2},{4,3},{5,4},{6,5},{7,6},{8,15},{9,8},{10,9... | collective-permute-start | bytes 9224 | tf_op jit(solution)/shard_map/ppermute | solution.py:19
  21.5 1.3 %copy-start.4 = (f32[1,3,3,256]{3,0,2,1:T(1,128)S(1)}, f32[1,3,3,256]{3,0,2,1:T(1,128)}, u32[]{:S(2)}) copy-start(f32[1,3,3,256]{3,0,2,1:T(1,128)} %param.9) | copy-start | bytes 27652
  21.9 1.0 %copy-start.3 = (f32[1,16,256]{2,1,0:T(8,128)S(1)}, f32[1,16,256]{2,1,0:T(8,128)}, u32[]{:S(2)}) copy-start(f32[1,16,256]{2,1,0:T(8,128)} %viscosity.1) | copy-start | bytes 49156

commit v7 on v6

--- a/solution.py
+++ b/solution.py
@@ -483,19 +483,35 @@
     region_out,
     through_out,
     global_out,
-    spots_out,
-    choose_out,
+    field_map_out,
+    face_map_out,
+    ahead_map_out,
 ):
     face = cells * cells
     ends_out[...] = jnp.concatenate(fold(base[...], cells, True) + [jnp.zeros((7, face), jnp.float32)], axis=0)
     count = primal_index.shape[1]
     group, _, place, _ = decode(primal_index[...], cells)
-    choose_out[...] = jnp.concatenate(
+    choose = jnp.concatenate(
         [one_hot(iota((3 * cells, count), 0) == place), one_hot(iota((16, count), 0) == group)], axis=0
     )
     _, spot, _, lane = decode(column_of(primal_index[...]), cells)
     at = iota((count, face), 1)
-    spots_out[...] = jnp.concatenate([jnp.where(at == lane, 1.0, 0.0), jnp.where(at == spot, 1.0, 0.0)], axis=1)
+    number = iota((count, 2 * face), 0) + 1
+    spots = jnp.where(jnp.concatenate([at == lane, at == spot], axis=1), number, 0).astype(jnp.float32)
+    maps = choice_times(choose, spots).astype(jnp.int32)
+    maps = jnp.where(maps > 0, maps - 1, LANES - 1)
+    field_map = maps[: 3 * cells, :face]
+    field_map_out[...] = field_map
+    face_map_out[...] = maps[3 * cells :, face:]
+    _, where_y, where_z = positions(cells, cells)
+    end = cells - 1
+    ahead_map_out[...] = jnp.concatenate(
+        [
+            jnp.where(where_y == end, LANES - 1, shift(field_map[cells : 2 * cells], -cells, 1)),
+            jnp.where(where_z == end, LANES - 1, shift(field_map[2 * cells :], -1, 1)),
+        ],
+        axis=0,
+    )
     blank = jnp.zeros((count, LANES - count), jnp.float32)
     for q in range(region_out.shape[0]):
         region_out[q] = jnp.concatenate([region_inverse[0, :, q * count : (q + 1) * count], blank], axis=1)
@@ -514,8 +530,9 @@
     after_x,
     after_y,
     after_z,
-    spots,
-    choose,
+    field_map,
+    face_map,
+    ahead_map,
     region_blocks,
     through,
     global_parts,
@@ -535,28 +552,42 @@
     me_region = lax.axis_index("region")
     everything = jnp.sum(received[...], axis=0)
     totals = [everything[half + 1 + i : half + 2 + i] for i in range(columns // LANES)]
-    total = jnp.concatenate(totals, axis=1)
+    after = [after_x[...], after_y[...], after_z[...]]
+    field = base[...]
+    field_x, field_y, field_z = [field[c * cells : (c + 1) * cells] for c in range(3)]
+    where_x, where_y, where_z = positions(cells, cells)
+    end = cells - 1
+    step = jnp.where(where_x == end, jnp.broadcast_to(after[0][0:1], (cells, face)), shift(field_x, -1, 0)) - field_x
+    step = step + jnp.where(where_y == end, 0.0, shift(field_y, -cells, 1)) - field_y
+    step = step + jnp.where(where_z == end, 0.0, shift(field_z, -1, 1)) - field_z
+    step = step + unfold(after[1][1:2], after[2][2:3], cells, True)
+    jump = ends[:9] - jnp.concatenate(after, axis=0)
     added = jnp.zeros((count, LANES), jnp.float32)
     for i, part in enumerate(totals):
         added = added + through[:, i * LANES : (i + 1) * LANES] * part
     for q in range(n_sub):
         added = added + region_blocks[q] * received[me_region * n_sub + q, half : half + 1, :]
     lifted = jnp.sum(added, axis=1, keepdims=True)
-    added = choice_times(choose[...], lifted * spots[...])
-    velocity = base[...] + added[: 3 * cells, :face]
-    upper_faces = ends[:9] + added[3 * cells : 3 * cells + 9, face:]
+    own_lane = iota((count, LANES), 0) == iota((count, LANES), 1)
+    lifted = jnp.sum(jnp.where(own_lane, lifted, 0.0), axis=0, keepdims=True)
+
+    def placed(numbers):
+        wide = jnp.broadcast_to(lifted, (numbers.shape[0], LANES))
+        return jnp.concatenate(
+            [lane_gather(wide, numbers[:, i * LANES : (i + 1) * LANES]) for i in range(face // LANES)], axis=1
+        )
+
+    added = placed(field_map)
+    ahead = placed(ahead_map)
+    velocity = field + added
     for c in range(3):
         velocity_out[0, c] = velocity[c * cells : (c + 1) * cells]
-    after = [after_x[...], after_y[...], after_z[...]]
-    ahead = unfold(after[1][1:2], after[2][2:3], cells, True)
-    where_x, where_y, where_z = positions(cells, cells)
-    end = cells - 1
-    field_x, field_y, field_z = [velocity[c * cells : (c + 1) * cells] for c in range(3)]
-    step_x = jnp.where(where_x == end, jnp.broadcast_to(after[0][0:1], (cells, face)), shift(field_x, -1, 0))
-    step_y = jnp.where(where_y == end, 0.0, shift(field_y, -cells, 1))
-    step_z = jnp.where(where_z == end, 0.0, shift(field_z, -1, 1))
-    step = (step_x - field_x) + (step_y - field_y) + (step_z - field_z) + ahead
+    added_x = added[:cells]
+    step = step + jnp.where(where_x == end, 0.0, shift(added_x, -1, 0)) - added_x
+    step = step + ahead[:cells] - added[cells : 2 * cells] + ahead[cells:] - added[2 * cells :]
     pressure_out[0] = -viscosity[0] * step
+    jump = jump + placed(face_map)[:9]
+    total = jnp.concatenate(totals, axis=1)
     piece = total.astype(jnp.bfloat16).astype(jnp.float32)
     row = iota((16, columns), 0)
     parts = jnp.where(row == 0, piece, jnp.where(row == 1, total - piece, 0.0)).astype(jnp.bfloat16)
@@ -576,11 +607,9 @@
     curvature = jnp.sum(curvature, axis=1, keepdims=True)
     squares = jnp.sum(jnp.where(lane == count + 1, own_line, 0.0), axis=1, keepdims=True)
     alpha = squares / curvature
-    for d in range(3):
-        jump = upper_faces[3 * d : 3 * d + 3] - after[d]
-        for c in range(3):
-            residual_out[3 * d + c] = residual[3 * d + c] - alpha * jump[c : c + 1]
-            multipliers_out[3 * d + c] = multipliers[3 * d + c] + alpha * direction[3 * d + c]
+    for i in range(9):
+        residual_out[i] = residual[i] - alpha * jump[i : i + 1]
+        multipliers_out[i] = multipliers[i] + alpha * direction[i]
 
 
 def body(
@@ -660,15 +689,16 @@
     after_x = shifted_2(lower_x, "region", -1)
     after_y = shifted_2(lower_y, "sub", -DOM_Z)
     after_z = shifted_2(lower_z, "sub", -1)
-    ends, region_blocks, through, global_parts, spots, choose = call(
+    ends, region_blocks, through, global_parts, field_map, face_map, ahead_map = call(
         functools.partial(between_kernel, cells),
         [
             like((16, face)),
             like((n_sub, count, LANES)),
             like((count, columns)),
             like((columns, 2 * columns), bf16),
-            like((count, 2 * face)),
-            like((rows + 16, count), bf16),
+            like((rows, face), jnp.int32),
+            like((16, face), jnp.int32),
+            like((2 * cells, face), jnp.int32),
         ],
         [base, primal_index, region_inverse, coarse_map, global_inverse],
     )
@@ -682,8 +712,9 @@
             after_x,
             after_y,
             after_z,
-            spots,
-            choose,
+            field_map,
+            face_map,
+            ahead_map,
             region_blocks,
             through,
             global_parts,

time: 24.2 us -> 24 us (level)
  transfers between devices with their start and end apart: 7 -> 7, of which waited for: 2 -> 2; matrix products, arithmetic and copies ran while one was open for 0% -> 0% of each run, Pallas kernels for 11% -> 12%
where the time goes in v7:
time: 24 us; the launch traced here: 23.8 us
  starting transfers between devices  16.8 us (70%)
  Pallas kernels  5.45 us (23%)
  waiting for transfers between devices  0.85 us (4%)
  between operations  0.74 us (3%)
    ppermute x6, starting transfers between devices, shifted_2(): return lax.ppermute(x, axis, [(i, (i + by) % count) for i in range(count)])  12 us
    pallas_call x5, Pallas kernels, call(): pl.pallas_call(kernel, out_shape=out_shape, in_specs=[vmem] * len(operand...  5.45 us
    all_to_all x1, starting transfers between devices, body(): received = lax.all_to_all(sent, ('region', 'sub'), 0, 0, tiled=True)  4.78 us
    ppermute x6, waiting for transfers between devices, shifted_2(): return lax.ppermute(x, axis, [(i, (i + by) % count) for i in range(count)])  0.85 us
  transfers between devices with their start and end apart: 7, of which 2 were waited for; matrix products, arithmetic and copies ran while one was open for 0% of the time, Pallas kernels for 12%

profile of v7, /device:TPU:0, one launch (start us, length us, event | category | flops | bytes accessed | tf_op | source)
XLA Modules:
  0.0 23.8 jit_solution(12128482850367472236)
XLA Ops:
  0.6 0.5 %collective-permute-start = (f32[1,3,3,256]{3,0,2,1:T(1,128)}, f32[1,3,3,256]{3,0,2,1:T(1,128)S(1)}, u32[]{:S(2)}, u32[]{:S(2)}) collective-permute-start(f32[1,3,3,256]{3,0,2,1:T(1,128)} %param.10), channel_id=1, source_target_pairs={{0,8},{8,16},{16,24},{24,0},{1,9},{9,17},{17,25},{25,1},{2,10},{10... | collective-permute-start | bytes 27656 | tf_op jit(solution)/shard_map/ppermute | solution.py:19
  1.1 2.6 %collective-permute-start.2 = (f32[1,3,3,256]{3,0,2,1:T(1,128)}, f32[1,3,3,256]{3,0,2,1:T(1,128)S(1)}, u32[]{:S(2)}, u32[]{:S(2)}) collective-permute-start(f32[1,3,3,256]{3,0,2,1:T(1,128)} %param.10), channel_id=1, source_target_pairs={{0,1},{1,2},{2,3},{3,4},{4,5},{5,6},{6,7},{7,0},{8,9},{9,10},{10,1... | collective-permute-start | bytes 27656 | tf_op jit(solution)/shard_map/ppermute | solution.py:19
  3.7 2.6 %collective-permute-start.1 = (f32[1,3,3,256]{3,0,2,1:T(1,128)}, f32[1,3,3,256]{3,0,2,1:T(1,128)S(1)}, u32[]{:S(2)}, u32[]{:S(2)}) collective-permute-start(f32[1,3,3,256]{3,0,2,1:T(1,128)} %param.10), channel_id=1, source_target_pairs={{0,4},{1,5},{2,6},{3,7},{4,0},{5,1},{6,2},{7,3},{8,12},{9,13},{10,... | collective-permute-start | bytes 27656 | tf_op jit(solution)/shard_map/ppermute | solution.py:19
  6.3 0.0 copy-start.2
  6.3 2.1 %shard_map.120 = (f32[9,1,256]{2,1,0:T(1,128)S(1)}, f32[9,1,256]{2,1,0:T(1,128)S(1)}, f32[48,256]{1,0:T(8,128)S(1)}, f32[8,128]{1,0:T(8,128)S(1)}, f32[2,16,256]...) custom-call(f32[9,1,256]{2,1,0:T(1,128)} %bitcast.13, ...), custom_call_target="tpu_custom_call" | custom-call | tf_op jit(solution)/shard_map/pallas_call | solution.py:645
  8.4 0.0 copy-start.1
  8.5 0.0 collective-permute-done
  8.5 0.1 collective-permute-done.2
  8.6 0.0 collective-permute-done.1
  8.6 1.7 %shard_map.121 = (f32[48,256]{1,0:T(8,128)S(1)}, f32[32,8,128]{2,1,0:T(8,128)}) custom-call(f32[48,256]{1,0:T(8,128)S(1)} %get-tuple-element.30.source_own, f32[9,1,256]{2,1,0:T(1,128)S(1)} %bitcast.9, f32[9,1,256]{2,1,0:T(1,128)S(1)} %bitcast.11, f32[9,1,256]{2,1,0:T(1,128)S(1)} %bitcast.10, f32[2,16,256]{2,1,0:T(8,128)S(1)} %get-tuple-element.31.inverses, ...), custom_call_target="tpu_custom_call" | custom-call | tf_op jit(solution)/shard_map/pallas_call | solution.py:645
  10.3 0.0 copy-start
  10.3 4.8 %all-to-all-start = ((f32[32,8,128]{2,1,0:T(8,128)}), f32[32,8,128]{2,1,0:T(8,128)S(1)}, u32[]{:S(2)}, u32[]{:S(2)}) async-start(f32[32,8,128]{2,1,0:T(8,128)} %get-tuple-element.38), calls=%async_computation | async-start | bytes 262144 | tf_op jit(solution)/shard_map/all_to_all | solution.py:685
  15.1 0.1 shard_map.123
  15.2 1.6 %collective-permute-start.3 = (f32[3,256]{1,0:T(4,128)S(1)}, f32[3,256]{1,0:T(4,128)S(1)}, u32[]{:S(2)}, u32[]{:S(2)}) collective-permute-start(f32[3,256]{1,0:T(4,128)S(1)} %get-tuple-element.41), channel_id=1, source_target_pairs={{0,24},{8,0},{16,8},{24,16},{1,25},{9,1},{17,9},{25,17},{2,26},{10... | collective-permute-start | bytes 9224 | tf_op jit(solution)/shard_map/ppermute | solution.py:19
  16.8 0.0 copy-start.5
  16.8 2.4 %collective-permute-start.4 = (f32[3,256]{1,0:T(4,128)S(1)}, f32[3,256]{1,0:T(4,128)S(1)}, u32[]{:S(2)}, u32[]{:S(2)}) collective-permute-start(f32[3,256]{1,0:T(4,128)S(1)} %get-tuple-element.42), channel_id=1, source_target_pairs={{0,4},{1,5},{2,6},{3,7},{4,0},{5,1},{6,2},{7,3},{8,12},{9,13},{10,... | collective-permute-start | bytes 9224 | tf_op jit(solution)/shard_map/ppermute | solution.py:19
  19.2 2.4 %collective-permute-start.5 = (f32[3,256]{1,0:T(4,128)S(1)}, f32[3,256]{1,0:T(4,128)S(1)}, u32[]{:S(2)}, u32[]{:S(2)}) collective-permute-start(f32[3,256]{1,0:T(4,128)S(1)} %get-tuple-element.43), channel_id=1, source_target_pairs={{0,7},{1,0},{2,1},{3,2},{4,3},{5,4},{6,5},{7,6},{8,15},{9,8},{10,9... | collective-permute-start | bytes 9224 | tf_op jit(solution)/shard_map/ppermute | solution.py:19
  21.5 0.0 copy-done.2
  21.5 0.0 copy-done.1
  21.5 0.0 copy-done
  21.5 0.0 copy-done.5
  21.5 0.0 copy-start.4
  21.6 0.6 %shard_map.122 = (f32[16,256]{1,0:T(8,128)S(1)}, f32[8,96,128]{2,1,0:T(8,128)S(1)}, f32[96,384]{1,0:T(8,128)S(1)}, bf16[384,768]{1,0:T(8,128)(2,1)S(1)}, s32[48,...) custom-call(f32[48,256]{1,0:T(8,128)S(1)} %get-tuple-element.39.base, s32[1,96]{1,0:T(1,128)S(1)} %copy-done.5, ...), custom_call_target="tpu_custom_call" | custom-call | tf_op jit(solution)/shard_map/pallas_call | solution.py:645
  22.1 0.0 copy-start.3
  22.1 0.0 collective-permute-done.3.after_x
  22.1 0.0 collective-permute-done.4.after_y
  22.2 0.7 %collective-permute-done.5.after_z = f32[3,256]{1,0:T(4,128)S(1)} collective-permute-done((f32[3,256]{1,0:T(4,128)S(1)}, f32[3,256]{1,0:T(4,128)S(1)}, u32[]{:S(2)}, u32[]{:S(2)}) %collective-permute-start.5) | collective-permute-done | bytes 3104 | tf_op jit(solution)/shard_map/ppermute | solution.py:19
  22.9 0.0 all-to-all-done.received
  22.9 0.0 copy-done.4
  22.9 0.0 copy-done.3
  22.9 1.0 %shard_map.124 = (f32[9,1,256]{2,1,0:T(1,128)}, f32[9,1,256]{2,1,0:T(1,128)}, f32[1,3,16,256]{3,2,1,0:T(8,128)}, f32[1,16,256]{2,1,0:T(8,128)}) custom-call(f32[32,8,128]{2,1,0:T(8,128)S(1)} %all-to-all-done.received, f32[48,256]{1,0:T(8,128)S(1)} %get-tuple-element.39.base, f32[16,256]{1,0:T(8,128)S(1)} %get-tuple-element.40.ends, ...), custom_call_target="tpu_custom_call" | custom-call | tf_op jit(solution)/shard_map/pallas_call | solution.py:645
Async XLA Ops:
  0.6 7.8 %collective-permute-start = (f32[1,3,3,256]{3,0,2,1:T(1,128)}, f32[1,3,3,256]{3,0,2,1:T(1,128)S(1)}, u32[]{:S(2)}, u32[]{:S(2)}) collective-permute-start(f32[1,3,3,256]{3,0,2,1:T(1,128)} %param.10), channel_id=1, source_target_pairs={{0,8},{8,16},{16,24},{24,0},{1,9},{9,17},{17,25},{25,1},{2,10},{10... | collective-permute-start | bytes 27656 | tf_op jit(solution)/shard_map/ppermute | solution.py:19
  1.1 7.5 %collective-permute-start.2 = (f32[1,3,3,256]{3,0,2,1:T(1,128)}, f32[1,3,3,256]{3,0,2,1:T(1,128)S(1)}, u32[]{:S(2)}, u32[]{:S(2)}) collective-permute-start(f32[1,3,3,256]{3,0,2,1:T(1,128)} %param.10), channel_id=1, source_target_pairs={{0,1},{1,2},{2,3},{3,4},{4,5},{5,6},{6,7},{7,0},{8,9},{9,10},{10,1... | collective-permute-start | bytes 27656 | tf_op jit(solution)/shard_map/ppermute | solution.py:19
  3.7 4.9 %collective-permute-start.1 = (f32[1,3,3,256]{3,0,2,1:T(1,128)}, f32[1,3,3,256]{3,0,2,1:T(1,128)S(1)}, u32[]{:S(2)}, u32[]{:S(2)}) collective-permute-start(f32[1,3,3,256]{3,0,2,1:T(1,128)} %param.10), channel_id=1, source_target_pairs={{0,4},{1,5},{2,6},{3,7},{4,0},{5,1},{6,2},{7,3},{8,12},{9,13},{10,... | collective-permute-start | bytes 27656 | tf_op jit(solution)/shard_map/ppermute | solution.py:19
  6.3 15.2 %copy-start.2 = (f32[1,96,384]{2,1,0:T(8,128)S(1)}, f32[1,96,384]{2,1,0:T(8,128)}, u32[]{:S(2)}) copy-start(f32[1,96,384]{2,1,0:T(8,128)} %coarse_map.1) | copy-start | bytes 442372
  8.4 13.1 %copy-start.1 = (f32[384,384]{1,0:T(8,128)S(1)}, f32[384,384]{1,0:T(8,128)}, u32[]{:S(2)}) copy-start(f32[384,384]{1,0:T(8,128)} %global_inverse.1) | copy-start | bytes 1769476
  10.3 11.2 %copy-start = (f32[1,96,768]{2,1,0:T(8,128)S(1)}, f32[1,96,768]{2,1,0:T(8,128)}, u32[]{:S(2)}) copy-start(f32[1,96,768]{2,1,0:T(8,128)} %region_inverse.1) | copy-start | bytes 884740
  10.3 12.5 %all-to-all-start = ((f32[32,8,128]{2,1,0:T(8,128)}), f32[32,8,128]{2,1,0:T(8,128)S(1)}, u32[]{:S(2)}, u32[]{:S(2)}) async-start(f32[32,8,128]{2,1,0:T(8,128)} %get-tuple-element.38), calls=%async_computation | async-start | bytes 262144 | tf_op jit(solution)/shard_map/all_to_all | solution.py:685
  15.2 6.9 %collective-permute-start.3 = (f32[3,256]{1,0:T(4,128)S(1)}, f32[3,256]{1,0:T(4,128)S(1)}, u32[]{:S(2)}, u32[]{:S(2)}) collective-permute-start(f32[3,256]{1,0:T(4,128)S(1)} %get-tuple-element.41), channel_id=1, source_target_pairs={{0,24},{8,0},{16,8},{24,16},{1,25},{9,1},{17,9},{25,17},{2,26},{10... | collective-permute-start | bytes 9224 | tf_op jit(solution)/shard_map/ppermute | solution.py:19
  16.8 4.7 %copy-start.5 = (s32[1,96]{1,0:T(1,128)S(1)}, s32[1,96]{1,0:T(1,128)}, u32[]{:S(2)}) copy-start(s32[1,96]{1,0:T(1,128)} %primal_index.1) | copy-start | bytes 1156
  16.8 5.4 %collective-permute-start.4 = (f32[3,256]{1,0:T(4,128)S(1)}, f32[3,256]{1,0:T(4,128)S(1)}, u32[]{:S(2)}, u32[]{:S(2)}) collective-permute-start(f32[3,256]{1,0:T(4,128)S(1)} %get-tuple-element.42), channel_id=1, source_target_pairs={{0,4},{1,5},{2,6},{3,7},{4,0},{5,1},{6,2},{7,3},{8,12},{9,13},{10,... | collective-permute-start | bytes 9224 | tf_op jit(solution)/shard_map/ppermute | solution.py:19
  19.2 3.7 %collective-permute-start.5 = (f32[3,256]{1,0:T(4,128)S(1)}, f32[3,256]{1,0:T(4,128)S(1)}, u32[]{:S(2)}, u32[]{:S(2)}) collective-permute-start(f32[3,256]{1,0:T(4,128)S(1)} %get-tuple-element.43), channel_id=1, source_target_pairs={{0,7},{1,0},{2,1},{3,2},{4,3},{5,4},{6,5},{7,6},{8,15},{9,8},{10,9... | collective-permute-start | bytes 9224 | tf_op jit(solution)/shard_map/ppermute | solution.py:19
  21.5 1.3 %copy-start.4 = (f32[1,3,3,256]{3,0,2,1:T(1,128)S(1)}, f32[1,3,3,256]{3,0,2,1:T(1,128)}, u32[]{:S(2)}) copy-start(f32[1,3,3,256]{3,0,2,1:T(1,128)} %param.9) | copy-start | bytes 27652
  22.1 0.7 %copy-start.3 = (f32[1,16,256]{2,1,0:T(8,128)S(1)}, f32[1,16,256]{2,1,0:T(8,128)}, u32[]{:S(2)}) copy-start(f32[1,16,256]{2,1,0:T(8,128)} %viscosity.1) | copy-start | bytes 49156

commit v8 on v7

--- a/solution.py
+++ b/solution.py
@@ -45,6 +45,21 @@
     width = both.shape[1] // 2
     y = jnp.dot(jnp.concatenate(parts_of(x, 2), axis=0), both, preferred_element_type=jnp.float32)
     return y[:rows, :width] + (y[rows:, :width] + y[:rows, width:])
+
+
+def stacked_parts(w):
+    first, second = parts_of(w, 2)
+    return jnp.concatenate([first, first, second, jnp.zeros_like(first)], axis=0)
+
+
+def times_stacked(x, stacked):
+    first, second = parts_of(x, 2)
+    left = iota(x.shape, 1) < x.shape[1] // 2
+    zero = jnp.zeros_like(x)
+    pair = jnp.where(left, first.astype(jnp.float32), second.astype(jnp.float32))
+    other = jnp.where(left, first.astype(jnp.float32), zero)
+    pair = jnp.concatenate([pair, other], axis=1).astype(jnp.bfloat16)
+    return jnp.dot(pair, stacked, preferred_element_type=jnp.float32)
 
 
 def both_parts(w):
@@ -312,13 +327,13 @@
     gather_out[...] = jnp.concatenate([gather, gather_near], axis=0)
     quarter_gather = gather_matrix(cells, 2)[0]
     coarsen, coarsen_near = block_matrices(half, False)
-    coarsen_out[...] = jnp.concatenate([coarsen, coarsen_near], axis=0)
+    coarsen_out[...] = jnp.concatenate([jnp.concatenate([x, x], axis=1) for x in (coarsen, coarsen_near)], axis=0)
     refine = jnp.concatenate(block_matrices(half, True), axis=1)
     for copy in copies[:3]:
         copy.wait()
     react = reaction[0]
     scale = damping / (plane_restrict(react, quarter_gather, cells, 1, 2) + 6.0 * 0.0625)
-    quarter_out[...] = 0.125 * scale
+    quarter_out[...] = 0.125 * jnp.concatenate([scale, scale], axis=1)
     power, one = sweep_power(scale, half // 2, 0.0625)
     second_power = square(power)
     diagonal = react + 6.0
@@ -339,7 +354,7 @@
     for copy in copies[3:]:
         copy.wait()
     refined = times_choice(powers_sum(one + power, second_power), refine)
-    sweeps_out[...] = both_parts(
+    sweeps_out[...] = stacked_parts(
         (1.0 - damping) * refined[:, : half**3] + 0.25 * half_scale * refined[:, half**3 :]
     )
     row_x = iota((cells, face), 0)
@@ -437,7 +452,7 @@
         swept = half_scale * right
         remain = times_choice(jnp.concatenate([(1.0 - damping) * right, 0.25 * swept], axis=1), coarsen[...])
         local = (2.0 - damping) * swept + 0.25 * half_scale * half_beside(swept)
-        return local + times_parts(remain * quarter[...], sweeps[...])
+        return local + times_stacked(remain * quarter[...], sweeps[...])
 
     def correct(residual):
         swept = inverse * residual
@@ -452,8 +467,11 @@
 
     field, residual = correct(source)
     swept = inverse * residual
-    then = (1.0 - damping) * residual + beside(swept)
-    energy = jnp.sum((source + residual) * field + swept * (residual + then), axis=0, keepdims=True)
+    ahead = jnp.where(where_x < last, shift(swept, -1, 0), 0.0)
+    ahead = ahead + jnp.where(where_y < last, shift(swept, -cells, 1), 0.0)
+    ahead = ahead + jnp.where(where_z < last, shift(swept, -1, 1), 0.0)
+    energy = (source + residual) * field + swept * (2.0 * residual - diagonal * swept + 2.0 * ahead)
+    energy = jnp.sum(energy, axis=0, keepdims=True)
     energy = functools.reduce(lambda a, b: a + b, [energy[:, i * LANES : (i + 1) * LANES] for i in range(face // LANES)])
     energy = jnp.sum(energy, axis=1, keepdims=True)
     message = front[...]
@@ -462,6 +480,7 @@
     for device in range(sizes[0] * sizes[1]):
         buffer[device] = message
     (copy,) = load([(buffer, send_out)], semaphores)
+    then = (1.0 - damping) * residual + beside(swept)
     field = field + swept
     more, residual = correct(then)
     base_out[...] = field + more + inverse * residual
@@ -666,10 +685,10 @@
             like((height, LANES)),
             like((2, cells, face)),
             like((1, half_cells)),
-            like((1, half_cells // 8)),
+            like((1, half_cells // 4)),
             like((2 * face, min(half_cells, LANES)), bf16),
-            like((2 * half_cells, half_cells // 8), bf16),
-            like((half_cells // 8, 2 * half_cells), bf16),
+            like((2 * half_cells, half_cells // 4), bf16),
+            like((half_cells // 2, half_cells), bf16),
         ],
         [],
         [direction, residual, reaction, primal_index, region_inverse, coarse_map],

time: 24 us -> 24 us (level)
  no operation moved by 1% of the time
where the time goes in v8:
time: 24 us; the launch traced here: 23.8 us
  starting transfers between devices  16.8 us (70%)
  Pallas kernels  5.41 us (23%)
  waiting for transfers between devices  0.85 us (4%)
  between operations  0.74 us (3%)
    ppermute x6, starting transfers between devices, shifted_2(): return lax.ppermute(x, axis, [(i, (i + by) % count) for i in range(count)])  12 us
    pallas_call x5, Pallas kernels, call(): pl.pallas_call(kernel, out_shape=out_shape, in_specs=[vmem] * len(operand...  5.41 us
    all_to_all x1, starting transfers between devices, body(): received = lax.all_to_all(sent, ('region', 'sub'), 0, 0, tiled=True)  4.78 us
    ppermute x6, waiting for transfers between devices, shifted_2(): return lax.ppermute(x, axis, [(i, (i + by) % count) for i in range(count)])  0.84 us
  transfers between devices with their start and end apart: 7, of which 2 were waited for; matrix products, arithmetic and copies ran while one was open for 0% of the time, Pallas kernels for 12%

profile of v8, /device:TPU:0, one launch (start us, length us, event | category | flops | bytes accessed | tf_op | source)
XLA Modules:
  0.0 23.8 jit_solution(12496492325529525350)
XLA Ops:
  0.6 0.5 %collective-permute-start = (f32[1,3,3,256]{3,0,2,1:T(1,128)}, f32[1,3,3,256]{3,0,2,1:T(1,128)S(1)}, u32[]{:S(2)}, u32[]{:S(2)}) collective-permute-start(f32[1,3,3,256]{3,0,2,1:T(1,128)} %param.10), channel_id=1, source_target_pairs={{0,8},{8,16},{16,24},{24,0},{1,9},{9,17},{17,25},{25,1},{2,10},{10... | collective-permute-start | bytes 27656 | tf_op jit(solution)/shard_map/ppermute | solution.py:19
  1.1 2.6 %collective-permute-start.2 = (f32[1,3,3,256]{3,0,2,1:T(1,128)}, f32[1,3,3,256]{3,0,2,1:T(1,128)S(1)}, u32[]{:S(2)}, u32[]{:S(2)}) collective-permute-start(f32[1,3,3,256]{3,0,2,1:T(1,128)} %param.10), channel_id=1, source_target_pairs={{0,1},{1,2},{2,3},{3,4},{4,5},{5,6},{6,7},{7,0},{8,9},{9,10},{10,1... | collective-permute-start | bytes 27656 | tf_op jit(solution)/shard_map/ppermute | solution.py:19
  3.7 2.6 %collective-permute-start.1 = (f32[1,3,3,256]{3,0,2,1:T(1,128)}, f32[1,3,3,256]{3,0,2,1:T(1,128)S(1)}, u32[]{:S(2)}, u32[]{:S(2)}) collective-permute-start(f32[1,3,3,256]{3,0,2,1:T(1,128)} %param.10), channel_id=1, source_target_pairs={{0,4},{1,5},{2,6},{3,7},{4,0},{5,1},{6,2},{7,3},{8,12},{9,13},{10,... | collective-permute-start | bytes 27656 | tf_op jit(solution)/shard_map/ppermute | solution.py:19
  6.3 2.1 %shard_map.120 = (f32[9,1,256]{2,1,0:T(1,128)S(1)}, f32[9,1,256]{2,1,0:T(1,128)S(1)}, f32[48,256]{1,0:T(8,128)S(1)}, f32[8,128]{1,0:T(8,128)S(1)}, f32[2,16,256]...) custom-call(f32[9,1,256]{2,1,0:T(1,128)} %bitcast.13, ...), custom_call_target="tpu_custom_call" | custom-call | tf_op jit(solution)/shard_map/pallas_call | solution.py:664
  8.4 0.0 copy-start.1
  8.5 0.0 collective-permute-done
  8.5 0.1 collective-permute-done.2
  8.6 0.0 collective-permute-done.1
  8.6 0.0 copy-start.2
  8.6 1.6 %shard_map.121 = (f32[48,256]{1,0:T(8,128)S(1)}, f32[32,8,128]{2,1,0:T(8,128)}) custom-call(f32[48,256]{1,0:T(8,128)S(1)} %get-tuple-element.30.source_own, f32[9,1,256]{2,1,0:T(1,128)S(1)} %bitcast.9, f32[9,1,256]{2,1,0:T(1,128)S(1)} %bitcast.11, f32[9,1,256]{2,1,0:T(1,128)S(1)} %bitcast.10, f32[2,16,256]{2,1,0:T(8,128)S(1)} %get-tuple-element.31.inverses, ...), custom_call_target="tpu_custom_call" | custom-call | tf_op jit(solution)/shard_map/pallas_call | solution.py:664
  10.3 0.0 copy-start
  10.3 4.8 %all-to-all-start = ((f32[32,8,128]{2,1,0:T(8,128)}), f32[32,8,128]{2,1,0:T(8,128)S(1)}, u32[]{:S(2)}, u32[]{:S(2)}) async-start(f32[32,8,128]{2,1,0:T(8,128)} %get-tuple-element.38), calls=%async_computation | async-start | bytes 262144 | tf_op jit(solution)/shard_map/all_to_all | solution.py:704
  15.1 0.1 shard_map.123
  15.2 1.6 %collective-permute-start.3 = (f32[3,256]{1,0:T(4,128)S(1)}, f32[3,256]{1,0:T(4,128)S(1)}, u32[]{:S(2)}, u32[]{:S(2)}) collective-permute-start(f32[3,256]{1,0:T(4,128)S(1)} %get-tuple-element.41), channel_id=1, source_target_pairs={{0,24},{8,0},{16,8},{24,16},{1,25},{9,1},{17,9},{25,17},{2,26},{10... | collective-permute-start | bytes 9224 | tf_op jit(solution)/shard_map/ppermute | solution.py:19
  16.7 0.0 copy-start.5
  16.7 2.4 %collective-permute-start.4 = (f32[3,256]{1,0:T(4,128)S(1)}, f32[3,256]{1,0:T(4,128)S(1)}, u32[]{:S(2)}, u32[]{:S(2)}) collective-permute-start(f32[3,256]{1,0:T(4,128)S(1)} %get-tuple-element.42), channel_id=1, source_target_pairs={{0,4},{1,5},{2,6},{3,7},{4,0},{5,1},{6,2},{7,3},{8,12},{9,13},{10,... | collective-permute-start | bytes 9224 | tf_op jit(solution)/shard_map/ppermute | solution.py:19
  19.1 2.4 %collective-permute-start.5 = (f32[3,256]{1,0:T(4,128)S(1)}, f32[3,256]{1,0:T(4,128)S(1)}, u32[]{:S(2)}, u32[]{:S(2)}) collective-permute-start(f32[3,256]{1,0:T(4,128)S(1)} %get-tuple-element.43), channel_id=1, source_target_pairs={{0,7},{1,0},{2,1},{3,2},{4,3},{5,4},{6,5},{7,6},{8,15},{9,8},{10,9... | collective-permute-start | bytes 9224 | tf_op jit(solution)/shard_map/ppermute | solution.py:19
  21.5 0.0 copy-done.1
  21.5 0.0 copy-done.2
  21.5 0.0 copy-done
  21.5 0.0 copy-done.5
  21.5 0.0 copy-start.4
  21.5 0.6 %shard_map.122 = (f32[16,256]{1,0:T(8,128)S(1)}, f32[8,96,128]{2,1,0:T(8,128)S(1)}, f32[96,384]{1,0:T(8,128)S(1)}, bf16[384,768]{1,0:T(8,128)(2,1)S(1)}, s32[48,...) custom-call(f32[48,256]{1,0:T(8,128)S(1)} %get-tuple-element.39.base, s32[1,96]{1,0:T(1,128)S(1)} %copy-done.5, ...), custom_call_target="tpu_custom_call" | custom-call | tf_op jit(solution)/shard_map/pallas_call | solution.py:664
  22.1 0.0 copy-start.3
  22.1 0.0 collective-permute-done.3.after_x
  22.1 0.0 collective-permute-done.4.after_y
  22.1 0.7 %collective-permute-done.5.after_z = f32[3,256]{1,0:T(4,128)S(1)} collective-permute-done((f32[3,256]{1,0:T(4,128)S(1)}, f32[3,256]{1,0:T(4,128)S(1)}, u32[]{:S(2)}, u32[]{:S(2)}) %collective-permute-start.5) | collective-permute-done | bytes 3104 | tf_op jit(solution)/shard_map/ppermute | solution.py:19
  22.8 0.0 all-to-all-done.received
  22.8 0.0 copy-done.4
  22.8 0.0 copy-done.3
  22.8 1.0 %shard_map.124 = (f32[9,1,256]{2,1,0:T(1,128)}, f32[9,1,256]{2,1,0:T(1,128)}, f32[1,3,16,256]{3,2,1,0:T(8,128)}, f32[1,16,256]{2,1,0:T(8,128)}) custom-call(f32[32,8,128]{2,1,0:T(8,128)S(1)} %all-to-all-done.received, f32[48,256]{1,0:T(8,128)S(1)} %get-tuple-element.39.base, f32[16,256]{1,0:T(8,128)S(1)} %get-tuple-element.40.ends, ...), custom_call_target="tpu_custom_call" | custom-call | tf_op jit(solution)/shard_map/pallas_call | solution.py:664
Async XLA Ops:
  0.6 7.8 %collective-permute-start = (f32[1,3,3,256]{3,0,2,1:T(1,128)}, f32[1,3,3,256]{3,0,2,1:T(1,128)S(1)}, u32[]{:S(2)}, u32[]{:S(2)}) collective-permute-start(f32[1,3,3,256]{3,0,2,1:T(1,128)} %param.10), channel_id=1, source_target_pairs={{0,8},{8,16},{16,24},{24,0},{1,9},{9,17},{17,25},{25,1},{2,10},{10... | collective-permute-start | bytes 27656 | tf_op jit(solution)/shard_map/ppermute | solution.py:19
  1.1 7.5 %collective-permute-start.2 = (f32[1,3,3,256]{3,0,2,1:T(1,128)}, f32[1,3,3,256]{3,0,2,1:T(1,128)S(1)}, u32[]{:S(2)}, u32[]{:S(2)}) collective-permute-start(f32[1,3,3,256]{3,0,2,1:T(1,128)} %param.10), channel_id=1, source_target_pairs={{0,1},{1,2},{2,3},{3,4},{4,5},{5,6},{6,7},{7,0},{8,9},{9,10},{10,1... | collective-permute-start | bytes 27656 | tf_op jit(solution)/shard_map/ppermute | solution.py:19
  3.7 4.9 %collective-permute-start.1 = (f32[1,3,3,256]{3,0,2,1:T(1,128)}, f32[1,3,3,256]{3,0,2,1:T(1,128)S(1)}, u32[]{:S(2)}, u32[]{:S(2)}) collective-permute-start(f32[1,3,3,256]{3,0,2,1:T(1,128)} %param.10), channel_id=1, source_target_pairs={{0,4},{1,5},{2,6},{3,7},{4,0},{5,1},{6,2},{7,3},{8,12},{9,13},{10,... | collective-permute-start | bytes 27656 | tf_op jit(solution)/shard_map/ppermute | solution.py:19
  8.4 13.0 %copy-start.1 = (f32[384,384]{1,0:T(8,128)S(1)}, f32[384,384]{1,0:T(8,128)}, u32[]{:S(2)}) copy-start(f32[384,384]{1,0:T(8,128)} %global_inverse.1) | copy-start | bytes 1769476
  8.6 12.9 %copy-start.2 = (f32[1,96,384]{2,1,0:T(8,128)S(1)}, f32[1,96,384]{2,1,0:T(8,128)}, u32[]{:S(2)}) copy-start(f32[1,96,384]{2,1,0:T(8,128)} %coarse_map.1) | copy-start | bytes 442372
  10.3 11.2 %copy-start = (f32[1,96,768]{2,1,0:T(8,128)S(1)}, f32[1,96,768]{2,1,0:T(8,128)}, u32[]{:S(2)}) copy-start(f32[1,96,768]{2,1,0:T(8,128)} %region_inverse.1) | copy-start | bytes 884740
  10.3 12.5 %all-to-all-start = ((f32[32,8,128]{2,1,0:T(8,128)}), f32[32,8,128]{2,1,0:T(8,128)S(1)}, u32[]{:S(2)}, u32[]{:S(2)}) async-start(f32[32,8,128]{2,1,0:T(8,128)} %get-tuple-element.38), calls=%async_computation | async-start | bytes 262144 | tf_op jit(solution)/shard_map/all_to_all | solution.py:704
  15.2 6.9 %collective-permute-start.3 = (f32[3,256]{1,0:T(4,128)S(1)}, f32[3,256]{1,0:T(4,128)S(1)}, u32[]{:S(2)}, u32[]{:S(2)}) collective-permute-start(f32[3,256]{1,0:T(4,128)S(1)} %get-tuple-element.41), channel_id=1, source_target_pairs={{0,24},{8,0},{16,8},{24,16},{1,25},{9,1},{17,9},{25,17},{2,26},{10... | collective-permute-start | bytes 9224 | tf_op jit(solution)/shard_map/ppermute | solution.py:19
  16.7 4.7 %copy-start.5 = (s32[1,96]{1,0:T(1,128)S(1)}, s32[1,96]{1,0:T(1,128)}, u32[]{:S(2)}) copy-start(s32[1,96]{1,0:T(1,128)} %primal_index.1) | copy-start | bytes 1156
  16.7 5.4 %collective-permute-start.4 = (f32[3,256]{1,0:T(4,128)S(1)}, f32[3,256]{1,0:T(4,128)S(1)}, u32[]{:S(2)}, u32[]{:S(2)}) collective-permute-start(f32[3,256]{1,0:T(4,128)S(1)} %get-tuple-element.42), channel_id=1, source_target_pairs={{0,4},{1,5},{2,6},{3,7},{4,0},{5,1},{6,2},{7,3},{8,12},{9,13},{10,... | collective-permute-start | bytes 9224 | tf_op jit(solution)/shard_map/ppermute | solution.py:19
  19.1 3.7 %collective-permute-start.5 = (f32[3,256]{1,0:T(4,128)S(1)}, f32[3,256]{1,0:T(4,128)S(1)}, u32[]{:S(2)}, u32[]{:S(2)}) collective-permute-start(f32[3,256]{1,0:T(4,128)S(1)} %get-tuple-element.43), channel_id=1, source_target_pairs={{0,7},{1,0},{2,1},{3,2},{4,3},{5,4},{6,5},{7,6},{8,15},{9,8},{10,9... | collective-permute-start | bytes 9224 | tf_op jit(solution)/shard_map/ppermute | solution.py:19
  21.5 1.3 %copy-start.4 = (f32[1,3,3,256]{3,0,2,1:T(1,128)S(1)}, f32[1,3,3,256]{3,0,2,1:T(1,128)}, u32[]{:S(2)}) copy-start(f32[1,3,3,256]{3,0,2,1:T(1,128)} %param.9) | copy-start | bytes 27652
  22.1 0.7 %copy-start.3 = (f32[1,16,256]{2,1,0:T(8,128)S(1)}, f32[1,16,256]{2,1,0:T(8,128)}, u32[]{:S(2)}) copy-start(f32[1,16,256]{2,1,0:T(8,128)} %viscosity.1) | copy-start | bytes 49156

commit v9 on v8

--- a/solution.py
+++ b/solution.py
@@ -275,6 +275,15 @@
         if done < COARSE_SWEEPS:
             power = square(power)
     return total
+
+
+def turn(k, count):
+    return (k + 1) * (LANES - count) % LANES
+
+
+def free_lanes(rows, count):
+    shape = (rows, LANES)
+    return (iota(shape, 1) // (LANES - count) == iota(shape, 0)) & (iota(shape, 0) < LANES // (LANES - count))
 
 
 def load(pairs, semaphores):
@@ -380,7 +389,9 @@
     squares = jnp.sum(jnp.sum(squares * squares, axis=0, keepdims=True), axis=1, keepdims=True)
     line = jnp.where(lane == count, own, jnp.where(lane == count + 1, squares, line))
     front_out[...] = jnp.zeros_like(front_out)
-    front_out[:opposite, :] = blocks[:opposite] * twice
+    blocks = blocks[:opposite] * twice
+    for k in range(opposite):
+        front_out[k : k + 1, :] = pltpu.roll(blocks[k : k + 1], turn(k, count), 1)
     front_out[opposite : opposite + 1, :] = line
     for i in range(share.shape[1] // LANES):
         front_out[opposite + 1 + i : opposite + 2 + i, :] = share[:, i * LANES : (i + 1) * LANES]
@@ -473,10 +484,8 @@
     energy = (source + residual) * field + swept * (2.0 * residual - diagonal * swept + 2.0 * ahead)
     energy = jnp.sum(energy, axis=0, keepdims=True)
     energy = functools.reduce(lambda a, b: a + b, [energy[:, i * LANES : (i + 1) * LANES] for i in range(face // LANES)])
-    energy = jnp.sum(energy, axis=1, keepdims=True)
     message = front[...]
-    at = (iota(message.shape, 0) == sizes[1] // 2) & (iota(message.shape, 1) == count)
-    message = message + jnp.where(at, energy, 0.0)
+    message = message + jnp.where(free_lanes(message.shape[0], count), energy, 0.0)
     for device in range(sizes[0] * sizes[1]):
         buffer[device] = message
     (copy,) = load([(buffer, send_out)], semaphores)
@@ -571,6 +580,14 @@
     me_region = lax.axis_index("region")
     everything = jnp.sum(received[...], axis=0)
     totals = [everything[half + 1 + i : half + 2 + i] for i in range(columns // LANES)]
+    lines = received[:, half, :]
+    lines = jnp.where(iota(lines.shape, 1) < count, lines, 0.0).reshape(n_region, n_sub, LANES)
+    groups = LANES // (LANES - count)
+    turned = [pltpu.roll(lines, turn(k, count), 2) for k in range(min(groups, half))]
+    quadratic = jnp.zeros((n_region, n_sub, LANES), jnp.float32)
+    for k in range(half):
+        products = received[:, k, :].reshape(n_region, n_sub, LANES)
+        quadratic = quadratic + products * pltpu.roll(turned[k % groups], n_sub - 1 - k, 1)
     after = [after_x[...], after_y[...], after_z[...]]
     field = base[...]
     field_x, field_y, field_z = [field[c * cells : (c + 1) * cells] for c in range(3)]
@@ -612,15 +629,11 @@
     parts = jnp.where(row == 0, piece, jnp.where(row == 1, total - piece, 0.0)).astype(jnp.bfloat16)
     top = jnp.dot(parts, global_parts[...], preferred_element_type=jnp.float32)
     top = top[0:1, :columns] + top[1:2, :columns] + top[0:1, columns:]
-    lines = received[:, half, :].reshape(n_region, n_sub, LANES)
-    quadratic = jnp.zeros((n_region, n_sub, LANES), jnp.float32)
-    for k in range(half):
-        products = received[:, k, :].reshape(n_region, n_sub, LANES)
-        quadratic = quadratic + products * pltpu.roll(lines, n_sub - 1 - k, 1)
     own_line = everything[half : half + 1]
     lane = iota((1, LANES), 1)
     quadratic = jnp.sum(quadratic.reshape(n_region * n_sub, LANES), axis=0, keepdims=True)
-    curvature = quadratic + jnp.where(lane == count, own_line, 0.0)
+    energy = jnp.where(free_lanes(everything.shape[0], count), everything, 0.0)
+    curvature = quadratic + jnp.where(lane == count, own_line, 0.0) + jnp.sum(energy, axis=0, keepdims=True)
     for i in range(columns // LANES):
         curvature = curvature + totals[i] * top[:, i * LANES : (i + 1) * LANES]
     curvature = jnp.sum(curvature, axis=1, keepdims=True)
@@ -644,6 +657,7 @@
     global_inverse,
 ):
     n_region, n_sub = sizes
+    assert LANES % (LANES - primal_index.shape[1]) == 0 and n_sub // 2 >= LANES // (LANES - primal_index.shape[1])
     cells = reaction.shape[1]
     face = reaction.shape[2]
     count = primal_index.shape[1]

time: 24 us -> 23.9 us (level)
  no operation moved by 1% of the time
where the time goes in v9:
time: 23.9 us; the launch traced here: 23.7 us
  starting transfers between devices  16.8 us (70%)
  Pallas kernels  5.32 us (22%)
  waiting for transfers between devices  0.84 us (4%)
  between operations  0.74 us (3%)
    ppermute x6, starting transfers between devices, shifted_2(): return lax.ppermute(x, axis, [(i, (i + by) % count) for i in range(count)])  12 us
    pallas_call x5, Pallas kernels, call(): pl.pallas_call(kernel, out_shape=out_shape, in_specs=[vmem] * len(operand...  5.32 us
    all_to_all x1, starting transfers between devices, body(): received = lax.all_to_all(sent, ('region', 'sub'), 0, 0, tiled=True)  4.78 us
    ppermute x6, waiting for transfers between devices, shifted_2(): return lax.ppermute(x, axis, [(i, (i + by) % count) for i in range(count)])  0.83 us
  transfers between devices with their start and end apart: 7, of which 2 were waited for; matrix products, arithmetic and copies ran while one was open for 0% of the time, Pallas kernels for 12%

profile of v9, /device:TPU:0, one launch (start us, length us, event | category | flops | bytes accessed | tf_op | source)
XLA Modules:
  0.0 23.7 jit_solution(13493499048985169831)
XLA Ops:
  0.6 0.5 %collective-permute-start = (f32[1,3,3,256]{3,0,2,1:T(1,128)}, f32[1,3,3,256]{3,0,2,1:T(1,128)S(1)}, u32[]{:S(2)}, u32[]{:S(2)}) collective-permute-start(f32[1,3,3,256]{3,0,2,1:T(1,128)} %param.10), channel_id=1, source_target_pairs={{0,8},{8,16},{16,24},{24,0},{1,9},{9,17},{17,25},{25,1},{2,10},{10... | collective-permute-start | bytes 27656 | tf_op jit(solution)/shard_map/ppermute | solution.py:19
  1.1 2.6 %collective-permute-start.2 = (f32[1,3,3,256]{3,0,2,1:T(1,128)}, f32[1,3,3,256]{3,0,2,1:T(1,128)S(1)}, u32[]{:S(2)}, u32[]{:S(2)}) collective-permute-start(f32[1,3,3,256]{3,0,2,1:T(1,128)} %param.10), channel_id=1, source_target_pairs={{0,1},{1,2},{2,3},{3,4},{4,5},{5,6},{6,7},{7,0},{8,9},{9,10},{10,1... | collective-permute-start | bytes 27656 | tf_op jit(solution)/shard_map/ppermute | solution.py:19
  3.7 2.6 %collective-permute-start.1 = (f32[1,3,3,256]{3,0,2,1:T(1,128)}, f32[1,3,3,256]{3,0,2,1:T(1,128)S(1)}, u32[]{:S(2)}, u32[]{:S(2)}) collective-permute-start(f32[1,3,3,256]{3,0,2,1:T(1,128)} %param.10), channel_id=1, source_target_pairs={{0,4},{1,5},{2,6},{3,7},{4,0},{5,1},{6,2},{7,3},{8,12},{9,13},{10,... | collective-permute-start | bytes 27656 | tf_op jit(solution)/shard_map/ppermute | solution.py:19
  6.3 2.1 %shard_map.120 = (f32[9,1,256]{2,1,0:T(1,128)S(1)}, f32[9,1,256]{2,1,0:T(1,128)S(1)}, f32[48,256]{1,0:T(8,128)S(1)}, f32[8,128]{1,0:T(8,128)S(1)}, f32[2,16,256]...) custom-call(f32[9,1,256]{2,1,0:T(1,128)} %bitcast.13, ...), custom_call_target="tpu_custom_call" | custom-call | tf_op jit(solution)/shard_map/pallas_call | solution.py:678
  8.5 0.0 copy-start.1
  8.5 0.0 collective-permute-done
  8.5 0.1 collective-permute-done.2
  8.6 0.0 collective-permute-done.1
  8.6 0.0 copy-start.2
  8.6 1.5 %shard_map.121 = (f32[48,256]{1,0:T(8,128)S(1)}, f32[32,8,128]{2,1,0:T(8,128)}) custom-call(f32[48,256]{1,0:T(8,128)S(1)} %get-tuple-element.30.source_own, f32[9,1,256]{2,1,0:T(1,128)S(1)} %bitcast.9, f32[9,1,256]{2,1,0:T(1,128)S(1)} %bitcast.11, f32[9,1,256]{2,1,0:T(1,128)S(1)} %bitcast.10, f32[2,16,256]{2,1,0:T(8,128)S(1)} %get-tuple-element.31.inverses, ...), custom_call_target="tpu_custom_call" | custom-call | tf_op jit(solution)/shard_map/pallas_call | solution.py:678
  10.1 0.0 copy-start
  10.2 4.8 %all-to-all-start = ((f32[32,8,128]{2,1,0:T(8,128)}), f32[32,8,128]{2,1,0:T(8,128)S(1)}, u32[]{:S(2)}, u32[]{:S(2)}) async-start(f32[32,8,128]{2,1,0:T(8,128)} %get-tuple-element.38), calls=%async_computation | async-start | bytes 262144 | tf_op jit(solution)/shard_map/all_to_all | solution.py:718
  14.9 0.1 shard_map.123
  15.1 1.6 %collective-permute-start.3 = (f32[3,256]{1,0:T(4,128)S(1)}, f32[3,256]{1,0:T(4,128)S(1)}, u32[]{:S(2)}, u32[]{:S(2)}) collective-permute-start(f32[3,256]{1,0:T(4,128)S(1)} %get-tuple-element.41), channel_id=1, source_target_pairs={{0,24},{8,0},{16,8},{24,16},{1,25},{9,1},{17,9},{25,17},{2,26},{10... | collective-permute-start | bytes 9224 | tf_op jit(solution)/shard_map/ppermute | solution.py:19
  16.6 0.0 copy-start.5
  16.6 2.4 %collective-permute-start.4 = (f32[3,256]{1,0:T(4,128)S(1)}, f32[3,256]{1,0:T(4,128)S(1)}, u32[]{:S(2)}, u32[]{:S(2)}) collective-permute-start(f32[3,256]{1,0:T(4,128)S(1)} %get-tuple-element.42), channel_id=1, source_target_pairs={{0,4},{1,5},{2,6},{3,7},{4,0},{5,1},{6,2},{7,3},{8,12},{9,13},{10,... | collective-permute-start | bytes 9224 | tf_op jit(solution)/shard_map/ppermute | solution.py:19
  19.0 2.4 %collective-permute-start.5 = (f32[3,256]{1,0:T(4,128)S(1)}, f32[3,256]{1,0:T(4,128)S(1)}, u32[]{:S(2)}, u32[]{:S(2)}) collective-permute-start(f32[3,256]{1,0:T(4,128)S(1)} %get-tuple-element.43), channel_id=1, source_target_pairs={{0,7},{1,0},{2,1},{3,2},{4,3},{5,4},{6,5},{7,6},{8,15},{9,8},{10,9... | collective-permute-start | bytes 9224 | tf_op jit(solution)/shard_map/ppermute | solution.py:19
  21.4 0.0 copy-done.1
  21.4 0.0 copy-done.2
  21.4 0.0 copy-done
  21.4 0.0 copy-done.5
  21.4 0.0 copy-start.4
  21.4 0.6 %shard_map.122 = (f32[16,256]{1,0:T(8,128)S(1)}, f32[8,96,128]{2,1,0:T(8,128)S(1)}, f32[96,384]{1,0:T(8,128)S(1)}, bf16[384,768]{1,0:T(8,128)(2,1)S(1)}, s32[48,...) custom-call(f32[48,256]{1,0:T(8,128)S(1)} %get-tuple-element.39.base, s32[1,96]{1,0:T(1,128)S(1)} %copy-done.5, ...), custom_call_target="tpu_custom_call" | custom-call | tf_op jit(solution)/shard_map/pallas_call | solution.py:678
  22.0 0.0 copy-start.3
  22.0 0.0 collective-permute-done.3.after_x
  22.0 0.0 collective-permute-done.4.after_y
  22.0 0.7 %collective-permute-done.5.after_z = f32[3,256]{1,0:T(4,128)S(1)} collective-permute-done((f32[3,256]{1,0:T(4,128)S(1)}, f32[3,256]{1,0:T(4,128)S(1)}, u32[]{:S(2)}, u32[]{:S(2)}) %collective-permute-start.5) | collective-permute-done | bytes 3104 | tf_op jit(solution)/shard_map/ppermute | solution.py:19
  22.7 0.0 all-to-all-done.received
  22.7 0.0 copy-done.4
  22.7 0.0 copy-done.3
  22.7 1.0 %shard_map.124 = (f32[9,1,256]{2,1,0:T(1,128)}, f32[9,1,256]{2,1,0:T(1,128)}, f32[1,3,16,256]{3,2,1,0:T(8,128)}, f32[1,16,256]{2,1,0:T(8,128)}) custom-call(f32[32,8,128]{2,1,0:T(8,128)S(1)} %all-to-all-done.received, f32[48,256]{1,0:T(8,128)S(1)} %get-tuple-element.39.base, f32[16,256]{1,0:T(8,128)S(1)} %get-tuple-element.40.ends, ...), custom_call_target="tpu_custom_call" | custom-call | tf_op jit(solution)/shard_map/pallas_call | solution.py:678
Async XLA Ops:
  0.6 7.8 %collective-permute-start = (f32[1,3,3,256]{3,0,2,1:T(1,128)}, f32[1,3,3,256]{3,0,2,1:T(1,128)S(1)}, u32[]{:S(2)}, u32[]{:S(2)}) collective-permute-start(f32[1,3,3,256]{3,0,2,1:T(1,128)} %param.10), channel_id=1, source_target_pairs={{0,8},{8,16},{16,24},{24,0},{1,9},{9,17},{17,25},{25,1},{2,10},{10... | collective-permute-start | bytes 27656 | tf_op jit(solution)/shard_map/ppermute | solution.py:19
  1.1 7.5 %collective-permute-start.2 = (f32[1,3,3,256]{3,0,2,1:T(1,128)}, f32[1,3,3,256]{3,0,2,1:T(1,128)S(1)}, u32[]{:S(2)}, u32[]{:S(2)}) collective-permute-start(f32[1,3,3,256]{3,0,2,1:T(1,128)} %param.10), channel_id=1, source_target_pairs={{0,1},{1,2},{2,3},{3,4},{4,5},{5,6},{6,7},{7,0},{8,9},{9,10},{10,1... | collective-permute-start | bytes 27656 | tf_op jit(solution)/shard_map/ppermute | solution.py:19
  3.7 4.9 %collective-permute-start.1 = (f32[1,3,3,256]{3,0,2,1:T(1,128)}, f32[1,3,3,256]{3,0,2,1:T(1,128)S(1)}, u32[]{:S(2)}, u32[]{:S(2)}) collective-permute-start(f32[1,3,3,256]{3,0,2,1:T(1,128)} %param.10), channel_id=1, source_target_pairs={{0,4},{1,5},{2,6},{3,7},{4,0},{5,1},{6,2},{7,3},{8,12},{9,13},{10,... | collective-permute-start | bytes 27656 | tf_op jit(solution)/shard_map/ppermute | solution.py:19
  8.5 12.9 %copy-start.1 = (f32[384,384]{1,0:T(8,128)S(1)}, f32[384,384]{1,0:T(8,128)}, u32[]{:S(2)}) copy-start(f32[384,384]{1,0:T(8,128)} %global_inverse.1) | copy-start | bytes 1769476
  8.6 12.8 %copy-start.2 = (f32[1,96,384]{2,1,0:T(8,128)S(1)}, f32[1,96,384]{2,1,0:T(8,128)}, u32[]{:S(2)}) copy-start(f32[1,96,384]{2,1,0:T(8,128)} %coarse_map.1) | copy-start | bytes 442372
  10.1 11.2 %copy-start = (f32[1,96,768]{2,1,0:T(8,128)S(1)}, f32[1,96,768]{2,1,0:T(8,128)}, u32[]{:S(2)}) copy-start(f32[1,96,768]{2,1,0:T(8,128)} %region_inverse.1) | copy-start | bytes 884740
  10.2 12.5 %all-to-all-start = ((f32[32,8,128]{2,1,0:T(8,128)}), f32[32,8,128]{2,1,0:T(8,128)S(1)}, u32[]{:S(2)}, u32[]{:S(2)}) async-start(f32[32,8,128]{2,1,0:T(8,128)} %get-tuple-element.38), calls=%async_computation | async-start | bytes 262144 | tf_op jit(solution)/shard_map/all_to_all | solution.py:718
  15.1 6.9 %collective-permute-start.3 = (f32[3,256]{1,0:T(4,128)S(1)}, f32[3,256]{1,0:T(4,128)S(1)}, u32[]{:S(2)}, u32[]{:S(2)}) collective-permute-start(f32[3,256]{1,0:T(4,128)S(1)} %get-tuple-element.41), channel_id=1, source_target_pairs={{0,24},{8,0},{16,8},{24,16},{1,25},{9,1},{17,9},{25,17},{2,26},{10... | collective-permute-start | bytes 9224 | tf_op jit(solution)/shard_map/ppermute | solution.py:19
  16.6 4.7 %copy-start.5 = (s32[1,96]{1,0:T(1,128)S(1)}, s32[1,96]{1,0:T(1,128)}, u32[]{:S(2)}) copy-start(s32[1,96]{1,0:T(1,128)} %primal_index.1) | copy-start | bytes 1156
  16.6 5.4 %collective-permute-start.4 = (f32[3,256]{1,0:T(4,128)S(1)}, f32[3,256]{1,0:T(4,128)S(1)}, u32[]{:S(2)}, u32[]{:S(2)}) collective-permute-start(f32[3,256]{1,0:T(4,128)S(1)} %get-tuple-element.42), channel_id=1, source_target_pairs={{0,4},{1,5},{2,6},{3,7},{4,0},{5,1},{6,2},{7,3},{8,12},{9,13},{10,... | collective-permute-start | bytes 9224 | tf_op jit(solution)/shard_map/ppermute | solution.py:19
  19.0 3.7 %collective-permute-start.5 = (f32[3,256]{1,0:T(4,128)S(1)}, f32[3,256]{1,0:T(4,128)S(1)}, u32[]{:S(2)}, u32[]{:S(2)}) collective-permute-start(f32[3,256]{1,0:T(4,128)S(1)} %get-tuple-element.43), channel_id=1, source_target_pairs={{0,7},{1,0},{2,1},{3,2},{4,3},{5,4},{6,5},{7,6},{8,15},{9,8},{10,9... | collective-permute-start | bytes 9224 | tf_op jit(solution)/shard_map/ppermute | solution.py:19
  21.4 1.3 %copy-start.4 = (f32[1,3,3,256]{3,0,2,1:T(1,128)S(1)}, f32[1,3,3,256]{3,0,2,1:T(1,128)}, u32[]{:S(2)}) copy-start(f32[1,3,3,256]{3,0,2,1:T(1,128)} %param.9) | copy-start | bytes 27652
  22.0 0.7 %copy-start.3 = (f32[1,16,256]{2,1,0:T(8,128)S(1)}, f32[1,16,256]{2,1,0:T(8,128)}, u32[]{:S(2)}) copy-start(f32[1,16,256]{2,1,0:T(8,128)} %viscosity.1) | copy-start | bytes 49156

commit v10 on v9

--- a/solution.py
+++ b/solution.py
@@ -419,7 +419,13 @@
 ):
     face = cells * cells
     rows = 3 * cells
-    below_x, below_y, below_z = [faces_of(ref)[d] for d, ref in enumerate((from_x, from_y, from_z))]
+    r = lax.axis_index("region")
+    n_region = sizes[0]
+    straight = r < n_region // 2
+    below_x = faces_of(from_x)[0]
+    y_faces, z_faces = faces_of(from_y), faces_of(from_z)
+    below_y = jnp.where(straight, y_faces[1], z_faces[1])
+    below_z = jnp.where(straight, z_faces[2], y_faces[2])
     n_region, n_sub = sizes
     row_x = iota((cells, face), 0)
     source = source_own[...] - unfold(below_y, below_z, cells, False)
@@ -686,8 +692,15 @@
         )(*operands, *[pltpu.with_memory_space_constraint(x, pltpu.HBM) for x in in_hbm])
 
     below_x = shifted_2(direction, "region", 1).reshape(lines)
-    below_y = shifted_2(direction, "sub", DOM_Z).reshape(lines)
-    below_z = shifted_2(direction, "sub", 1).reshape(lines)
+    def mixed(flip):
+        pairs = []
+        for r in range(n_region):
+            by = DOM_Z if (r < n_region // 2) == flip else 1
+            pairs += [(r * n_sub + q, r * n_sub + (q + by) % n_sub) for q in range(n_sub)]
+        return lax.ppermute(direction, ("region", "sub"), pairs).reshape(lines)
+
+    below_y = mixed(True)
+    below_z = mixed(False)
     multipliers, direction, residual = [x.reshape(lines) for x in (multipliers, direction, residual)]
     half_cells = (cells // 2) ** 3
     direction, residual, source, front, inverses, halves, quarter, gather, coarsen, sweeps = call(

time: 23.9 us -> 23.7 us (level)
    ppermute x6 -> x4, starting transfers between devices: 12 us -> 6.8 us  [shifted_2(): return lax.ppermute(x, axis, [(i, (i + by) % count) for i in range(count)])]
    ppermute x0 -> x2, starting transfers between devices: none -> 5.17 us  [mixed(): return lax.ppermute(direction, ('region', 'sub'), pairs).reshape(lines)]
    ppermute x6 -> x4, waiting for transfers between devices: 0.83 us -> 0.71 us  [shifted_2(): return lax.ppermute(x, axis, [(i, (i + by) % count) for i in range(count)])]
where the time goes in v10:
time: 23.7 us; the launch traced here: 23.5 us
  starting transfers between devices  16.6 us (70%)
  Pallas kernels  5.33 us (22%)
  waiting for transfers between devices  0.84 us (4%)
  between operations  0.74 us (3%)
    ppermute x4, starting transfers between devices, shifted_2(): return lax.ppermute(x, axis, [(i, (i + by) % count) for i in range(count)])  6.8 us
    pallas_call x5, Pallas kernels, call(): pl.pallas_call(kernel, out_shape=out_shape, in_specs=[vmem] * len(operand...  5.33 us
    ppermute x2, starting transfers between devices, mixed(): return lax.ppermute(direction, ('region', 'sub'), pairs).reshape(lines)  5.17 us
    all_to_all x1, starting transfers between devices, body(): received = lax.all_to_all(sent, ('region', 'sub'), 0, 0, tiled=True)  4.61 us
    ppermute x4, waiting for transfers between devices, shifted_2(): return lax.ppermute(x, axis, [(i, (i + by) % count) for i in range(count)])  0.71 us
  transfers between devices with their start and end apart: 7, of which 2 were waited for; matrix products, arithmetic and copies ran while one was open for 0% of the time, Pallas kernels for 12%

profile of v10, /device:TPU:0, one launch (start us, length us, event | category | flops | bytes accessed | tf_op | source)
XLA Modules:
  0.0 23.5 jit_solution(11379253512117713481)
XLA Ops:
  0.6 0.5 %collective-permute-start = (f32[1,3,3,256]{3,0,2,1:T(1,128)}, f32[1,3,3,256]{3,0,2,1:T(1,128)S(1)}, u32[]{:S(2)}, u32[]{:S(2)}) collective-permute-start(f32[1,3,3,256]{3,0,2,1:T(1,128)} %param.10), channel_id=1, source_target_pairs={{0,8},{8,16},{16,24},{24,0},{1,9},{9,17},{17,25},{25,1},{2,10},{10... | collective-permute-start | bytes 27656 | tf_op jit(solution)/shard_map/ppermute | solution.py:19
  1.1 2.6 %collective-permute-start.2 = (f32[1,3,3,256]{3,0,2,1:T(1,128)}, f32[1,3,3,256]{3,0,2,1:T(1,128)S(1)}, u32[]{:S(2)}, u32[]{:S(2)}) collective-permute-start(f32[1,3,3,256]{3,0,2,1:T(1,128)} %param.10), channel_id=1, source_target_pairs={{0,1},{1,2},{2,3},{3,4},{4,5},{5,6},{6,7},{7,0},{8,9},{9,10},{10,1... | collective-permute-start | bytes 27656 | tf_op jit(solution)/shard_map/ppermute | solution.py:700
  3.7 2.6 %collective-permute-start.1 = (f32[1,3,3,256]{3,0,2,1:T(1,128)}, f32[1,3,3,256]{3,0,2,1:T(1,128)S(1)}, u32[]{:S(2)}, u32[]{:S(2)}) collective-permute-start(f32[1,3,3,256]{3,0,2,1:T(1,128)} %param.10), channel_id=1, source_target_pairs={{0,4},{1,5},{2,6},{3,7},{4,0},{5,1},{6,2},{7,3},{8,12},{9,13},{10,... | collective-permute-start | bytes 27656 | tf_op jit(solution)/shard_map/ppermute | solution.py:700
  6.3 2.1 %shard_map.120 = (f32[9,1,256]{2,1,0:T(1,128)S(1)}, f32[9,1,256]{2,1,0:T(1,128)S(1)}, f32[48,256]{1,0:T(8,128)S(1)}, f32[8,128]{1,0:T(8,128)S(1)}, f32[2,16,256]...) custom-call(f32[9,1,256]{2,1,0:T(1,128)} %bitcast.13, ...), custom_call_target="tpu_custom_call" | custom-call | tf_op jit(solution)/shard_map/pallas_call | solution.py:684
  8.5 0.0 copy-start.1
  8.5 0.0 collective-permute-done
  8.5 0.1 collective-permute-done.2
  8.6 0.0 collective-permute-done.1
  8.6 0.0 copy-start.2
  8.6 1.5 %shard_map.121 = (f32[48,256]{1,0:T(8,128)S(1)}, f32[32,8,128]{2,1,0:T(8,128)}) custom-call(f32[48,256]{1,0:T(8,128)S(1)} %get-tuple-element.30.source_own, f32[9,1,256]{2,1,0:T(1,128)S(1)} %bitcast.9, f32[9,1,256]{2,1,0:T(1,128)S(1)} %bitcast.11, f32[9,1,256]{2,1,0:T(1,128)S(1)} %bitcast.10, f32[2,16,256]{2,1,0:T(8,128)S(1)} %get-tuple-element.31.inverses, ...), custom_call_target="tpu_custom_call" | custom-call | tf_op jit(solution)/shard_map/pallas_call | solution.py:684
  10.1 0.0 copy-start
  10.2 4.6 %all-to-all-start = ((f32[32,8,128]{2,1,0:T(8,128)}), f32[32,8,128]{2,1,0:T(8,128)S(1)}, u32[]{:S(2)}, u32[]{:S(2)}) async-start(f32[32,8,128]{2,1,0:T(8,128)} %get-tuple-element.38), calls=%async_computation | async-start | bytes 262144 | tf_op jit(solution)/shard_map/all_to_all | solution.py:731
  14.8 0.1 shard_map.123
  14.9 1.6 %collective-permute-start.3 = (f32[3,256]{1,0:T(4,128)S(1)}, f32[3,256]{1,0:T(4,128)S(1)}, u32[]{:S(2)}, u32[]{:S(2)}) collective-permute-start(f32[3,256]{1,0:T(4,128)S(1)} %get-tuple-element.41), channel_id=1, source_target_pairs={{0,24},{8,0},{16,8},{24,16},{1,25},{9,1},{17,9},{25,17},{2,26},{10... | collective-permute-start | bytes 9224 | tf_op jit(solution)/shard_map/ppermute | solution.py:19
  16.5 0.0 copy-start.5
  16.5 2.4 %collective-permute-start.4 = (f32[3,256]{1,0:T(4,128)S(1)}, f32[3,256]{1,0:T(4,128)S(1)}, u32[]{:S(2)}, u32[]{:S(2)}) collective-permute-start(f32[3,256]{1,0:T(4,128)S(1)} %get-tuple-element.42), channel_id=1, source_target_pairs={{0,4},{1,5},{2,6},{3,7},{4,0},{5,1},{6,2},{7,3},{8,12},{9,13},{10,... | collective-permute-start | bytes 9224 | tf_op jit(solution)/shard_map/ppermute | solution.py:19
  18.8 2.4 %collective-permute-start.5 = (f32[3,256]{1,0:T(4,128)S(1)}, f32[3,256]{1,0:T(4,128)S(1)}, u32[]{:S(2)}, u32[]{:S(2)}) collective-permute-start(f32[3,256]{1,0:T(4,128)S(1)} %get-tuple-element.43), channel_id=1, source_target_pairs={{0,7},{1,0},{2,1},{3,2},{4,3},{5,4},{6,5},{7,6},{8,15},{9,8},{10,9... | collective-permute-start | bytes 9224 | tf_op jit(solution)/shard_map/ppermute | solution.py:19
  21.2 0.0 copy-done.1
  21.2 0.0 copy-done.2
  21.2 0.0 copy-done
  21.2 0.0 copy-done.5
  21.2 0.0 copy-start.4
  21.2 0.6 %shard_map.122 = (f32[16,256]{1,0:T(8,128)S(1)}, f32[8,96,128]{2,1,0:T(8,128)S(1)}, f32[96,384]{1,0:T(8,128)S(1)}, bf16[384,768]{1,0:T(8,128)(2,1)S(1)}, s32[48,...) custom-call(f32[48,256]{1,0:T(8,128)S(1)} %get-tuple-element.39.base, s32[1,96]{1,0:T(1,128)S(1)} %copy-done.5, ...), custom_call_target="tpu_custom_call" | custom-call | tf_op jit(solution)/shard_map/pallas_call | solution.py:684
  21.8 0.0 copy-start.3
  21.8 0.0 collective-permute-done.3.after_x
  21.8 0.0 collective-permute-done.4.after_y
  21.8 0.7 %collective-permute-done.5.after_z = f32[3,256]{1,0:T(4,128)S(1)} collective-permute-done((f32[3,256]{1,0:T(4,128)S(1)}, f32[3,256]{1,0:T(4,128)S(1)}, u32[]{:S(2)}, u32[]{:S(2)}) %collective-permute-start.5) | collective-permute-done | bytes 3104 | tf_op jit(solution)/shard_map/ppermute | solution.py:19
  22.5 0.0 all-to-all-done.received
  22.5 0.0 copy-done.4
  22.5 0.0 copy-done.3
  22.5 1.0 %shard_map.124 = (f32[9,1,256]{2,1,0:T(1,128)}, f32[9,1,256]{2,1,0:T(1,128)}, f32[1,3,16,256]{3,2,1,0:T(8,128)}, f32[1,16,256]{2,1,0:T(8,128)}) custom-call(f32[32,8,128]{2,1,0:T(8,128)S(1)} %all-to-all-done.received, f32[48,256]{1,0:T(8,128)S(1)} %get-tuple-element.39.base, f32[16,256]{1,0:T(8,128)S(1)} %get-tuple-element.40.ends, ...), custom_call_target="tpu_custom_call" | custom-call | tf_op jit(solution)/shard_map/pallas_call | solution.py:684
Async XLA Ops:
  0.6 7.8 %collective-permute-start = (f32[1,3,3,256]{3,0,2,1:T(1,128)}, f32[1,3,3,256]{3,0,2,1:T(1,128)S(1)}, u32[]{:S(2)}, u32[]{:S(2)}) collective-permute-start(f32[1,3,3,256]{3,0,2,1:T(1,128)} %param.10), channel_id=1, source_target_pairs={{0,8},{8,16},{16,24},{24,0},{1,9},{9,17},{17,25},{25,1},{2,10},{10... | collective-permute-start | bytes 27656 | tf_op jit(solution)/shard_map/ppermute | solution.py:19
  1.1 7.5 %collective-permute-start.2 = (f32[1,3,3,256]{3,0,2,1:T(1,128)}, f32[1,3,3,256]{3,0,2,1:T(1,128)S(1)}, u32[]{:S(2)}, u32[]{:S(2)}) collective-permute-start(f32[1,3,3,256]{3,0,2,1:T(1,128)} %param.10), channel_id=1, source_target_pairs={{0,1},{1,2},{2,3},{3,4},{4,5},{5,6},{6,7},{7,0},{8,9},{9,10},{10,1... | collective-permute-start | bytes 27656 | tf_op jit(solution)/shard_map/ppermute | solution.py:700
  3.7 4.9 %collective-permute-start.1 = (f32[1,3,3,256]{3,0,2,1:T(1,128)}, f32[1,3,3,256]{3,0,2,1:T(1,128)S(1)}, u32[]{:S(2)}, u32[]{:S(2)}) collective-permute-start(f32[1,3,3,256]{3,0,2,1:T(1,128)} %param.10), channel_id=1, source_target_pairs={{0,4},{1,5},{2,6},{3,7},{4,0},{5,1},{6,2},{7,3},{8,12},{9,13},{10,... | collective-permute-start | bytes 27656 | tf_op jit(solution)/shard_map/ppermute | solution.py:700
  8.5 12.7 %copy-start.1 = (f32[384,384]{1,0:T(8,128)S(1)}, f32[384,384]{1,0:T(8,128)}, u32[]{:S(2)}) copy-start(f32[384,384]{1,0:T(8,128)} %global_inverse.1) | copy-start | bytes 1769476
  8.6 12.6 %copy-start.2 = (f32[1,96,384]{2,1,0:T(8,128)S(1)}, f32[1,96,384]{2,1,0:T(8,128)}, u32[]{:S(2)}) copy-start(f32[1,96,384]{2,1,0:T(8,128)} %coarse_map.1) | copy-start | bytes 442372
  10.1 11.1 %copy-start = (f32[1,96,768]{2,1,0:T(8,128)S(1)}, f32[1,96,768]{2,1,0:T(8,128)}, u32[]{:S(2)}) copy-start(f32[1,96,768]{2,1,0:T(8,128)} %region_inverse.1) | copy-start | bytes 884740
  10.2 12.4 %all-to-all-start = ((f32[32,8,128]{2,1,0:T(8,128)}), f32[32,8,128]{2,1,0:T(8,128)S(1)}, u32[]{:S(2)}, u32[]{:S(2)}) async-start(f32[32,8,128]{2,1,0:T(8,128)} %get-tuple-element.38), calls=%async_computation | async-start | bytes 262144 | tf_op jit(solution)/shard_map/all_to_all | solution.py:731
  14.9 6.9 %collective-permute-start.3 = (f32[3,256]{1,0:T(4,128)S(1)}, f32[3,256]{1,0:T(4,128)S(1)}, u32[]{:S(2)}, u32[]{:S(2)}) collective-permute-start(f32[3,256]{1,0:T(4,128)S(1)} %get-tuple-element.41), channel_id=1, source_target_pairs={{0,24},{8,0},{16,8},{24,16},{1,25},{9,1},{17,9},{25,17},{2,26},{10... | collective-permute-start | bytes 9224 | tf_op jit(solution)/shard_map/ppermute | solution.py:19
  16.5 4.7 %copy-start.5 = (s32[1,96]{1,0:T(1,128)S(1)}, s32[1,96]{1,0:T(1,128)}, u32[]{:S(2)}) copy-start(s32[1,96]{1,0:T(1,128)} %primal_index.1) | copy-start | bytes 1156
  16.5 5.4 %collective-permute-start.4 = (f32[3,256]{1,0:T(4,128)S(1)}, f32[3,256]{1,0:T(4,128)S(1)}, u32[]{:S(2)}, u32[]{:S(2)}) collective-permute-start(f32[3,256]{1,0:T(4,128)S(1)} %get-tuple-element.42), channel_id=1, source_target_pairs={{0,4},{1,5},{2,6},{3,7},{4,0},{5,1},{6,2},{7,3},{8,12},{9,13},{10,... | collective-permute-start | bytes 9224 | tf_op jit(solution)/shard_map/ppermute | solution.py:19
  18.8 3.7 %collective-permute-start.5 = (f32[3,256]{1,0:T(4,128)S(1)}, f32[3,256]{1,0:T(4,128)S(1)}, u32[]{:S(2)}, u32[]{:S(2)}) collective-permute-start(f32[3,256]{1,0:T(4,128)S(1)} %get-tuple-element.43), channel_id=1, source_target_pairs={{0,7},{1,0},{2,1},{3,2},{4,3},{5,4},{6,5},{7,6},{8,15},{9,8},{10,9... | collective-permute-start | bytes 9224 | tf_op jit(solution)/shard_map/ppermute | solution.py:19
  21.2 1.3 %copy-start.4 = (f32[1,3,3,256]{3,0,2,1:T(1,128)S(1)}, f32[1,3,3,256]{3,0,2,1:T(1,128)}, u32[]{:S(2)}) copy-start(f32[1,3,3,256]{3,0,2,1:T(1,128)} %param.9) | copy-start | bytes 27652
  21.8 0.7 %copy-start.3 = (f32[1,16,256]{2,1,0:T(8,128)S(1)}, f32[1,16,256]{2,1,0:T(8,128)}, u32[]{:S(2)}) copy-start(f32[1,16,256]{2,1,0:T(8,128)} %viscosity.1) | copy-start | bytes 49156
